TPU v7x, 256 devices: a whole 4x4x8 slice. The times are simulated.
256 devices in a mesh: blk: 32 (over y, z), img: 4 (over x_lo, core), doc: 2 (over x_hi).
Axes of the slice: x: 4 (x_hi: 2, x_lo: 2; x = x_hi * 2 + x_lo), y: 4, z: 8, core: 2. Of those that a mesh axis runs over, the one named last changes fastest.
Arguments:
- features: bfloat16 [64, 257, 1280], P(('doc', 'blk')), parts along dimension 0, may hold values from -6 to 6
- latents: bfloat16 [64, 1280], replicated, may hold values from -6 to 6
- context_gain: float32 [1280], replicated, may hold values from 0.25 to 1.75
- latent_gain: float32 [1280], replicated, may hold values from 0.25 to 1.75
- final_gain: float32 [1280], replicated, may hold values from 0.25 to 1.75
- rs_query: bfloat16 [1280, 1536], P('blk', 'img'), may hold values from -0.15625 to 0.15625
- rs_key: bfloat16 [1280, 1536], P('blk', 'img'), may hold values from -0.15625 to 0.15625
- rs_value: bfloat16 [1280, 1536], P('blk', 'img'), may hold values from -0.15625 to 0.15625
- rs_out: bfloat16 [1536, 1280], P('img', 'blk'), may hold values from -0.15625 to 0.15625
- x_key: bfloat16 [1280, 4096], P(None, 'img'), may hold values from -0.15625 to 0.15625
- x_value: bfloat16 [1280, 4096], P(None, 'img'), may hold values from -0.15625 to 0.15625
- text_query: bfloat16 [8192, 4096], P(('doc', 'blk'), 'img'), parts along dimension 0, may hold values from -180 to 180
- text_key: bfloat16 [8192, 4096], P(('doc', 'blk'), 'img'), parts along dimension 0, may hold values from -6 to 6
- text_value: bfloat16 [8192, 4096], P(('doc', 'blk'), 'img'), parts along dimension 0, may hold values from -6 to 6
- cross_query: bfloat16 [8192, 4096], P(('doc', 'blk'), 'img'), parts along dimension 0, may hold values from -240 to 240
- cross_gate: float32 [4096], P('img'), may hold values from -1.5 to 1.5
- image_pos: int32 [64], P('doc'), parts along dimension 0, may hold values from 0 to 4095, as said below
Outputs:
- cross_out: bfloat16 [8192, 4096], P(('doc', 'blk'), 'img'), parts along dimension 0
- self_out: bfloat16 [8192, 4096], P(('doc', 'blk'), 'img'), parts along dimension 0
There are 2 independent parts, one for each index of `doc`. A program takes and returns all parts, laid end to end along the dimension named above; an argument that names none is the same for every part. Nothing has to cross between parts.
Inputs may be any that keep to these rules, and one draw needn't show every extreme that they name: `image_pos`: all different, in no particular order; the 128 positions of one blk index hold at most 3 of them, and some blk index holds exactly 3; one image stands at the last position.
All inputs are finite; a program needn't handle non-finite values.
Results may differ from a plain program's by a relative error of at most 0.04.
Values may be sent and summed in bfloat16 or wider, within the bound.
No kernel may reach another device: no remote copies, remote signals or barrier semaphores. Data moves between devices by JAX's collectives and lax.ppermute only.
A program may use at most 128 MiB of HBM per device.

v0:
```python
import jax
import jax.numpy as jnp
from jax import lax
from jax.sharding import PartitionSpec as P

HD = 128
RHD = 96
CITE = 3


epsilon = 1e-05


def shifted(value, axis, steps):
    count = lax.axis_size(axis)
    leading, last = (max(0, -steps), min(count, count - steps))
    return lax.ppermute(value, axis, [(source, source + steps) for source in range(leading, last)])


def layer_norm(values, gain):
    values = values.astype(jnp.float32)
    center = jnp.mean(values, -1, keepdims=True)
    spread = jnp.mean(jnp.square(values - center), -1, keepdims=True)
    return (values - center) * lax.rsqrt(spread + epsilon) * gain


def attend(scores, visible, value_rows):
    scores = jnp.where(visible, scores, -1e30)
    row_peak = jnp.max(scores, -1, keepdims=True)
    weights = jnp.where(visible, jnp.exp(scores - row_peak), 0.0)
    row_total = jnp.sum(weights, -1)
    context = jnp.einsum(
        "hqk,khd->qhd", weights.astype(jnp.bfloat16), value_rows, preferred_element_type=jnp.float32
    )
    return context / jnp.transpose(row_total)[:, :, None]


def shards(
    features,
    latents,
    context_gain,
    latent_gain,
    final_gain,
    rs_query,
    rs_key,
    rs_value,
    rs_out,
    x_key,
    x_value,
    text_query,
    text_key,
    text_value,
    cross_query,
    cross_gate,
    image_pos,
):
    blocks = lax.axis_size("blk")
    shard_index = lax.axis_index("blk")
    latent_rows = latents.shape[0]
    full_width = latents.shape[1]
    latent_norm = layer_norm(latents, latent_gain).astype(jnp.bfloat16)
    feature_norm = layer_norm(features[0], context_gain).astype(jnp.bfloat16)
    context = jnp.concatenate([feature_norm, latent_norm], 0)
    inner_width = rs_query.shape[1]
    pieces = (
        lax.all_gather(rs_query, "blk", axis=0, tiled=True),
        lax.all_gather(rs_key, "blk", axis=0, tiled=True),
        lax.all_gather(rs_value, "blk", axis=0, tiled=True),
    )
    piece_rows = pieces[0].shape[0]
    query_rows = jnp.dot(latent_norm, pieces[0], preferred_element_type=jnp.float32)
    key_rows = jnp.dot(context, pieces[1], preferred_element_type=jnp.float32)
    value_rows = jnp.dot(context, pieces[2], preferred_element_type=jnp.float32)
    head_count = inner_width // RHD
    query_rows = query_rows.astype(jnp.bfloat16).reshape(latent_rows, head_count, RHD)
    key_rows = key_rows.astype(jnp.bfloat16).reshape(-1, head_count, RHD)
    value_rows = value_rows.astype(jnp.bfloat16).reshape(-1, head_count, RHD)
    scores = jnp.einsum(
        "qhd,khd->hqk", query_rows, key_rows, preferred_element_type=jnp.float32
    ) * RHD ** (-0.5)
    head_context = (
        attend(scores, True, value_rows).astype(jnp.bfloat16).reshape(latent_rows, inner_width)
    )
    partial_out = jnp.dot(
        head_context,
        lax.all_gather(rs_out, "blk", axis=1, tiled=True),
        preferred_element_type=jnp.float32,
    )
    tokens = text_query.shape[0]
    start_row = shard_index * tokens
    image_count = image_pos.shape[0]
    image_ids = jnp.arange(image_count, dtype=jnp.int32)
    image_rank = jnp.sum((image_pos[None, :] < image_pos[:, None]).astype(jnp.int32), axis=1)
    first_image = jnp.sum((image_pos < start_row).astype(jnp.int32))
    wanted = first_image - 1 + jnp.arange(CITE + 1, dtype=jnp.int32)
    matches = image_rank[None, :] == wanted[:, None]
    stored = jnp.sum(jnp.where(matches, image_ids[None, :], 0), axis=1)
    present = jnp.any(matches, axis=1)
    summed = lax.psum(partial_out, "img")
    resampled = layer_norm(latents.astype(jnp.float32) + summed, final_gain).astype(jnp.bfloat16)
    all_latents = lax.all_gather(resampled[None], "blk", axis=0, tiled=True)
    window = jnp.where(present[:, None, None], all_latents[stored], jnp.zeros((), jnp.bfloat16))
    window = window.reshape(-1, full_width)
    cross_keys = jnp.dot(window, x_key, preferred_element_type=jnp.float32).astype(jnp.bfloat16)
    cross_values = jnp.dot(window, x_value, preferred_element_type=jnp.float32).astype(jnp.bfloat16)
    local_heads = text_query.shape[1] // HD
    positions = start_row + jnp.arange(tokens, dtype=jnp.int32)
    token_rank = jnp.sum((image_pos[None, :] <= positions[:, None]).astype(jnp.int32), axis=1) - 1
    local_slot = token_rank - first_image + 1
    key_slot = jnp.arange((CITE + 1) * latent_rows, dtype=jnp.int32) // latent_rows
    cross_visible = (key_slot[None, :] == local_slot[:, None])[None]
    cross_rows = cross_query.reshape(tokens, local_heads, HD)
    cross_scores = jnp.einsum(
        "thd,khd->htk",
        cross_rows,
        cross_keys.reshape(-1, local_heads, HD),
        preferred_element_type=jnp.float32,
    ) * HD ** (-0.5)
    cross_context = attend(cross_scores, cross_visible, cross_values.reshape(-1, local_heads, HD))
    cross_context = cross_context * jnp.tanh(cross_gate).reshape(local_heads, HD)
    cross_out = (
        jnp.where((token_rank >= 0)[:, None, None], cross_context, 0.0)
        .reshape(tokens, -1)
        .astype(jnp.bfloat16)
    )
    self_rows = text_query.reshape(tokens, local_heads, HD)
    last_row = start_row + tokens - 1

    def fold_piece(fold_state, pieces, first_row):
        piece_keys, piece_values = pieces
        piece_rows = piece_keys.shape[0]

        def update(inner_state):
            row_peak, row_total, context_sum = inner_state
            scores = jnp.einsum(
                "thd,khd->htk",
                self_rows,
                piece_keys.reshape(piece_rows, local_heads, HD),
                preferred_element_type=jnp.float32,
            ) * HD ** (-0.5)
            key_positions = first_row + jnp.arange(piece_rows, dtype=jnp.int32)
            visible = (key_positions[None, :] <= positions[:, None])[None]
            scores = jnp.where(visible, scores, -1e30)
            new_peak = jnp.maximum(row_peak, jnp.max(scores, -1))
            rescale = jnp.exp(row_peak - new_peak)
            weights = jnp.where(visible, jnp.exp(scores - new_peak[:, :, None]), 0.0)
            row_total = row_total * rescale + jnp.sum(weights, -1)
            context_sum = context_sum * jnp.transpose(rescale)[:, :, None] + jnp.einsum(
                "htk,khd->thd",
                weights.astype(jnp.bfloat16),
                piece_values.reshape(piece_rows, local_heads, HD),
                preferred_element_type=jnp.float32,
            )
            return (new_peak, row_total, context_sum)

        def unchanged(inner_state):
            return inner_state

        return lax.cond(first_row <= last_row, update, unchanged, fold_state)

    start_fold = (
        jnp.full((local_heads, tokens), -1e30, jnp.float32),
        jnp.zeros((local_heads, tokens), jnp.float32),
        jnp.zeros((tokens, local_heads, HD), jnp.float32),
    )
    fold_state = fold_piece(start_fold, (text_key, text_value), start_row)
    stacked = jnp.stack([text_key, text_value])

    def shift_turn(step_index, carried):
        inner_state, moving = carried
        moving = shifted(moving, "blk", 1)
        anchor = (shard_index - step_index - 1 + blocks) % blocks
        inner_state = fold_piece(inner_state, (moving[0], moving[1]), anchor * tokens)
        return (inner_state, moving)

    fold_state, stacked = lax.fori_loop(0, blocks - 1, shift_turn, (fold_state, stacked))
    row_peak, row_total, context_sum = fold_state
    self_out = (
        (context_sum / jnp.transpose(row_total)[:, :, None])
        .reshape(tokens, -1)
        .astype(jnp.bfloat16)
    )
    return (cross_out, self_out)


def solution(mesh):
    in_specs = (
        P(("doc", "blk"), None, None),
        P(),
        P(),
        P(),
        P(),
        P("blk", "img"),
        P("blk", "img"),
        P("blk", "img"),
        P("img", "blk"),
        P(None, "img"),
        P(None, "img"),
        P(("doc", "blk"), "img"),
        P(("doc", "blk"), "img"),
        P(("doc", "blk"), "img"),
        P(("doc", "blk"), "img"),
        P("img"),
        P("doc"),
    )
    out_specs = (P(("doc", "blk"), "img"), P(("doc", "blk"), "img"))
    return jax.shard_map(shards, mesh=mesh, in_specs=in_specs, out_specs=out_specs, check_vma=False)
```

profile of v0, /device:TPU:26, one launch (start us, length us, event | category | flops | bytes accessed | tf_op | source)
XLA Modules:
  0.0 910.4 jit_solution(7678973259980003672)
XLA Ops:
  12.4 52.6 %all_gather.17 = bf16[1280,384]{1,0:T(8,128)(2,1)S(1)} all-gather(bf16[40,384]{1,0:T(8,128)(2,1)S(1)} %copy-done.12), channel_id=1, replica_groups=mesh['blk'=32,'img'=4,'doc'=2] {'blk'}, dimensions={0}, use_global_device_ids=true | all-gather | bytes 1013760 | tf_op jit(solution)/shard_map/all_gather | solution.py:67
  67.6 48.0 %all_gather.16 = bf16[1280,384]{1,0:T(8,128)(2,1)S(1)} all-gather(bf16[40,384]{1,0:T(8,128)(2,1)S(1)} %copy-done.13), channel_id=1, replica_groups=mesh['blk'=32,'img'=4,'doc'=2] {'blk'}, dimensions={0}, use_global_device_ids=true | all-gather | bytes 1013760 | tf_op jit(solution)/shard_map/all_gather | solution.py:66
  116.8 49.1 %all_gather.15 = bf16[1280,384]{1,0:T(8,128)(2,1)S(1)} all-gather(bf16[40,384]{1,0:T(8,128)(2,1)S(1)} %copy-done.14), channel_id=1, replica_groups=mesh['blk'=32,'img'=4,'doc'=2] {'blk'}, dimensions={0}, use_global_device_ids=true | all-gather | bytes 1013760 | tf_op jit(solution)/shard_map/all_gather | solution.py:68
  170.5 47.8 %all_gather.18 = bf16[384,1280]{0,1:T(8,128)(2,1)S(1)} all-gather(bf16[384,40]{0,1:T(8,128)(2,1)S(1)} %copy-done.15), channel_id=1, replica_groups=mesh['blk'=32,'img'=4,'doc'=2] {'blk'}, dimensions={1}, use_global_device_ids=true | all-gather | bytes 1013760 | tf_op jit(solution)/shard_map/all_gather | solution.py:86
  219.5 39.8 %all-reduce.2.cloned.1.call-done = f32[64,1280]{1,0:T(8,128)} async-done(((f32[64,1280]{1,0:T(8,128)}), f32[64,1280]{1,0:T(8,128)}) %all-reduce.2.cloned.1.call-update) | async-done | bytes 327696 | tf_op jit(solution)/shard_map/psum | solution.py:99
  276.5 609.7 %while.24 = (s32[]{:T(128)}, f32[8,128]{1,0:T(8,128)}, f32[8,128]{1,0:T(8,128)S(1)}, f32[128,8,128]{2,0,1:T(8,128)}, bf16[2,128,1024]{1,2,0:T(8,128)(2,1)}, /*in...) while((s32[]{:T(128)}, f32[8,128]{1,0:T(8,128)}, ...), condition=%wide.region_25.26_spmd.clone, body=%wide.region_20.25_spmd.clone.sunk | while | flops 68570384 | bytes 11931140 | solution.py:176
  280.0 18.8 %collective-permute-done = bf16[2,128,1024]{1,2,0:T(8,128)(2,1)S(1)} collective-permute-done((bf16[2,128,1024]{1,2,0:T(8,128)(2,1)}, bf16[2,128,1024]{1,2,0:T(8,128)(2,1)S(1)}, u32[]{:S(2)}, u32[]{:S(2)}) %collective-permute-start) | collective-permute-done | bytes 524320 | tf_op jit(solution)/shard_map/while/body/eval_jaxpr/ppermute | solution.py:17
  305.2 16.3 %collective-permute-done = bf16[2,128,1024]{1,2,0:T(8,128)(2,1)S(1)} collective-permute-done((bf16[2,128,1024]{1,2,0:T(8,128)(2,1)}, bf16[2,128,1024]{1,2,0:T(8,128)(2,1)S(1)}, u32[]{:S(2)}, u32[]{:S(2)}) %collective-permute-start) | collective-permute-done | bytes 524320 | tf_op jit(solution)/shard_map/while/body/eval_jaxpr/ppermute | solution.py:17
  328.0 27.0 %collective-permute-done = bf16[2,128,1024]{1,2,0:T(8,128)(2,1)S(1)} collective-permute-done((bf16[2,128,1024]{1,2,0:T(8,128)(2,1)}, bf16[2,128,1024]{1,2,0:T(8,128)(2,1)S(1)}, u32[]{:S(2)}, u32[]{:S(2)}) %collective-permute-start) | collective-permute-done | bytes 524320 | tf_op jit(solution)/shard_map/while/body/eval_jaxpr/ppermute | solution.py:17
  361.4 12.7 %collective-permute-done = bf16[2,128,1024]{1,2,0:T(8,128)(2,1)S(1)} collective-permute-done((bf16[2,128,1024]{1,2,0:T(8,128)(2,1)}, bf16[2,128,1024]{1,2,0:T(8,128)(2,1)S(1)}, u32[]{:S(2)}, u32[]{:S(2)}) %collective-permute-start) | collective-permute-done | bytes 524320 | tf_op jit(solution)/shard_map/while/body/eval_jaxpr/ppermute | solution.py:17
  380.5 11.8 %collective-permute-done = bf16[2,128,1024]{1,2,0:T(8,128)(2,1)S(1)} collective-permute-done((bf16[2,128,1024]{1,2,0:T(8,128)(2,1)}, bf16[2,128,1024]{1,2,0:T(8,128)(2,1)S(1)}, u32[]{:S(2)}, u32[]{:S(2)}) %collective-permute-start) | collective-permute-done | bytes 524320 | tf_op jit(solution)/shard_map/while/body/eval_jaxpr/ppermute | solution.py:17
  416.7 11.4 %collective-permute-done = bf16[2,128,1024]{1,2,0:T(8,128)(2,1)S(1)} collective-permute-done((bf16[2,128,1024]{1,2,0:T(8,128)(2,1)}, bf16[2,128,1024]{1,2,0:T(8,128)(2,1)S(1)}, u32[]{:S(2)}, u32[]{:S(2)}) %collective-permute-start) | collective-permute-done | bytes 524320 | tf_op jit(solution)/shard_map/while/body/eval_jaxpr/ppermute | solution.py:17
  434.6 11.4 %collective-permute-done = bf16[2,128,1024]{1,2,0:T(8,128)(2,1)S(1)} collective-permute-done((bf16[2,128,1024]{1,2,0:T(8,128)(2,1)}, bf16[2,128,1024]{1,2,0:T(8,128)(2,1)S(1)}, u32[]{:S(2)}, u32[]{:S(2)}) %collective-permute-start) | collective-permute-done | bytes 524320 | tf_op jit(solution)/shard_map/while/body/eval_jaxpr/ppermute | solution.py:17
  452.5 11.4 %collective-permute-done = bf16[2,128,1024]{1,2,0:T(8,128)(2,1)S(1)} collective-permute-done((bf16[2,128,1024]{1,2,0:T(8,128)(2,1)}, bf16[2,128,1024]{1,2,0:T(8,128)(2,1)S(1)}, u32[]{:S(2)}, u32[]{:S(2)}) %collective-permute-start) | collective-permute-done | bytes 524320 | tf_op jit(solution)/shard_map/while/body/eval_jaxpr/ppermute | solution.py:17
  470.4 11.4 %collective-permute-done = bf16[2,128,1024]{1,2,0:T(8,128)(2,1)S(1)} collective-permute-done((bf16[2,128,1024]{1,2,0:T(8,128)(2,1)}, bf16[2,128,1024]{1,2,0:T(8,128)(2,1)S(1)}, u32[]{:S(2)}, u32[]{:S(2)}) %collective-permute-start) | collective-permute-done | bytes 524320 | tf_op jit(solution)/shard_map/while/body/eval_jaxpr/ppermute | solution.py:17
  488.3 12.2 %collective-permute-done = bf16[2,128,1024]{1,2,0:T(8,128)(2,1)S(1)} collective-permute-done((bf16[2,128,1024]{1,2,0:T(8,128)(2,1)}, bf16[2,128,1024]{1,2,0:T(8,128)(2,1)S(1)}, u32[]{:S(2)}, u32[]{:S(2)}) %collective-permute-start) | collective-permute-done | bytes 524320 | tf_op jit(solution)/shard_map/while/body/eval_jaxpr/ppermute | solution.py:17
  506.9 13.3 %collective-permute-done = bf16[2,128,1024]{1,2,0:T(8,128)(2,1)S(1)} collective-permute-done((bf16[2,128,1024]{1,2,0:T(8,128)(2,1)}, bf16[2,128,1024]{1,2,0:T(8,128)(2,1)S(1)}, u32[]{:S(2)}, u32[]{:S(2)}) %collective-permute-start) | collective-permute-done | bytes 524320 | tf_op jit(solution)/shard_map/while/body/eval_jaxpr/ppermute | solution.py:17
  526.7 14.3 %collective-permute-done = bf16[2,128,1024]{1,2,0:T(8,128)(2,1)S(1)} collective-permute-done((bf16[2,128,1024]{1,2,0:T(8,128)(2,1)}, bf16[2,128,1024]{1,2,0:T(8,128)(2,1)S(1)}, u32[]{:S(2)}, u32[]{:S(2)}) %collective-permute-start) | collective-permute-done | bytes 524320 | tf_op jit(solution)/shard_map/while/body/eval_jaxpr/ppermute | solution.py:17
  547.5 15.4 %collective-permute-done = bf16[2,128,1024]{1,2,0:T(8,128)(2,1)S(1)} collective-permute-done((bf16[2,128,1024]{1,2,0:T(8,128)(2,1)}, bf16[2,128,1024]{1,2,0:T(8,128)(2,1)S(1)}, u32[]{:S(2)}, u32[]{:S(2)}) %collective-permute-start) | collective-permute-done | bytes 524320 | tf_op jit(solution)/shard_map/while/body/eval_jaxpr/ppermute | solution.py:17
  569.4 16.7 %collective-permute-done = bf16[2,128,1024]{1,2,0:T(8,128)(2,1)S(1)} collective-permute-done((bf16[2,128,1024]{1,2,0:T(8,128)(2,1)}, bf16[2,128,1024]{1,2,0:T(8,128)(2,1)S(1)}, u32[]{:S(2)}, u32[]{:S(2)}) %collective-permute-start) | collective-permute-done | bytes 524320 | tf_op jit(solution)/shard_map/while/body/eval_jaxpr/ppermute | solution.py:17
  592.5 16.3 %collective-permute-done = bf16[2,128,1024]{1,2,0:T(8,128)(2,1)S(1)} collective-permute-done((bf16[2,128,1024]{1,2,0:T(8,128)(2,1)}, bf16[2,128,1024]{1,2,0:T(8,128)(2,1)S(1)}, u32[]{:S(2)}, u32[]{:S(2)}) %collective-permute-start) | collective-permute-done | bytes 524320 | tf_op jit(solution)/shard_map/while/body/eval_jaxpr/ppermute | solution.py:17
  615.3 15.5 %collective-permute-done = bf16[2,128,1024]{1,2,0:T(8,128)(2,1)S(1)} collective-permute-done((bf16[2,128,1024]{1,2,0:T(8,128)(2,1)}, bf16[2,128,1024]{1,2,0:T(8,128)(2,1)S(1)}, u32[]{:S(2)}, u32[]{:S(2)}) %collective-permute-start) | collective-permute-done | bytes 524320 | tf_op jit(solution)/shard_map/while/body/eval_jaxpr/ppermute | solution.py:17
  637.2 14.6 %collective-permute-done = bf16[2,128,1024]{1,2,0:T(8,128)(2,1)S(1)} collective-permute-done((bf16[2,128,1024]{1,2,0:T(8,128)(2,1)}, bf16[2,128,1024]{1,2,0:T(8,128)(2,1)S(1)}, u32[]{:S(2)}, u32[]{:S(2)}) %collective-permute-start) | collective-permute-done | bytes 524320 | tf_op jit(solution)/shard_map/while/body/eval_jaxpr/ppermute | solution.py:17
  658.2 13.6 %collective-permute-done = bf16[2,128,1024]{1,2,0:T(8,128)(2,1)S(1)} collective-permute-done((bf16[2,128,1024]{1,2,0:T(8,128)(2,1)}, bf16[2,128,1024]{1,2,0:T(8,128)(2,1)S(1)}, u32[]{:S(2)}, u32[]{:S(2)}) %collective-permute-start) | collective-permute-done | bytes 524320 | tf_op jit(solution)/shard_map/while/body/eval_jaxpr/ppermute | solution.py:17
  678.4 12.7 %collective-permute-done = bf16[2,128,1024]{1,2,0:T(8,128)(2,1)S(1)} collective-permute-done((bf16[2,128,1024]{1,2,0:T(8,128)(2,1)}, bf16[2,128,1024]{1,2,0:T(8,128)(2,1)S(1)}, u32[]{:S(2)}, u32[]{:S(2)}) %collective-permute-start) | collective-permute-done | bytes 524320 | tf_op jit(solution)/shard_map/while/body/eval_jaxpr/ppermute | solution.py:17
  697.5 11.8 %collective-permute-done = bf16[2,128,1024]{1,2,0:T(8,128)(2,1)S(1)} collective-permute-done((bf16[2,128,1024]{1,2,0:T(8,128)(2,1)}, bf16[2,128,1024]{1,2,0:T(8,128)(2,1)S(1)}, u32[]{:S(2)}, u32[]{:S(2)}) %collective-permute-start) | collective-permute-done | bytes 524320 | tf_op jit(solution)/shard_map/while/body/eval_jaxpr/ppermute | solution.py:17
  751.6 12.4 %collective-permute-done = bf16[2,128,1024]{1,2,0:T(8,128)(2,1)S(1)} collective-permute-done((bf16[2,128,1024]{1,2,0:T(8,128)(2,1)}, bf16[2,128,1024]{1,2,0:T(8,128)(2,1)S(1)}, u32[]{:S(2)}, u32[]{:S(2)}) %collective-permute-start) | collective-permute-done | bytes 524320 | tf_op jit(solution)/shard_map/while/body/eval_jaxpr/ppermute | solution.py:17
  770.5 16.8 %collective-permute-done = bf16[2,128,1024]{1,2,0:T(8,128)(2,1)S(1)} collective-permute-done((bf16[2,128,1024]{1,2,0:T(8,128)(2,1)}, bf16[2,128,1024]{1,2,0:T(8,128)(2,1)S(1)}, u32[]{:S(2)}, u32[]{:S(2)}) %collective-permute-start) | collective-permute-done | bytes 524320 | tf_op jit(solution)/shard_map/while/body/eval_jaxpr/ppermute | solution.py:17
  791.8 14.2 %collective-permute-done = bf16[2,128,1024]{1,2,0:T(8,128)(2,1)S(1)} collective-permute-done((bf16[2,128,1024]{1,2,0:T(8,128)(2,1)}, bf16[2,128,1024]{1,2,0:T(8,128)(2,1)S(1)}, u32[]{:S(2)}, u32[]{:S(2)}) %collective-permute-start) | collective-permute-done | bytes 524320 | tf_op jit(solution)/shard_map/while/body/eval_jaxpr/ppermute | solution.py:17
  808.8 15.1 %collective-permute-done = bf16[2,128,1024]{1,2,0:T(8,128)(2,1)S(1)} collective-permute-done((bf16[2,128,1024]{1,2,0:T(8,128)(2,1)}, bf16[2,128,1024]{1,2,0:T(8,128)(2,1)S(1)}, u32[]{:S(2)}, u32[]{:S(2)}) %collective-permute-start) | collective-permute-done | bytes 524320 | tf_op jit(solution)/shard_map/while/body/eval_jaxpr/ppermute | solution.py:17
  826.7 14.2 %collective-permute-done = bf16[2,128,1024]{1,2,0:T(8,128)(2,1)S(1)} collective-permute-done((bf16[2,128,1024]{1,2,0:T(8,128)(2,1)}, bf16[2,128,1024]{1,2,0:T(8,128)(2,1)S(1)}, u32[]{:S(2)}, u32[]{:S(2)}) %collective-permute-start) | collective-permute-done | bytes 524320 | tf_op jit(solution)/shard_map/while/body/eval_jaxpr/ppermute | solution.py:17
  843.7 13.3 %collective-permute-done = bf16[2,128,1024]{1,2,0:T(8,128)(2,1)S(1)} collective-permute-done((bf16[2,128,1024]{1,2,0:T(8,128)(2,1)}, bf16[2,128,1024]{1,2,0:T(8,128)(2,1)S(1)}, u32[]{:S(2)}, u32[]{:S(2)}) %collective-permute-start) | collective-permute-done | bytes 524320 | tf_op jit(solution)/shard_map/while/body/eval_jaxpr/ppermute | solution.py:17
  (554 shorter events, 374.5 us)
Async XLA Ops:
  7.2 252.1 %all-reduce.2.cloned.1.call-start = ((), (), s32[]{:S(2)}) async-start(), calls=%async_computation | async-start | bytes 655360 | tf_op jit(solution)/shard_map/psum | solution.py:99
  219.5 668.6 %all-gather.3.cloned.1.call-start = ((), (), s32[]{:S(2)}) async-start(), calls=%async_computation.1 | async-start | bytes 5406720 | tf_op jit(solution)/shard_map/all_gather | solution.py:101
  276.5 22.3 %collective-permute-start = (bf16[2,128,1024]{1,2,0:T(8,128)(2,1)}, bf16[2,128,1024]{1,2,0:T(8,128)(2,1)S(1)}, u32[]{:S(2)}, u32[]{:S(2)}) collective-permute-start(bf16[2,128,1024]{1,2,0:T(8,128)(2,1)} %get-tuple-element.555), channel_id=1, source_target_pairs={{0,8},{8,16},{16,24},{24,32},{32,40},{40,48},{48,56},{56,64},{64,7... | collective-permute-start | bytes 1572872 | tf_op jit(solution)/shard_map/while/body/eval_jaxpr/ppermute | solution.py:17
  303.2 18.3 %collective-permute-start = (bf16[2,128,1024]{1,2,0:T(8,128)(2,1)}, bf16[2,128,1024]{1,2,0:T(8,128)(2,1)S(1)}, u32[]{:S(2)}, u32[]{:S(2)}) collective-permute-start(bf16[2,128,1024]{1,2,0:T(8,128)(2,1)} %get-tuple-element.555), channel_id=1, source_target_pairs={{0,8},{8,16},{16,24},{24,32},{32,40},{40,48},{48,56},{56,64},{64,7... | collective-permute-start | bytes 1572872 | tf_op jit(solution)/shard_map/while/body/eval_jaxpr/ppermute | solution.py:17
  326.0 28.9 %collective-permute-start = (bf16[2,128,1024]{1,2,0:T(8,128)(2,1)}, bf16[2,128,1024]{1,2,0:T(8,128)(2,1)S(1)}, u32[]{:S(2)}, u32[]{:S(2)}) collective-permute-start(bf16[2,128,1024]{1,2,0:T(8,128)(2,1)} %get-tuple-element.555), channel_id=1, source_target_pairs={{0,8},{8,16},{16,24},{24,32},{32,40},{40,48},{48,56},{56,64},{64,7... | collective-permute-start | bytes 1572872 | tf_op jit(solution)/shard_map/while/body/eval_jaxpr/ppermute | solution.py:17
  359.4 14.6 %collective-permute-start = (bf16[2,128,1024]{1,2,0:T(8,128)(2,1)}, bf16[2,128,1024]{1,2,0:T(8,128)(2,1)S(1)}, u32[]{:S(2)}, u32[]{:S(2)}) collective-permute-start(bf16[2,128,1024]{1,2,0:T(8,128)(2,1)} %get-tuple-element.555), channel_id=1, source_target_pairs={{0,8},{8,16},{16,24},{24,32},{32,40},{40,48},{48,56},{56,64},{64,7... | collective-permute-start | bytes 1572872 | tf_op jit(solution)/shard_map/while/body/eval_jaxpr/ppermute | solution.py:17
  378.6 13.7 %collective-permute-start = (bf16[2,128,1024]{1,2,0:T(8,128)(2,1)}, bf16[2,128,1024]{1,2,0:T(8,128)(2,1)S(1)}, u32[]{:S(2)}, u32[]{:S(2)}) collective-permute-start(bf16[2,128,1024]{1,2,0:T(8,128)(2,1)} %get-tuple-element.555), channel_id=1, source_target_pairs={{0,8},{8,16},{16,24},{24,32},{32,40},{40,48},{48,56},{56,64},{64,7... | collective-permute-start | bytes 1572872 | tf_op jit(solution)/shard_map/while/body/eval_jaxpr/ppermute | solution.py:17
  396.8 13.4 %collective-permute-start = (bf16[2,128,1024]{1,2,0:T(8,128)(2,1)}, bf16[2,128,1024]{1,2,0:T(8,128)(2,1)S(1)}, u32[]{:S(2)}, u32[]{:S(2)}) collective-permute-start(bf16[2,128,1024]{1,2,0:T(8,128)(2,1)} %get-tuple-element.555), channel_id=1, source_target_pairs={{0,8},{8,16},{16,24},{24,32},{32,40},{40,48},{48,56},{56,64},{64,7... | collective-permute-start | bytes 1572872 | tf_op jit(solution)/shard_map/while/body/eval_jaxpr/ppermute | solution.py:17
  414.7 13.4 %collective-permute-start = (bf16[2,128,1024]{1,2,0:T(8,128)(2,1)}, bf16[2,128,1024]{1,2,0:T(8,128)(2,1)S(1)}, u32[]{:S(2)}, u32[]{:S(2)}) collective-permute-start(bf16[2,128,1024]{1,2,0:T(8,128)(2,1)} %get-tuple-element.555), channel_id=1, source_target_pairs={{0,8},{8,16},{16,24},{24,32},{32,40},{40,48},{48,56},{56,64},{64,7... | collective-permute-start | bytes 1572872 | tf_op jit(solution)/shard_map/while/body/eval_jaxpr/ppermute | solution.py:17
  432.6 13.4 %collective-permute-start = (bf16[2,128,1024]{1,2,0:T(8,128)(2,1)}, bf16[2,128,1024]{1,2,0:T(8,128)(2,1)S(1)}, u32[]{:S(2)}, u32[]{:S(2)}) collective-permute-start(bf16[2,128,1024]{1,2,0:T(8,128)(2,1)} %get-tuple-element.555), channel_id=1, source_target_pairs={{0,8},{8,16},{16,24},{24,32},{32,40},{40,48},{48,56},{56,64},{64,7... | collective-permute-start | bytes 1572872 | tf_op jit(solution)/shard_map/while/body/eval_jaxpr/ppermute | solution.py:17
  450.5 13.4 %collective-permute-start = (bf16[2,128,1024]{1,2,0:T(8,128)(2,1)}, bf16[2,128,1024]{1,2,0:T(8,128)(2,1)S(1)}, u32[]{:S(2)}, u32[]{:S(2)}) collective-permute-start(bf16[2,128,1024]{1,2,0:T(8,128)(2,1)} %get-tuple-element.555), channel_id=1, source_target_pairs={{0,8},{8,16},{16,24},{24,32},{32,40},{40,48},{48,56},{56,64},{64,7... | collective-permute-start | bytes 1572872 | tf_op jit(solution)/shard_map/while/body/eval_jaxpr/ppermute | solution.py:17
  468.4 13.4 %collective-permute-start = (bf16[2,128,1024]{1,2,0:T(8,128)(2,1)}, bf16[2,128,1024]{1,2,0:T(8,128)(2,1)S(1)}, u32[]{:S(2)}, u32[]{:S(2)}) collective-permute-start(bf16[2,128,1024]{1,2,0:T(8,128)(2,1)} %get-tuple-element.555), channel_id=1, source_target_pairs={{0,8},{8,16},{16,24},{24,32},{32,40},{40,48},{48,56},{56,64},{64,7... | collective-permute-start | bytes 1572872 | tf_op jit(solution)/shard_map/while/body/eval_jaxpr/ppermute | solution.py:17
  486.4 14.1 %collective-permute-start = (bf16[2,128,1024]{1,2,0:T(8,128)(2,1)}, bf16[2,128,1024]{1,2,0:T(8,128)(2,1)S(1)}, u32[]{:S(2)}, u32[]{:S(2)}) collective-permute-start(bf16[2,128,1024]{1,2,0:T(8,128)(2,1)} %get-tuple-element.555), channel_id=1, source_target_pairs={{0,8},{8,16},{16,24},{24,32},{32,40},{40,48},{48,56},{56,64},{64,7... | collective-permute-start | bytes 1572872 | tf_op jit(solution)/shard_map/while/body/eval_jaxpr/ppermute | solution.py:17
  505.0 15.2 %collective-permute-start = (bf16[2,128,1024]{1,2,0:T(8,128)(2,1)}, bf16[2,128,1024]{1,2,0:T(8,128)(2,1)S(1)}, u32[]{:S(2)}, u32[]{:S(2)}) collective-permute-start(bf16[2,128,1024]{1,2,0:T(8,128)(2,1)} %get-tuple-element.555), channel_id=1, source_target_pairs={{0,8},{8,16},{16,24},{24,32},{32,40},{40,48},{48,56},{56,64},{64,7... | collective-permute-start | bytes 1572872 | tf_op jit(solution)/shard_map/while/body/eval_jaxpr/ppermute | solution.py:17
  524.7 16.3 %collective-permute-start = (bf16[2,128,1024]{1,2,0:T(8,128)(2,1)}, bf16[2,128,1024]{1,2,0:T(8,128)(2,1)S(1)}, u32[]{:S(2)}, u32[]{:S(2)}) collective-permute-start(bf16[2,128,1024]{1,2,0:T(8,128)(2,1)} %get-tuple-element.555), channel_id=1, source_target_pairs={{0,8},{8,16},{16,24},{24,32},{32,40},{40,48},{48,56},{56,64},{64,7... | collective-permute-start | bytes 1572872 | tf_op jit(solution)/shard_map/while/body/eval_jaxpr/ppermute | solution.py:17
  545.5 17.4 %collective-permute-start = (bf16[2,128,1024]{1,2,0:T(8,128)(2,1)}, bf16[2,128,1024]{1,2,0:T(8,128)(2,1)S(1)}, u32[]{:S(2)}, u32[]{:S(2)}) collective-permute-start(bf16[2,128,1024]{1,2,0:T(8,128)(2,1)} %get-tuple-element.555), channel_id=1, source_target_pairs={{0,8},{8,16},{16,24},{24,32},{32,40},{40,48},{48,56},{56,64},{64,7... | collective-permute-start | bytes 1572872 | tf_op jit(solution)/shard_map/while/body/eval_jaxpr/ppermute | solution.py:17
  567.4 18.6 %collective-permute-start = (bf16[2,128,1024]{1,2,0:T(8,128)(2,1)}, bf16[2,128,1024]{1,2,0:T(8,128)(2,1)S(1)}, u32[]{:S(2)}, u32[]{:S(2)}) collective-permute-start(bf16[2,128,1024]{1,2,0:T(8,128)(2,1)} %get-tuple-element.555), channel_id=1, source_target_pairs={{0,8},{8,16},{16,24},{24,32},{32,40},{40,48},{48,56},{56,64},{64,7... | collective-permute-start | bytes 1572872 | tf_op jit(solution)/shard_map/while/body/eval_jaxpr/ppermute | solution.py:17
  590.5 18.2 %collective-permute-start = (bf16[2,128,1024]{1,2,0:T(8,128)(2,1)}, bf16[2,128,1024]{1,2,0:T(8,128)(2,1)S(1)}, u32[]{:S(2)}, u32[]{:S(2)}) collective-permute-start(bf16[2,128,1024]{1,2,0:T(8,128)(2,1)} %get-tuple-element.555), channel_id=1, source_target_pairs={{0,8},{8,16},{16,24},{24,32},{32,40},{40,48},{48,56},{56,64},{64,7... | collective-permute-start | bytes 1572872 | tf_op jit(solution)/shard_map/while/body/eval_jaxpr/ppermute | solution.py:17
  613.3 17.4 %collective-permute-start = (bf16[2,128,1024]{1,2,0:T(8,128)(2,1)}, bf16[2,128,1024]{1,2,0:T(8,128)(2,1)S(1)}, u32[]{:S(2)}, u32[]{:S(2)}) collective-permute-start(bf16[2,128,1024]{1,2,0:T(8,128)(2,1)} %get-tuple-element.555), channel_id=1, source_target_pairs={{0,8},{8,16},{16,24},{24,32},{32,40},{40,48},{48,56},{56,64},{64,7... | collective-permute-start | bytes 1572872 | tf_op jit(solution)/shard_map/while/body/eval_jaxpr/ppermute | solution.py:17
  635.3 16.5 %collective-permute-start = (bf16[2,128,1024]{1,2,0:T(8,128)(2,1)}, bf16[2,128,1024]{1,2,0:T(8,128)(2,1)S(1)}, u32[]{:S(2)}, u32[]{:S(2)}) collective-permute-start(bf16[2,128,1024]{1,2,0:T(8,128)(2,1)} %get-tuple-element.555), channel_id=1, source_target_pairs={{0,8},{8,16},{16,24},{24,32},{32,40},{40,48},{48,56},{56,64},{64,7... | collective-permute-start | bytes 1572872 | tf_op jit(solution)/shard_map/while/body/eval_jaxpr/ppermute | solution.py:17
  656.3 15.6 %collective-permute-start = (bf16[2,128,1024]{1,2,0:T(8,128)(2,1)}, bf16[2,128,1024]{1,2,0:T(8,128)(2,1)S(1)}, u32[]{:S(2)}, u32[]{:S(2)}) collective-permute-start(bf16[2,128,1024]{1,2,0:T(8,128)(2,1)} %get-tuple-element.555), channel_id=1, source_target_pairs={{0,8},{8,16},{16,24},{24,32},{32,40},{40,48},{48,56},{56,64},{64,7... | collective-permute-start | bytes 1572872 | tf_op jit(solution)/shard_map/while/body/eval_jaxpr/ppermute | solution.py:17
  676.4 14.7 %collective-permute-start = (bf16[2,128,1024]{1,2,0:T(8,128)(2,1)}, bf16[2,128,1024]{1,2,0:T(8,128)(2,1)S(1)}, u32[]{:S(2)}, u32[]{:S(2)}) collective-permute-start(bf16[2,128,1024]{1,2,0:T(8,128)(2,1)} %get-tuple-element.555), channel_id=1, source_target_pairs={{0,8},{8,16},{16,24},{24,32},{32,40},{40,48},{48,56},{56,64},{64,7... | collective-permute-start | bytes 1572872 | tf_op jit(solution)/shard_map/while/body/eval_jaxpr/ppermute | solution.py:17
  695.6 13.7 %collective-permute-start = (bf16[2,128,1024]{1,2,0:T(8,128)(2,1)}, bf16[2,128,1024]{1,2,0:T(8,128)(2,1)S(1)}, u32[]{:S(2)}, u32[]{:S(2)}) collective-permute-start(bf16[2,128,1024]{1,2,0:T(8,128)(2,1)} %get-tuple-element.555), channel_id=1, source_target_pairs={{0,8},{8,16},{16,24},{24,32},{32,40},{40,48},{48,56},{56,64},{64,7... | collective-permute-start | bytes 1572872 | tf_op jit(solution)/shard_map/while/body/eval_jaxpr/ppermute | solution.py:17
  713.9 13.4 %collective-permute-start = (bf16[2,128,1024]{1,2,0:T(8,128)(2,1)}, bf16[2,128,1024]{1,2,0:T(8,128)(2,1)S(1)}, u32[]{:S(2)}, u32[]{:S(2)}) collective-permute-start(bf16[2,128,1024]{1,2,0:T(8,128)(2,1)} %get-tuple-element.555), channel_id=1, source_target_pairs={{0,8},{8,16},{16,24},{24,32},{32,40},{40,48},{48,56},{56,64},{64,7... | collective-permute-start | bytes 1572872 | tf_op jit(solution)/shard_map/while/body/eval_jaxpr/ppermute | solution.py:17
  731.8 13.4 %collective-permute-start = (bf16[2,128,1024]{1,2,0:T(8,128)(2,1)}, bf16[2,128,1024]{1,2,0:T(8,128)(2,1)S(1)}, u32[]{:S(2)}, u32[]{:S(2)}) collective-permute-start(bf16[2,128,1024]{1,2,0:T(8,128)(2,1)} %get-tuple-element.555), channel_id=1, source_target_pairs={{0,8},{8,16},{16,24},{24,32},{32,40},{40,48},{48,56},{56,64},{64,7... | collective-permute-start | bytes 1572872 | tf_op jit(solution)/shard_map/while/body/eval_jaxpr/ppermute | solution.py:17
  749.7 14.4 %collective-permute-start = (bf16[2,128,1024]{1,2,0:T(8,128)(2,1)}, bf16[2,128,1024]{1,2,0:T(8,128)(2,1)S(1)}, u32[]{:S(2)}, u32[]{:S(2)}) collective-permute-start(bf16[2,128,1024]{1,2,0:T(8,128)(2,1)} %get-tuple-element.555), channel_id=1, source_target_pairs={{0,8},{8,16},{16,24},{24,32},{32,40},{40,48},{48,56},{56,64},{64,7... | collective-permute-start | bytes 1572872 | tf_op jit(solution)/shard_map/while/body/eval_jaxpr/ppermute | solution.py:17
  768.6 18.8 %collective-permute-start = (bf16[2,128,1024]{1,2,0:T(8,128)(2,1)}, bf16[2,128,1024]{1,2,0:T(8,128)(2,1)S(1)}, u32[]{:S(2)}, u32[]{:S(2)}) collective-permute-start(bf16[2,128,1024]{1,2,0:T(8,128)(2,1)} %get-tuple-element.555), channel_id=1, source_target_pairs={{0,8},{8,16},{16,24},{24,32},{32,40},{40,48},{48,56},{56,64},{64,7... | collective-permute-start | bytes 1572872 | tf_op jit(solution)/shard_map/while/body/eval_jaxpr/ppermute | solution.py:17
  788.1 17.9 %collective-permute-start = (bf16[2,128,1024]{1,2,0:T(8,128)(2,1)}, bf16[2,128,1024]{1,2,0:T(8,128)(2,1)S(1)}, u32[]{:S(2)}, u32[]{:S(2)}) collective-permute-start(bf16[2,128,1024]{1,2,0:T(8,128)(2,1)} %get-tuple-element.555), channel_id=1, source_target_pairs={{0,8},{8,16},{16,24},{24,32},{32,40},{40,48},{48,56},{56,64},{64,7... | collective-permute-start | bytes 1572872 | tf_op jit(solution)/shard_map/while/body/eval_jaxpr/ppermute | solution.py:17
  806.9 17.1 %collective-permute-start = (bf16[2,128,1024]{1,2,0:T(8,128)(2,1)}, bf16[2,128,1024]{1,2,0:T(8,128)(2,1)S(1)}, u32[]{:S(2)}, u32[]{:S(2)}) collective-permute-start(bf16[2,128,1024]{1,2,0:T(8,128)(2,1)} %get-tuple-element.555), channel_id=1, source_target_pairs={{0,8},{8,16},{16,24},{24,32},{32,40},{40,48},{48,56},{56,64},{64,7... | collective-permute-start | bytes 1572872 | tf_op jit(solution)/shard_map/while/body/eval_jaxpr/ppermute | solution.py:17
  824.8 16.1 %collective-permute-start = (bf16[2,128,1024]{1,2,0:T(8,128)(2,1)}, bf16[2,128,1024]{1,2,0:T(8,128)(2,1)S(1)}, u32[]{:S(2)}, u32[]{:S(2)}) collective-permute-start(bf16[2,128,1024]{1,2,0:T(8,128)(2,1)} %get-tuple-element.555), channel_id=1, source_target_pairs={{0,8},{8,16},{16,24},{24,32},{32,40},{40,48},{48,56},{56,64},{64,7... | collective-permute-start | bytes 1572872 | tf_op jit(solution)/shard_map/while/body/eval_jaxpr/ppermute | solution.py:17
  841.7 15.2 %collective-permute-start = (bf16[2,128,1024]{1,2,0:T(8,128)(2,1)}, bf16[2,128,1024]{1,2,0:T(8,128)(2,1)S(1)}, u32[]{:S(2)}, u32[]{:S(2)}) collective-permute-start(bf16[2,128,1024]{1,2,0:T(8,128)(2,1)} %get-tuple-element.555), channel_id=1, source_target_pairs={{0,8},{8,16},{16,24},{24,32},{32,40},{40,48},{48,56},{56,64},{64,7... | collective-permute-start | bytes 1572872 | tf_op jit(solution)/shard_map/while/body/eval_jaxpr/ppermute | solution.py:17
  872.0 13.4 %collective-permute-start = (bf16[2,128,1024]{1,2,0:T(8,128)(2,1)}, bf16[2,128,1024]{1,2,0:T(8,128)(2,1)S(1)}, u32[]{:S(2)}, u32[]{:S(2)}) collective-permute-start(bf16[2,128,1024]{1,2,0:T(8,128)(2,1)} %get-tuple-element.555), channel_id=1, source_target_pairs={{0,8},{8,16},{16,24},{24,32},{32,40},{40,48},{48,56},{56,64},{64,7... | collective-permute-start | bytes 1572872 | tf_op jit(solution)/shard_map/while/body/eval_jaxpr/ppermute | solution.py:17
  (70 other events, 1534.8 us)
Sparse Core Ops, SparseCore 0:
  219.6 39.7 all-reduce.1
  263.6 94.8 all-gather.2
where the time goes:
time: 914 us; the launch traced here: 910 us
  waiting for transfers between devices  472 us (52%)
  blocking collectives  197 us (22%)
  local copies, waits for them, and re-layouts  69.7 us (8%)
  starting transfers between devices  62.5 us (7%)
  other arithmetic  55.2 us (6%)
  matrix products  36.4 us (4%)
  between operations  15.1 us (2%)
    ppermute x31, waiting for transfers between devices, shifted(): lax.ppermute(value, axis, [(source, source + steps) for source in range(l...  432 us
    ppermute x31, starting transfers between devices, shifted(): lax.ppermute(value, axis, [(source, source + steps) for source in range(l...  62.5 us
    all_gather x1, blocking collectives, shards(): lax.all_gather(rs_key, 'blk', axis=0, tiled=True)  52.6 us
    all_gather x1, blocking collectives, shards(): lax.all_gather(rs_value, 'blk', axis=0, tiled=True)  49.1 us
    all_gather x1, blocking collectives, shards(): lax.all_gather(rs_query, 'blk', axis=0, tiled=True)  48 us
    all_gather x1, blocking collectives, shards(): lax.all_gather(rs_out, 'blk', axis=1, tiled=True)  47.8 us
    psum x1, waiting for transfers between devices, shards(): summed = lax.psum(partial_out, 'img')  39.8 us
    cond x120, local copies, waits for them, and re-layouts  30.7 us
  transfers between devices with their start and end apart: 33, of which 32 were waited for; matrix products, arithmetic and copies ran while one was open for 12% of the time, Pallas kernels for 0%

commit v1 on v0

v1 whole, which is shorter than its diff:
```python
import functools

import jax
import jax.numpy as jnp
from jax import lax
from jax.experimental import pallas as pl
from jax.experimental.pallas import tpu as pltpu
from jax.sharding import Mesh
from jax.sharding import PartitionSpec as P

HD = 128
RHD = 96
CITE = 3
BLK = ("y", "z")
IMG = ("xl", "core")
LOG2E = 1.4426950408889634

epsilon = 1e-05


def layer_norm(values, gain):
    values = values.astype(jnp.float32)
    center = jnp.mean(values, -1, keepdims=True)
    spread = jnp.mean(jnp.square(values - center), -1, keepdims=True)
    return (values - center) * lax.rsqrt(spread + epsilon) * gain


def attend(scores, visible, value_rows):
    scores = jnp.where(visible, scores, -1e30)
    row_peak = jnp.max(scores, -1, keepdims=True)
    weights = jnp.where(visible, jnp.exp(scores - row_peak), 0.0)
    row_total = jnp.sum(weights, -1)
    context = jnp.einsum(
        "hqk,khd->qhd", weights.astype(jnp.bfloat16), value_rows, preferred_element_type=jnp.float32
    )
    return context / jnp.transpose(row_total)[:, :, None]


def self_kernel(own_ref, q_ref, kv_ref, o_ref, s_ref):
    own = own_ref[0]
    pieces, blocks, rows2, width = kv_ref.shape
    rows = rows2 // 2
    group = 128 // rows
    factor = width**-0.5 * LOG2E
    index_q = lax.broadcasted_iota(jnp.int32, (128, 128), 0)
    index_k = lax.broadcasted_iota(jnp.int32, (128, 128), 1)
    place_q = index_q // rows * 128 + own * rows + index_q % rows
    place_k = index_k // rows * 128 + index_k % rows
    for turn in range(blocks // group):
        first = turn * group
        query = q_ref[first : first + group].reshape(128, width)
        span = (first + group) * rows
        peak = None
        for piece in range(pieces):
            keys = kv_ref[piece, 0 : first + group, 0:rows, :].reshape(span, width)
            scores = lax.dot_general(
                query, keys, (((1,), (1,)), ((), ())), preferred_element_type=jnp.float32
            )
            scores = scores * factor
            tail = jnp.where(place_k + piece * rows <= place_q, scores[:, span - 128 :], -1e30)
            s_ref[piece, :, span - 128 : span] = tail
            top = jnp.max(tail, -1, keepdims=True)
            if span > 128:
                s_ref[piece, :, 0 : span - 128] = scores[:, : span - 128]
                top = jnp.maximum(top, jnp.max(scores[:, : span - 128], -1, keepdims=True))
            peak = top if peak is None else jnp.maximum(peak, top)
        total = jnp.zeros((128, 1), jnp.float32)
        context = jnp.zeros((128, width), jnp.float32)
        for piece in range(pieces):
            weights = jnp.exp2(s_ref[piece, :, 0:span] - peak)
            total = total + jnp.sum(weights, -1, keepdims=True)
            values = kv_ref[piece, 0 : first + group, rows : 2 * rows, :].reshape(span, width)
            context = context + jnp.dot(
                weights.astype(jnp.bfloat16), values, preferred_element_type=jnp.float32
            )
        o_ref[first : first + group] = (
            (context / total).astype(jnp.bfloat16).reshape(group, rows, width)
        )


def self_attention(own, query, pairs):
    pieces, blocks, rows2, width = pairs.shape
    vmem = pl.BlockSpec(memory_space=pltpu.VMEM)
    return pl.pallas_call(
        self_kernel,
        out_shape=jax.ShapeDtypeStruct((blocks, rows2 // 2, width), jnp.bfloat16),
        in_specs=[pl.BlockSpec(memory_space=pltpu.SMEM), vmem, vmem],
        out_specs=vmem,
        scratch_shapes=[pltpu.VMEM((pieces, 128, blocks * rows2 // 2), jnp.float32)],
        compiler_params=pltpu.CompilerParams(vmem_limit_bytes=32 * 1024 * 1024),
        cost_estimate=pl.CostEstimate(
            flops=1200000000, bytes_accessed=3000000, transcendentals=2400000
        ),
        name="self_attention",
    )(own, query, pairs)


def by_head(rows, y_size, z_size):
    tokens = rows.shape[0]
    split = rows.reshape(y_size, tokens // y_size, z_size, HD)
    return jnp.transpose(split, (0, 2, 1, 3)).reshape(y_size * z_size, tokens // y_size, HD)


def shards(
    features,
    latents,
    context_gain,
    latent_gain,
    final_gain,
    rs_query,
    rs_key,
    rs_value,
    rs_out,
    x_key,
    x_value,
    text_query,
    text_key,
    text_value,
    cross_query,
    cross_gate,
    image_pos,
):
    y_size, z_size = lax.axis_size("y"), lax.axis_size("z")
    blocks = y_size * z_size
    heads_of = lax.axis_size(IMG)
    shard_index = lax.axis_index(BLK)
    own_y = lax.axis_index("y")
    tokens = text_query.shape[0]
    local_heads = text_query.shape[1] // HD
    piece = tokens // y_size
    latent_rows, full_width = latents.shape

    packed = jnp.concatenate(
        [by_head(part, y_size, z_size) for part in (text_query, text_key, text_value)], 1
    )
    packed = lax.all_to_all(packed, BLK, 0, 0, tiled=True)
    head_query = packed[:, 0:piece]
    pairs = lax.all_gather(packed[:, piece:], "y", axis=0, tiled=False)

    columns = rs_query.shape[1]
    bundle = jnp.concatenate([rs_query, rs_key, rs_value, jnp.transpose(rs_out)], 1)
    bundle = lax.all_gather(bundle, BLK, axis=0, tiled=True)
    latent_norm = layer_norm(latents, latent_gain).astype(jnp.bfloat16)
    feature_norm = layer_norm(features[0], context_gain).astype(jnp.bfloat16)
    context = jnp.concatenate([feature_norm, latent_norm], 0)
    query_rows = jnp.dot(latent_norm, bundle[:, :columns], preferred_element_type=jnp.float32)
    pair_rows = jnp.dot(
        context, bundle[:, columns : 3 * columns], preferred_element_type=jnp.float32
    )
    head_count = columns // RHD
    query_rows = query_rows.astype(jnp.bfloat16).reshape(latent_rows, head_count, RHD)
    pair_rows = pair_rows.astype(jnp.bfloat16)
    key_rows = pair_rows[:, :columns].reshape(-1, head_count, RHD)
    value_rows = pair_rows[:, columns:].reshape(-1, head_count, RHD)
    scores = jnp.einsum(
        "qhd,khd->hqk", query_rows, key_rows, preferred_element_type=jnp.float32
    ) * RHD ** (-0.5)
    head_context = (
        attend(scores, True, value_rows).astype(jnp.bfloat16).reshape(latent_rows, columns)
    )
    partial_out = lax.dot_general(
        head_context,
        bundle[:, 3 * columns :],
        (((1,), (1,)), ((), ())),
        preferred_element_type=jnp.float32,
    )
    quarter = latent_rows // heads_of
    summed = lax.psum_scatter(partial_out, IMG, scatter_dimension=0, tiled=True)
    own_latents = lax.dynamic_slice_in_dim(latents, lax.axis_index(IMG) * quarter, quarter, 0)
    resampled = layer_norm(own_latents.astype(jnp.float32) + summed, final_gain)
    resampled = resampled.astype(jnp.bfloat16)

    starts = jnp.arange(blocks, dtype=jnp.int32) * tokens
    image_rank = jnp.sum((image_pos[None, :] < image_pos[:, None]).astype(jnp.int32), axis=1)
    first_all = jnp.sum((image_pos[None, :] < starts[:, None]).astype(jnp.int32), axis=1)
    wanted = first_all[:, None] - 1 + jnp.arange(CITE + 1, dtype=jnp.int32)
    choice = (image_rank[None, None, :] == wanted[:, :, None]).astype(jnp.bfloat16)

    slots = CITE + 1
    spread = resampled.reshape(blocks, -1)
    spread = lax.all_to_all(spread, BLK, 0, 0, tiled=True)
    chosen = jnp.dot(
        choice.reshape(blocks * slots, -1), spread, preferred_element_type=jnp.float32
    ).astype(jnp.bfloat16)
    chosen = lax.all_to_all(chosen.reshape(blocks, slots, -1), BLK, 0, 0, tiled=True)
    chosen = chosen.reshape(quarter, blocks // quarter, slots, -1)
    chosen = jnp.transpose(chosen, (2, 0, 1, 3)).reshape(slots * quarter, full_width)
    window = lax.all_gather(chosen, IMG, axis=0, tiled=True)

    cross_keys = jnp.dot(window, x_key, preferred_element_type=jnp.float32).astype(jnp.bfloat16)
    cross_values = jnp.dot(window, x_value, preferred_element_type=jnp.float32).astype(jnp.bfloat16)
    start_row = shard_index * tokens
    positions = start_row + jnp.arange(tokens, dtype=jnp.int32)
    token_rank = jnp.sum((image_pos[None, :] <= positions[:, None]).astype(jnp.int32), axis=1) - 1
    first_image = jnp.sum((image_pos < start_row).astype(jnp.int32))
    local_slot = token_rank - first_image + 1
    key_slot = jnp.arange(slots * latent_rows, dtype=jnp.int32) // quarter % slots
    cross_visible = (key_slot[None, :] == local_slot[:, None])[None]
    cross_rows = cross_query.reshape(tokens, local_heads, HD)
    cross_scores = jnp.einsum(
        "thd,khd->htk",
        cross_rows,
        cross_keys.reshape(-1, local_heads, HD),
        preferred_element_type=jnp.float32,
    ) * HD ** (-0.5)
    cross_context = attend(cross_scores, cross_visible, cross_values.reshape(-1, local_heads, HD))
    cross_context = cross_context * jnp.tanh(cross_gate).reshape(local_heads, HD)
    cross_out = (
        jnp.where((token_rank >= 0)[:, None, None], cross_context, 0.0)
        .reshape(tokens, -1)
        .astype(jnp.bfloat16)
    )

    self_rows = self_attention(own_y.astype(jnp.int32)[None], head_query, pairs)
    self_rows = lax.all_to_all(self_rows, BLK, 0, 0, tiled=True)
    self_out = jnp.transpose(self_rows.reshape(y_size, z_size, piece, HD), (0, 2, 1, 3))
    return (cross_out, self_out.reshape(tokens, -1))


def solution(mesh):
    blocks, heads_of, documents = mesh.devices.shape
    z_size = 8
    devices = mesh.devices.reshape(blocks // z_size, z_size, 2, heads_of // 2, documents)
    inner = Mesh(devices, ("y", "z", "xl", "core", "doc"))
    rows = ("doc", "y", "z")
    in_specs = (
        P(rows, None, None),
        P(),
        P(),
        P(),
        P(),
        P(BLK, IMG),
        P(BLK, IMG),
        P(BLK, IMG),
        P(IMG, BLK),
        P(None, IMG),
        P(None, IMG),
        P(rows, IMG),
        P(rows, IMG),
        P(rows, IMG),
        P(rows, IMG),
        P(IMG),
        P("doc"),
    )
    out_specs = (P(rows, IMG), P(rows, IMG))
    return jax.shard_map(
        shards, mesh=inner, in_specs=in_specs, out_specs=out_specs, check_vma=False
    )
```

time: 914 us -> 217 us (0.24)
  waiting for transfers between devices: 472 us -> 101 us
  blocking collectives: 197 us -> 8.15 us
  local copies, waits for them, and re-layouts: 69.7 us -> 15.8 us
  other arithmetic: 55.2 us -> 11.4 us
  starting transfers between devices: 62.5 us -> 37.4 us
  matrix products: 36.4 us -> 17.5 us
    ppermute x31 -> x0, waiting for transfers between devices: 432 us -> none  [shifted(): lax.ppermute(value, axis, [(source, source + steps) for source in range(l...]
    all_gather x4 -> x1, blocking collectives: 197 us -> 8.15 us  [shards(): window = lax.all_gather(chosen, IMG, axis=0, tiled=True)]
    all_gather x1 -> x2, waiting for transfers between devices: 0.01 us -> 69.6 us  [the longest x1 69.6 us: shards(): bundle = lax.all_gather(bundle, BLK, axis=0, tiled=True)]
    ppermute x31 -> x0, starting transfers between devices: 62.5 us -> none  [shifted(): lax.ppermute(value, axis, [(source, source + steps) for source in range(l...]
    psum x1 -> x0, waiting for transfers between devices: 39.8 us -> none  [shards(): summed = lax.psum(partial_out, 'img')]
    all_to_all x0 -> x4, starting transfers between devices: none -> 37.3 us  [the longest x1 11.7 us: shards(): packed = lax.all_to_all(packed, BLK, 0, 0, tiled=True)]
    cond x120 -> x0, local copies, waits for them, and re-layouts: 30.7 us -> none
    while x31 -> x0, local copies, waits for them, and re-layouts: 25.1 us -> none
  transfers between devices with their start and end apart: 33 -> 7, of which waited for: 32 -> 5; matrix products, arithmetic and copies ran while one was open for 12% -> 14% of each run, Pallas kernels for 0% -> 3%
where the time goes in v1:
time: 217 us; the launch traced here: 213 us
  waiting for transfers between devices  101 us (47%)
  starting transfers between devices  37.4 us (17%)
  matrix products  17.5 us (8%)
  between operations  15.9 us (7%)
  local copies, waits for them, and re-layouts  15.8 us (7%)
  other arithmetic  11.4 us (5%)
  blocking collectives  8.15 us (4%)
  Pallas kernels  5.8 us (3%)
    all_gather x1, waiting for transfers between devices, shards(): bundle = lax.all_gather(bundle, BLK, axis=0, tiled=True)  69.6 us
    reduce_scatter x1, waiting for transfers between devices, shards(): summed = lax.psum_scatter(partial_out, IMG, scatter_dimension=0, tiled=True)  14.2 us
    all_to_all x1, starting transfers between devices, shards(): packed = lax.all_to_all(packed, BLK, 0, 0, tiled=True)  11.7 us
    all_to_all x1, starting transfers between devices, shards(): spread = lax.all_to_all(spread, BLK, 0, 0, tiled=True)  10.2 us
    all_to_all x1, starting transfers between devices, shards(): self_rows = lax.all_to_all(self_rows, BLK, 0, 0, tiled=True)  9.16 us
    all_to_all x1, waiting for transfers between devices, shards(): self_rows = lax.all_to_all(self_rows, BLK, 0, 0, tiled=True)  8.68 us
    all_gather x1, blocking collectives, shards(): window = lax.all_gather(chosen, IMG, axis=0, tiled=True)  8.15 us
    all_to_all x1, waiting for transfers between devices, shards(): lax.all_to_all(chosen.reshape(blocks, slots, -1), BLK, 0, 0, tiled=True)  7.65 us
  transfers between devices with their start and end apart: 7, of which 5 were waited for; matrix products, arithmetic and copies ran while one was open for 14% of the time, Pallas kernels for 3%

profile of v1, /device:TPU:26, one launch (start us, length us, event | category | flops | bytes accessed | tf_op | source)
XLA Modules:
  0.0 212.9 jit_solution(9792624980512087363)
XLA Ops:
  8.1 1.6 pad_maximum_fusion.1
  9.7 1.0 copy.97
  10.8 1.0 copy.98
  12.0 0.9 pad_maximum_fusion
  12.9 11.7 %all-to-all-start.2 = ((bf16[32,96,128]{2,1,0:T(8,128)(2,1)}), bf16[32,96,128]{2,1,0:T(8,128)(2,1)}, u32[]{:S(2)}, u32[]{:S(2)}) async-start(bf16[32,96,128]{2,1,0:T(8,128)(2,1)} %pad_maximum_fusion), calls=%async_computation.3 | async-start | bytes 1572864 | tf_op jit(solution)/shard_map/all_to_all | solution.py:136
  26.4 1.2 fusion.13
  27.6 69.6 %all-gather.4.cloned.1.call-done = bf16[1280,1536]{1,0:T(8,128)(2,1)} async-done(((bf16[40,1536]{1,0:T(8,128)(2,1)}), bf16[1280,1536]{1,0:T(8,128)(2,1)}) %all-gather.4.cloned.1.call-update) | async-done | bytes 3932176 | tf_op jit(solution)/shard_map/all_gather | solution.py:142
  97.1 2.6 %fusion.14 = bf16[321,768]{1,0:T(8,128)(2,1)S(1)} fusion(bf16[1280,1536]{1,0:T(8,128)(2,1)} %all-gather.4.cloned.1.call-done, bf16[64,1280]{1,0:T(8,128)(2,1)} %fusion.39, bf16[257,1280]{1,0:T(8,128)(2,1)} %fusion.13), kind=kOutput, calls=%fused_computation.19 | convolution fusion | flops 633001728 | bytes 3298816 | tf_op jit(solution)/shard_map/dot_general | solution.py:147
  100.5 1.2 copy.76
  101.7 1.5 convolution_convert_fusion.3
  103.3 0.9 copy.75
  104.7 1.3 fusion.23
  106.2 2.4 %fusion.24 = f32[64,1280]{1,0:T(8,128)} fusion(bf16[64,384]{1,0:T(8,128)(2,1)S(1)} %reshape.208, bf16[1280,1536]{1,0:T(8,128)(2,1)} %all-gather.4.cloned.1.call-done), kind=kOutput, calls=%fused_computation.32 | convolution fusion | flops 62914560 | bytes 1359872 | tf_op jit(solution)/shard_map/dot_general | solution.py:161
  108.7 1.9 slice.34
  111.7 1.0 slice.33.q_ref
  112.7 14.2 %reduce-scatter.2.cloned.1.call-done = f32[16,1280]{1,0:T(8,128)} async-done(((f32[64,1280]{1,0:T(8,128)}), f32[16,1280]{1,0:T(8,128)}) %reduce-scatter.2.cloned.1.call-update) | async-done | bytes 81936 | tf_op jit(solution)/shard_map/reduce_scatter | solution.py:168
  126.9 1.0 fusion.54
  127.9 1.1 multiply_reduce_fusion
  129.0 1.0 multiply_convert_fusion
  132.1 10.2 %all-to-all-start = ((bf16[32,2,320]{2,1,0:T(2,128)(2,1)}), bf16[32,2,320]{2,1,0:T(2,128)(2,1)S(1)}, u32[]{:S(2)}, u32[]{:S(2)}) async-start(bf16[32,2,320]{2,1,0:T(2,128)(2,1)} %reshape.224), calls=%async_computation.1 | async-start | bytes 98304 | tf_op jit(solution)/shard_map/all_to_all | solution.py:181
  142.3 1.6 copy-done.1
  143.9 5.8 %self_attention.1 = bf16[32,32,128]{2,1,0:T(8,128)(2,1)} custom-call(s32[1]{0:T(128)} %bitcast.14.own_ref, bf16[32,32,128]{2,1,0:T(8,128)(2,1)S(1)} %slice.33.q_ref, bf16[4,32,64,128]{3,2,1,0:T(8,128)(2,1)S(1)} %bitcast.117), custom_call_target="tpu_custom_call" | custom-call | flops 1200000000 | bytes 3000000 | tf_op jit(solution)/shard_map/self_attention/pallas_call | solution.py:84
  150.4 9.2 %all-to-all-start.3 = ((bf16[32,32,128]{2,1,0:T(8,128)(2,1)}), bf16[32,32,128]{2,1,0:T(8,128)(2,1)S(1)}, u32[]{:S(2)}, u32[]{:S(2)}) async-start(bf16[32,32,128]{2,1,0:T(8,128)(2,1)} %self_attention.1), calls=%async_computation.4 | async-start | bytes 524288 | tf_op jit(solution)/shard_map/all_to_all | solution.py:215
  161.4 8.7 %all-to-all-done.3 = bf16[32,32,128]{2,1,0:T(8,128)(2,1)S(1)} async-done(((bf16[32,32,128]{2,1,0:T(8,128)(2,1)}), bf16[32,32,128]{2,1,0:T(8,128)(2,1)S(1)}, u32[]{:S(2)}, u32[]{:S(2)}) %all-to-all-start.3) | async-done | bytes 262176 | tf_op jit(solution)/shard_map/all_to_all | solution.py:215
  170.1 6.3 %all-to-all-start.1 = ((bf16[32,4,640]{2,1,0:T(4,128)(2,1)}), bf16[32,4,640]{2,1,0:T(4,128)(2,1)S(1)}, u32[]{:S(2)}, u32[]{:S(2)}) async-start(bf16[32,4,640]{2,1,0:T(4,128)(2,1)} %reshape.209), calls=%async_computation.2 | async-start | bytes 327680 | tf_op jit(solution)/shard_map/all_to_all | solution.py:185
  177.3 7.6 %all-to-all-done.1 = bf16[32,4,640]{2,1,0:T(4,128)(2,1)S(1)} async-done(((bf16[32,4,640]{2,1,0:T(4,128)(2,1)}), bf16[32,4,640]{2,1,0:T(4,128)(2,1)S(1)}, u32[]{:S(2)}, u32[]{:S(2)}) %all-to-all-start.1) | async-done | bytes 163872 | tf_op jit(solution)/shard_map/all_to_all | solution.py:185
  185.1 8.1 %all_gather.13 = bf16[256,1280]{1,0:T(8,128)(2,1)S(1)} all-gather(bf16[64,1280]{1,0:T(8,128)(2,1)S(1)} %bitcast.129), channel_id=1, replica_groups=mesh['y'=4,'z'=8,'xl'=2,'core'=2,'doc'=2] {'xl','core'}, dimensions={0}, use_global_device_ids=true | all-gather | bytes 819200 | tf_op jit(solution)/shard_map/all_gather | solution.py:188
  195.0 1.3 fusion.7
  196.3 1.6 fusion.64
  197.9 3.4 %convolution_convert_fusion.1 = bf16[256,1024]{1,0:T(8,128)(2,1)} fusion(bf16[256,1280]{1,0:T(8,128)(2,1)S(1)} %all_gather.13, bf16[1280,1024]{1,0:T(8,128)(2,1)} %param.27), kind=kOutput, calls=%fused_computation.18 | convolution fusion | flops 671350784 | bytes 3801088 | tf_op jit(solution)/shard_map/dot_general | solution.py:191
  201.3 1.2 copy.92
  202.6 2.0 fusion.21
  (81 shorter events, 12.9 us)
Async XLA Ops:
  8.0 185.3 %copy-start = (bf16[1280,1024]{1,0:T(8,128)(2,1)S(1)}, bf16[1280,1024]{1,0:T(8,128)(2,1)}, u32[]{:S(2)}) copy-start(bf16[1280,1024]{1,0:T(8,128)(2,1)} %param.26) | copy-start | bytes 7864324
  8.0 3.8 %copy-start.4 = (bf16[128,1024]{1,0:T(8,128)(2,1)S(1)}, bf16[128,1024]{1,0:T(8,128)(2,1)}, u32[]{:S(2)}) copy-start(bf16[128,1024]{1,0:T(8,128)(2,1)} %param.30) | copy-start | bytes 786436
  8.0 89.1 %all-gather.4.cloned.1.call-start = ((), (), s32[]{:S(2)}) async-start(), calls=%async_computation.5 | async-start | bytes 4055040 | tf_op jit(solution)/shard_map/all_gather | solution.py:142
  12.0 12.7 %copy-start.3 = (bf16[64,1280]{1,0:T(8,128)(2,1)S(1)}, bf16[64,1280]{1,0:T(8,128)(2,1)}, u32[]{:S(2)}) copy-start(bf16[64,1280]{1,0:T(8,128)(2,1)} %param.18) | copy-start | bytes 491524
  12.0 13.1 %copy-start.2 = (bf16[1,257,1280]{2,1,0:T(8,128)(2,1)S(1)}, bf16[1,257,1280]{2,1,0:T(8,128)(2,1)}, u32[]{:S(2)}) copy-start(bf16[1,257,1280]{2,1,0:T(8,128)(2,1)} %param.17) | copy-start | bytes 1973764
  12.9 12.7 %copy-start.8 = (f32[1280]{0:T(1024)S(1)}, f32[1280]{0:T(1024)}, u32[]{:S(2)}) copy-start(f32[1280]{0:T(1024)} %param.20) | copy-start | bytes 15364
  12.9 13.5 %copy-start.6 = (f32[1280]{0:T(1024)S(1)}, f32[1280]{0:T(1024)}, u32[]{:S(2)}) copy-start(f32[1280]{0:T(1024)} %param.19) | copy-start | bytes 15364
  12.9 95.7 %all-to-all-start.2 = ((bf16[32,96,128]{2,1,0:T(8,128)(2,1)}), bf16[32,96,128]{2,1,0:T(8,128)(2,1)}, u32[]{:S(2)}, u32[]{:S(2)}) async-start(bf16[32,96,128]{2,1,0:T(8,128)(2,1)} %pad_maximum_fusion), calls=%async_computation.3 | async-start | bytes 1572864 | tf_op jit(solution)/shard_map/all_to_all | solution.py:136
  24.6 102.3 %reduce-scatter.2.cloned.1.call-start = ((), (), s32[]{:S(2)}) async-start(), calls=%async_computation.6 | async-start | bytes 409600 | tf_op jit(solution)/shard_map/reduce_scatter | solution.py:168
  27.6 74.1 %copy-start.5 = (bf16[64,1280]{1,0:T(8,128)(2,1)S(1)}, bf16[64,1280]{1,0:T(8,128)(2,1)}, u32[]{:S(2)}) copy-start(bf16[64,1280]{1,0:T(8,128)(2,1)} %fusion.39) | copy-start | bytes 491524
  106.2 4.4 %copy-start.10 = (s32[32]{0:T(128)S(1)}, s32[32]{0:T(128)}, u32[]{:S(2)}) copy-start(s32[32]{0:T(128)} %param.33) | copy-start | bytes 388
  108.6 20.4 %copy-start.7 = (f32[1280]{0:T(1024)S(1)}, f32[1280]{0:T(1024)}, u32[]{:S(2)}) copy-start(f32[1280]{0:T(1024)} %param.21) | copy-start | bytes 15364
  108.6 33.7 %all-gather.6.cloned.1.call-start = ((), (), s32[]{:S(2)}) async-start(), calls=%async_computation.7 | async-start | bytes 2621440 | tf_op jit(solution)/shard_map/all_gather | solution.py:138
  132.1 18.2 %all-to-all-start = ((bf16[32,2,320]{2,1,0:T(2,128)(2,1)}), bf16[32,2,320]{2,1,0:T(2,128)(2,1)S(1)}, u32[]{:S(2)}, u32[]{:S(2)}) async-start(bf16[32,2,320]{2,1,0:T(2,128)(2,1)} %reshape.224), calls=%async_computation.1 | async-start | bytes 98304 | tf_op jit(solution)/shard_map/all_to_all | solution.py:181
  142.3 1.6 copy-start.1
  143.9 16.3 %copy-start.9 = (f32[1024]{0:T(1024)S(1)}, f32[1024]{0:T(1024)}, u32[]{:S(2)}) copy-start(f32[1024]{0:T(1024)} %param.32) | copy-start | bytes 12292
  150.4 19.7 %all-to-all-start.3 = ((bf16[32,32,128]{2,1,0:T(8,128)(2,1)}), bf16[32,32,128]{2,1,0:T(8,128)(2,1)S(1)}, u32[]{:S(2)}, u32[]{:S(2)}) async-start(bf16[32,32,128]{2,1,0:T(8,128)(2,1)} %self_attention.1), calls=%async_computation.4 | async-start | bytes 524288 | tf_op jit(solution)/shard_map/all_to_all | solution.py:215
  170.1 14.9 %all-to-all-start.1 = ((bf16[32,4,640]{2,1,0:T(4,128)(2,1)}), bf16[32,4,640]{2,1,0:T(4,128)(2,1)S(1)}, u32[]{:S(2)}, u32[]{:S(2)}) async-start(bf16[32,4,640]{2,1,0:T(4,128)(2,1)} %reshape.209), calls=%async_computation.2 | async-start | bytes 327680 | tf_op jit(solution)/shard_map/all_to_all | solution.py:185
  193.3 1.7 copy-start.11
  194.1 0.8 copy-start.12
Sparse Core Ops, SparseCore 0:
  12.0 85.0 all-gather.3
  108.7 18.1 reduce-scatter.1
Sparse Core Ops, SparseCore 1:
  110.9 30.3 all-gather.5

commit v2 on v1

v2 whole, which is shorter than its diff:
```python
import functools

import jax
import jax.numpy as jnp
from jax import lax
from jax.experimental import pallas as pl
from jax.experimental.pallas import tpu as pltpu
from jax.sharding import Mesh
from jax.sharding import PartitionSpec as P

HD = 128
RHD = 96
CITE = 3
BLK = ("y", "z")
IMG = ("xl", "core")
LOG2E = 1.4426950408889634
MIB = 1024 * 1024

epsilon = 1e-05

VMEM = pl.BlockSpec(memory_space=pltpu.VMEM)
SMEM = pl.BlockSpec(memory_space=pltpu.SMEM)


def layer_norm(values, gain):
    values = values.astype(jnp.float32)
    center = jnp.mean(values, -1, keepdims=True)
    spread = jnp.mean(jnp.square(values - center), -1, keepdims=True)
    return (values - center) * lax.rsqrt(spread + epsilon) * gain


def dot_t(left, right):
    return lax.dot_general(
        left, right, (((1,), (1,)), ((), ())), preferred_element_type=jnp.float32
    )


def call(kernel, out_shape, in_specs, name, flops, limit=40, scratch=()):
    return pl.pallas_call(
        kernel,
        out_shape=out_shape,
        in_specs=in_specs,
        out_specs=jax.tree.map(lambda _: VMEM, out_shape),
        scratch_shapes=list(scratch),
        compiler_params=pltpu.CompilerParams(vmem_limit_bytes=limit * MIB),
        cost_estimate=pl.CostEstimate(flops=flops, bytes_accessed=3000000, transcendentals=0),
        name=name,
    )


def pack_kernel(query_ref, key_ref, value_ref, out_ref, packed_ref):
    heads = query_ref.shape[1] // RHD
    copies = packed_ref.shape[0] // heads
    out_columns = out_ref[...].T
    for head in range(heads):
        span = slice(head * RHD, (head + 1) * RHD)
        row = jnp.concatenate(
            [query_ref[:, span], key_ref[:, span], value_ref[:, span], out_columns[:, span]], 1
        )
        for copy in range(copies):
            packed_ref[head * copies + copy] = row


def heads_kernel(core_ref, own_ref, other_ref, latent_ref, weight_ref, out_ref):
    core = core_ref[0]
    images, latent_rows, _ = out_ref.shape
    half = own_ref.shape[0] // images
    overlap = 2 * half - 257
    weight = weight_ref[...]

    def project(rows):
        return jnp.dot(rows, weight, preferred_element_type=jnp.float32).astype(jnp.bfloat16)

    latent = project(latent_ref[...])
    query = latent[:, :RHD]
    latent_key, latent_value = latent[:, RHD : 2 * RHD], latent[:, 2 * RHD : 3 * RHD]
    scale = RHD ** (-0.5)
    latent_scores = dot_t(query, latent_key) * scale
    latent_peak = jnp.max(latent_scores, -1, keepdims=True)
    place = lax.broadcasted_iota(jnp.int32, (latent_rows, half), 1)
    own_seen = place >= overlap * core
    other_seen = place >= overlap * (1 - core)
    own = jnp.dot(own_ref[...], weight, preferred_element_type=jnp.float32)
    other = jnp.dot(other_ref[...], weight, preferred_element_type=jnp.float32)
    for image in range(images):
        peak, parts = latent_peak, [(latent_scores, latent_value)]
        for rows, seen in ((own, own_seen), (other, other_seen)):
            rows = rows[image * half : (image + 1) * half].astype(jnp.bfloat16)
            scores = dot_t(query, rows[:, RHD : 2 * RHD]) * scale
            scores = jnp.where(seen, scores, -1e30)
            peak = jnp.maximum(peak, jnp.max(scores, -1, keepdims=True))
            parts.append((scores, rows[:, 2 * RHD : 3 * RHD]))
        total, context = 0.0, 0.0
        for scores, values in parts:
            weights = jnp.exp(scores - peak)
            total = total + jnp.sum(weights, -1, keepdims=True)
            context = context + jnp.dot(
                weights.astype(jnp.bfloat16), values, preferred_element_type=jnp.float32
            )
        out_ref[image] = (context / total).astype(jnp.bfloat16)


def project_kernel(*refs):
    parts, partial_ref = refs[:-1], refs[-1]
    count = len(parts) // 2
    total = 0.0
    for context_ref, weight_ref in zip(parts[:count], parts[count:]):
        total = total + dot_t(context_ref[...], weight_ref[...])
    partial_ref[...] = total


def cross_kernel(window_ref, key_ref, value_ref, query_ref, gate_ref, slot_ref, out_ref):
    stacks, flat, lanes = window_ref.shape
    quarter = 16
    tokens, columns = query_ref.shape
    count = stacks * quarter
    window = window_ref[...].reshape(stacks, flat // quarter, quarter, lanes)
    window = jnp.concatenate(
        [window[:, tile].reshape(count, lanes) for tile in range(flat // quarter)], 1
    )
    place = lax.broadcasted_iota(jnp.int32, (tokens, count), 1) // quarter % (CITE + 1)
    seen = place == slot_ref[...]
    scale = HD ** (-0.5)
    wide = 4 * HD
    for first in range(0, columns, wide):
        span = slice(first, first + wide)
        keys = jnp.dot(window, key_ref[:, span], preferred_element_type=jnp.float32)
        values = jnp.dot(window, value_ref[:, span], preferred_element_type=jnp.float32)
        keys, values = keys.astype(jnp.bfloat16), values.astype(jnp.bfloat16)
        for head in range(0, wide, HD):
            here = slice(head, head + HD)
            there = slice(first + head, first + head + HD)
            scores = dot_t(query_ref[:, there], keys[:, here]) * scale
            scores = jnp.where(seen, scores, -1e30)
            weights = jnp.exp(scores - jnp.max(scores, -1, keepdims=True))
            weights = jnp.where(seen, weights, 0.0)
            total = jnp.sum(weights, -1, keepdims=True)
            context = jnp.dot(
                weights.astype(jnp.bfloat16), values[:, here], preferred_element_type=jnp.float32
            )
            context = context / total * jnp.tanh(gate_ref[:, there])
            context = jnp.where(slot_ref[...] >= 0, context, 0.0)
            out_ref[:, there] = context.astype(jnp.bfloat16)


def self_kernel(own_ref, q_ref, kv_ref, o_ref, s_ref):
    own = own_ref[0]
    pieces, blocks, rows2, width = kv_ref.shape
    rows = rows2 // 2
    group = 128 // rows
    factor = width**-0.5 * LOG2E
    index_q = lax.broadcasted_iota(jnp.int32, (128, 128), 0)
    index_k = lax.broadcasted_iota(jnp.int32, (128, 128), 1)
    place_q = index_q // rows * 128 + own * rows + index_q % rows
    place_k = index_k // rows * 128 + index_k % rows
    for turn in range(blocks // group):
        first = turn * group
        query = q_ref[first : first + group].reshape(128, width)
        span = (first + group) * rows
        peak = None
        for piece in range(pieces):
            keys = kv_ref[piece, 0 : first + group, 0:rows, :].reshape(span, width)
            scores = lax.dot_general(
                query, keys, (((1,), (1,)), ((), ())), preferred_element_type=jnp.float32
            )
            scores = scores * factor
            tail = jnp.where(place_k + piece * rows <= place_q, scores[:, span - 128 :], -1e30)
            s_ref[piece, :, span - 128 : span] = tail
            top = jnp.max(tail, -1, keepdims=True)
            if span > 128:
                s_ref[piece, :, 0 : span - 128] = scores[:, : span - 128]
                top = jnp.maximum(top, jnp.max(scores[:, : span - 128], -1, keepdims=True))
            peak = top if peak is None else jnp.maximum(peak, top)
        total = jnp.zeros((128, 1), jnp.float32)
        context = jnp.zeros((128, width), jnp.float32)
        for piece in range(pieces):
            weights = jnp.exp2(s_ref[piece, :, 0:span] - peak)
            total = total + jnp.sum(weights, -1, keepdims=True)
            values = kv_ref[piece, 0 : first + group, rows : 2 * rows, :].reshape(span, width)
            context = context + jnp.dot(
                weights.astype(jnp.bfloat16), values, preferred_element_type=jnp.float32
            )
        o_ref[first : first + group] = (
            (context / total).astype(jnp.bfloat16).reshape(group, rows, width)
        )


def by_head(rows, y_size, z_size):
    tokens = rows.shape[0]
    split = rows.reshape(y_size, tokens // y_size, z_size, HD)
    return jnp.transpose(split, (0, 2, 1, 3)).reshape(y_size * z_size, tokens // y_size, HD)


def shards(
    features,
    latents,
    context_gain,
    latent_gain,
    final_gain,
    rs_query,
    rs_key,
    rs_value,
    rs_out,
    x_key,
    x_value,
    text_query,
    text_key,
    text_value,
    cross_query,
    cross_gate,
    image_pos,
):
    y_size, z_size = lax.axis_size("y"), lax.axis_size("z")
    blocks = y_size * z_size
    heads_of = lax.axis_size(IMG)
    shard_index = lax.axis_index(BLK)
    own_y = lax.axis_index("y").astype(jnp.int32)
    own_core = lax.axis_index("core").astype(jnp.int32)
    own_img = lax.axis_index(IMG)
    tokens = text_query.shape[0]
    piece = tokens // y_size
    latent_rows, full_width = latents.shape
    bf16, f32 = jnp.bfloat16, jnp.float32

    depth, columns = rs_query.shape
    weights = call(
        pack_kernel,
        jax.ShapeDtypeStruct((blocks, depth, 4 * RHD), bf16),
        [VMEM] * 4,
        "pack_weights",
        1000000,
    )(rs_query, rs_key, rs_value, rs_out)
    weights = lax.all_to_all(weights, BLK, 0, 0, tiled=True)
    weights = weights.reshape(blocks * depth, 4 * RHD)

    patches = features.shape[1]
    half = -(-patches // 16) * 8
    own_rows = lax.dynamic_slice_in_dim(features[0], own_core * (patches - half), half, 0)
    own_rows = layer_norm(own_rows, context_gain).astype(bf16)
    own_rows = lax.all_gather(own_rows, "y", axis=0, tiled=True)
    other_rows = lax.ppermute(own_rows, "core", [(0, 1), (1, 0)])
    latent_norm = layer_norm(latents, latent_gain).astype(bf16)

    packed = jnp.concatenate(
        [by_head(part, y_size, z_size) for part in (text_query, text_key, text_value)], 1
    )
    packed, weights = lax.optimization_barrier((packed, weights))
    packed = lax.all_to_all(packed, BLK, 0, 0, tiled=True)
    head_query = packed[:, 0:piece]
    pairs = lax.all_gather(packed[:, piece:], "y", axis=0, tiled=False)

    contexts = call(
        heads_kernel,
        jax.ShapeDtypeStruct((y_size, latent_rows, RHD), bf16),
        [SMEM] + [VMEM] * 4,
        "resampler_heads",
        1000000000,
    )(own_core[None], own_rows, other_rows, latent_norm, weights)

    out_weight = weights[:, 3 * RHD :]
    context_parts, weight_parts = [], []
    for step in range(y_size):
        part = lax.dynamic_index_in_dim(contexts, (own_y + step) % y_size, 0, keepdims=False)
        turn = [(source, (source + step) % y_size) for source in range(y_size)]
        context_parts.append(lax.ppermute(part, "y", turn) if step else part)
        weight_parts.append(lax.ppermute(out_weight, "y", turn) if step else out_weight)
    partial_out = call(
        project_kernel,
        jax.ShapeDtypeStruct((latent_rows, full_width), f32),
        [VMEM] * (2 * y_size),
        "project_out",
        70000000,
    )(*context_parts, *weight_parts)

    quarter = latent_rows // heads_of
    summed = lax.dynamic_slice_in_dim(partial_out, own_img * quarter, quarter, 0)
    for step in range(1, heads_of):
        part = lax.dynamic_slice_in_dim(partial_out, (own_img ^ step) * quarter, quarter, 0)
        pairs_of = [(source, source ^ step) for source in range(heads_of)]
        summed = summed + lax.ppermute(part, IMG, pairs_of)
    own_latents = lax.dynamic_slice_in_dim(latents, own_img * quarter, quarter, 0)
    resampled = layer_norm(own_latents.astype(f32) + summed, final_gain).astype(bf16)

    starts = jnp.arange(blocks, dtype=jnp.int32) * tokens
    image_rank = jnp.sum((image_pos[None, :] < image_pos[:, None]).astype(jnp.int32), axis=1)
    first_all = jnp.sum((image_pos[None, :] < starts[:, None]).astype(jnp.int32), axis=1)
    wanted = first_all[:, None] - 1 + jnp.arange(CITE + 1, dtype=jnp.int32)
    choice = (image_rank[None, None, :] == wanted[:, :, None]).astype(bf16)

    slots = CITE + 1
    tiles = full_width // 128
    chunk = quarter * tiles // blocks
    spread = jnp.transpose(resampled.reshape(quarter, tiles, 128), (1, 0, 2))
    spread = lax.all_to_all(spread.reshape(blocks, chunk, 128), BLK, 0, 0, tiled=True)
    chosen = jnp.einsum("dsi,icl->dscl", choice, spread, preferred_element_type=f32)
    chosen = chosen.astype(bf16).reshape(blocks, slots * chunk, 128)
    chosen = lax.all_to_all(chosen, BLK, 0, 0, tiled=True)
    chosen, pairs = lax.optimization_barrier((chosen, pairs))
    chosen = jnp.transpose(chosen.reshape(blocks, slots, chunk, 128), (1, 0, 2, 3))
    chosen = chosen.reshape(slots, blocks * chunk, 128)
    window = lax.all_gather(chosen, IMG, axis=0, tiled=True)

    start_row = shard_index * tokens
    positions = start_row + jnp.arange(tokens, dtype=jnp.int32)
    token_rank = jnp.sum((image_pos[None, :] <= positions[:, None]).astype(jnp.int32), axis=1) - 1
    first_image = jnp.sum((image_pos < start_row).astype(jnp.int32))
    local_slot = jnp.where(token_rank >= 0, token_rank - first_image + 1, -1)
    cross_out = call(
        cross_kernel,
        jax.ShapeDtypeStruct(cross_query.shape, bf16),
        [VMEM] * 6,
        "cross_attention",
        1500000000,
    )(window, x_key, x_value, cross_query, cross_gate[None], local_slot[:, None])

    self_rows = call(
        self_kernel,
        jax.ShapeDtypeStruct((blocks, piece, HD), bf16),
        [SMEM, VMEM, VMEM],
        "self_attention",
        1200000000,
        scratch=[pltpu.VMEM((y_size, 128, blocks * piece), f32)],
    )(own_y[None], head_query, pairs)
    self_rows = lax.all_to_all(self_rows, BLK, 0, 0, tiled=True)
    self_out = jnp.transpose(self_rows.reshape(y_size, z_size, piece, HD), (0, 2, 1, 3))
    return (cross_out, self_out.reshape(tokens, -1))


def solution(mesh):
    blocks, heads_of, documents = mesh.devices.shape
    z_size = 8
    devices = mesh.devices.reshape(blocks // z_size, z_size, 2, heads_of // 2, documents)
    inner = Mesh(devices, ("y", "z", "xl", "core", "doc"))
    rows = ("doc", "y", "z")
    in_specs = (
        P(rows, None, None),
        P(),
        P(),
        P(),
        P(),
        P(BLK, IMG),
        P(BLK, IMG),
        P(BLK, IMG),
        P(IMG, BLK),
        P(None, IMG),
        P(None, IMG),
        P(rows, IMG),
        P(rows, IMG),
        P(rows, IMG),
        P(rows, IMG),
        P(IMG),
        P("doc"),
    )
    out_specs = (P(rows, IMG), P(rows, IMG))
    return jax.shard_map(
        shards, mesh=inner, in_specs=in_specs, out_specs=out_specs, check_vma=False
    )
```

time: 217 us -> 181 us (0.83)
  waiting for transfers between devices: 101 us -> 73 us
  matrix products: 17.5 us -> 0.24 us
  starting transfers between devices: 37.4 us -> 49.2 us
  Pallas kernels: 5.8 us -> 16 us
  other arithmetic: 11.4 us -> 5.8 us
  local copies, waits for them, and re-layouts: 15.8 us -> 11.6 us
    all_gather x1, waiting for transfers between devices: 69.6 us -> 0.68 us  [shards(): own_rows = lax.all_gather(own_rows, 'y', axis=0, tiled=True)]
    all_to_all x2 -> x3, waiting for transfers between devices: 8.28 us -> 37.6 us  [the longest x1 22.2 us: shards(): weights = lax.all_to_all(weights, BLK, 0, 0, tiled=True)]
    all_to_all x1, waiting for transfers between devices: 0.01 us -> 19.4 us  [shards(): packed = lax.all_to_all(packed, BLK, 0, 0, tiled=True)]
    dot_general x10 -> x1, matrix products: 15.9 us -> 0.24 us  [shards(): jnp.einsum('dsi,icl->dscl', choice, spread, preferred_element_type=f32)]
    ppermute x0 -> x10, waiting for transfers between devices: none -> 15.4 us  [the longest x3 8.19 us: shards(): lax.ppermute(out_weight, 'y', turn)]
    reduce_scatter x1 -> x0, waiting for transfers between devices: 14.2 us -> none  [shards(): summed = lax.psum_scatter(partial_out, IMG, scatter_dimension=0, tiled=True)]
    pallas_call x1 -> x5, Pallas kernels: 5.8 us -> 16 us  [the longest x1 5.78 us: shards(): call(self_kernel, jax.ShapeDtypeStruct((blocks, piece, HD), bf16), [SMEM,...]
    ppermute x0 -> x10, starting transfers between devices: none -> 10.1 us  [the longest x3 4.62 us: shards(): context_parts.append(lax.ppermute(part, 'y', turn) if step else part)]
  transfers between devices with their start and end apart: 7 -> 17, of which waited for: 5 -> 10; matrix products, arithmetic and copies ran while one was open for 14% -> 6% of each run, Pallas kernels for 3% -> 5%
where the time goes in v2:
time: 181 us; the launch traced here: 177 us
  waiting for transfers between devices  73 us (40%)
  starting transfers between devices  49.2 us (27%)
  Pallas kernels  16 us (9%)
  between operations  14.4 us (8%)
  local copies, waits for them, and re-layouts  11.6 us (6%)
  blocking collectives  6.95 us (4%)
  other arithmetic  5.8 us (3%)
    all_to_all x1, waiting for transfers between devices, shards(): weights = lax.all_to_all(weights, BLK, 0, 0, tiled=True)  22.2 us
    all_to_all x1, waiting for transfers between devices, shards(): packed = lax.all_to_all(packed, BLK, 0, 0, tiled=True)  19.4 us
    all_to_all x1, starting transfers between devices, shards(): weights = lax.all_to_all(weights, BLK, 0, 0, tiled=True)  11.7 us
    all_to_all x1, waiting for transfers between devices, shards(): lax.all_to_all(spread.reshape(blocks, chunk, 128), BLK, 0, 0, tiled=True)  8.2 us
    ppermute x3, waiting for transfers between devices, shards(): lax.ppermute(out_weight, 'y', turn)  8.19 us
    all_to_all x1, starting transfers between devices, shards(): lax.all_to_all(spread.reshape(blocks, chunk, 128), BLK, 0, 0, tiled=True)  8.07 us
    unnamed x43, local copies, waits for them, and re-layouts  7.54 us
    all_to_all x1, starting transfers between devices, shards(): packed = lax.all_to_all(packed, BLK, 0, 0, tiled=True)  7.43 us
  transfers between devices with their start and end apart: 17, of which 10 were waited for; matrix products, arithmetic and copies ran while one was open for 6% of the time, Pallas kernels for 5%

profile of v2, /device:TPU:26, one launch (start us, length us, event | category | flops | bytes accessed | tf_op | source)
XLA Modules:
  0.0 177.3 jit_solution(15163430634649465535)
XLA Ops:
  7.2 0.9 copy.50.out_ref
  10.3 1.1 pack_weights.1
  11.5 11.7 %all-to-all-start = ((bf16[32,40,384]{2,1,0:T(8,128)(2,1)}), bf16[32,40,384]{2,1,0:T(8,128)(2,1)S(1)}, u32[]{:S(2)}, u32[]{:S(2)}) async-start(bf16[32,40,384]{2,1,0:T(8,128)(2,1)} %pack_weights.1), calls=%async_computation | async-start | bytes 1966080 | tf_op jit(solution)/shard_map/all_to_all | solution.py:233
  23.7 1.0 fusion.5
  25.1 1.0 pad_maximum_fusion
  26.1 22.2 %all-to-all-done = bf16[32,40,384]{2,1,0:T(8,128)(2,1)S(1)} async-done(((bf16[32,40,384]{2,1,0:T(8,128)(2,1)}), bf16[32,40,384]{2,1,0:T(8,128)(2,1)S(1)}, u32[]{:S(2)}, u32[]{:S(2)}) %all-to-all-start) | async-done | bytes 983072 | tf_op jit(solution)/shard_map/all_to_all | solution.py:233
  48.2 7.4 %all-to-all-start.3 = ((bf16[32,96,128]{2,1,0:T(8,128)(2,1)}), bf16[32,96,128]{2,1,0:T(8,128)(2,1)S(1)}, u32[]{:S(2)}, u32[]{:S(2)}) async-start(bf16[32,96,128]{2,1,0:T(8,128)(2,1)} %pad_maximum_fusion), calls=%async_computation.3 | async-start | bytes 1572864 | tf_op jit(solution)/shard_map/all_to_all | solution.py:248
  56.8 19.4 %all-to-all-done.3 = bf16[32,96,128]{2,1,0:T(8,128)(2,1)S(1)} async-done(((bf16[32,96,128]{2,1,0:T(8,128)(2,1)}), bf16[32,96,128]{2,1,0:T(8,128)(2,1)S(1)}, u32[]{:S(2)}, u32[]{:S(2)}) %all-to-all-start.3) | async-done | bytes 786464 | tf_op jit(solution)/shard_map/all_to_all | solution.py:248
  76.1 0.9 slice.12
  77.6 2.5 %collective-permute-start.4 = (bf16[1280,96]{1,0:T(8,128)(2,1)S(1)}, bf16[1280,96]{1,0:T(8,128)(2,1)S(1)}, u32[]{:S(2)}, u32[]{:S(2)}) collective-permute-start(bf16[1280,96]{1,0:T(8,128)(2,1)S(1)} %slice.9.refs_4_), channel_id=1, source_target_pairs={{0,64},{64,128},{128,192},{192,0},{1,65},{65,129},{129,193},{193,1... | collective-permute-start | bytes 737288 | tf_op jit(solution)/shard_map/ppermute | solution.py:266
  80.2 0.8 collective-permute-start.6
  81.1 4.8 %resampler_heads.1 = bf16[4,64,96]{2,1,0:T(8,128)(2,1)S(1)} custom-call(s32[1]{0:T(128)} %bitcast.2.core_ref, bf16[544,1280]{1,0:T(8,128)(2,1)S(1)} %copy-done.2, bf16[544,1280]{1,0:T(8,128)(2,1)} %collective-permute-done.other_ref, bf16[64,1280]{1,0:T(8,128)(2,1)S(1)} %fusion.10.latent_ref, bf16[1280,384]{1,0:T(8,128)(2,1)S(1)} %bitcast.70), custom_call_target="tpu_custom_call" | custom-call | flops 1000000000 | bytes 3000000 | tf_op jit(solution)/shard_map/resampler_heads/pallas_call | solution.py:252
  85.9 2.5 %collective-permute-start.1 = (bf16[64,96]{1,0:T(8,128)(2,1)S(1)}, bf16[64,96]{1,0:T(8,128)(2,1)S(1)}, u32[]{:S(2)}, u32[]{:S(2)}) collective-permute-start(bf16[64,96]{1,0:T(8,128)(2,1)S(1)} %get-tuple-element.19), channel_id=1, source_target_pairs={{0,64},{64,128},{128,192},{192,0},{1,65},{65,129},{129,193},{193,1... | collective-permute-start | bytes 36872 | tf_op jit(solution)/shard_map/ppermute | solution.py:265
  88.4 2.1 %collective-permute-start.2 = (bf16[64,96]{1,0:T(8,128)(2,1)S(1)}, bf16[64,96]{1,0:T(8,128)(2,1)S(1)}, u32[]{:S(2)}, u32[]{:S(2)}) collective-permute-start(bf16[64,96]{1,0:T(8,128)(2,1)S(1)} %get-tuple-element.18), channel_id=1, source_target_pairs={{0,128},{64,192},{128,0},{192,64},{1,129},{65,193},{129,1},{193,65... | collective-permute-start | bytes 36872 | tf_op jit(solution)/shard_map/ppermute | solution.py:265
  90.5 1.3 collective-permute-done.4.refs_5_
  92.0 6.9 %collective-permute-done.6.refs_7_ = bf16[1280,96]{1,0:T(8,128)(2,1)} collective-permute-done((bf16[1280,96]{1,0:T(8,128)(2,1)S(1)}, bf16[1280,96]{1,0:T(8,128)(2,1)}, u32[]{:S(2)}, u32[]{:S(2)}) %collective-permute-start.6) | collective-permute-done | bytes 245792 | tf_op jit(solution)/shard_map/ppermute | solution.py:266
  98.9 2.9 %collective-permute-done.2.refs_2_ = bf16[64,96]{1,0:T(8,128)(2,1)S(1)} collective-permute-done((bf16[64,96]{1,0:T(8,128)(2,1)S(1)}, bf16[64,96]{1,0:T(8,128)(2,1)S(1)}, u32[]{:S(2)}, u32[]{:S(2)}) %collective-permute-start.2) | collective-permute-done | bytes 12320 | tf_op jit(solution)/shard_map/ppermute | solution.py:265
  101.8 1.5 project_out.1
  104.1 1.3 collective-permute-start.9
  105.4 3.5 %collective-permute-done.8 = f32[16,1280]{1,0:T(8,128)S(1)} collective-permute-done((f32[16,1280]{1,0:T(8,128)S(1)}, f32[16,1280]{1,0:T(8,128)S(1)}, u32[]{:S(2)}, u32[]{:S(2)}) %collective-permute-start.8) | collective-permute-done | bytes 81952 | tf_op jit(solution)/shard_map/ppermute | solution.py:280
  109.6 0.9 fusion.19
  111.6 8.1 %all-to-all-start.1 = ((bf16[32,5,128]{2,1,0:T(8,128)(2,1)}), bf16[32,5,128]{2,1,0:T(8,128)(2,1)S(1)}, u32[]{:S(2)}, u32[]{:S(2)}) async-start(bf16[32,5,128]{2,1,0:T(8,128)(2,1)} %reshape.159), calls=%async_computation.1 | async-start | bytes 131072 | tf_op jit(solution)/shard_map/all_to_all | solution.py:294
  119.7 8.2 %all-to-all-done.1 = bf16[32,5,128]{2,1,0:T(8,128)(2,1)S(1)} async-done(((bf16[32,5,128]{2,1,0:T(8,128)(2,1)}), bf16[32,5,128]{2,1,0:T(8,128)(2,1)S(1)}, u32[]{:S(2)}, u32[]{:S(2)}) %all-to-all-start.1) | async-done | bytes 40992 | tf_op jit(solution)/shard_map/all_to_all | solution.py:294
  128.9 5.7 %all-to-all-start.2 = ((bf16[32,20,128]{2,1,0:T(8,128)(2,1)}), bf16[32,20,128]{2,1,0:T(8,128)(2,1)S(1)}, u32[]{:S(2)}, u32[]{:S(2)}) async-start(bf16[32,20,128]{2,1,0:T(8,128)(2,1)} %copy.53), calls=%async_computation.2 | async-start | bytes 393216 | tf_op jit(solution)/shard_map/all_to_all | solution.py:297
  135.4 1.0 slice.13.q_ref
  136.4 7.2 %all-to-all-done.2 = bf16[32,20,128]{2,1,0:T(8,128)(2,1)S(1)} async-done(((bf16[32,20,128]{2,1,0:T(8,128)(2,1)}), bf16[32,20,128]{2,1,0:T(8,128)(2,1)S(1)}, u32[]{:S(2)}, u32[]{:S(2)}) %all-to-all-start.2) | async-done | bytes 163872 | tf_op jit(solution)/shard_map/all_to_all | solution.py:297
  143.6 1.6 copy-done.8
  145.2 5.8 %self_attention.1 = bf16[32,32,128]{2,1,0:T(8,128)(2,1)} custom-call(s32[1]{0:T(128)} %bitcast.24.own_ref, bf16[32,32,128]{2,1,0:T(8,128)(2,1)S(1)} %slice.13.q_ref, bf16[4,32,64,128]{3,2,1,0:T(8,128)(2,1)S(1)} %bitcast.72), custom_call_target="tpu_custom_call" | custom-call | flops 1200000000 | bytes 3000000 | tf_op jit(solution)/shard_map/self_attention/pallas_call | solution.py:316
  151.0 6.2 %all-to-all-start.4 = ((bf16[32,32,128]{2,1,0:T(8,128)(2,1)}), bf16[32,32,128]{2,1,0:T(8,128)(2,1)S(1)}, u32[]{:S(2)}, u32[]{:S(2)}) async-start(bf16[32,32,128]{2,1,0:T(8,128)(2,1)} %self_attention.1), calls=%async_computation.4 | async-start | bytes 524288 | tf_op jit(solution)/shard_map/all_to_all | solution.py:324
  158.1 6.9 %all_gather.15.window_ref = bf16[16,160,128]{2,1,0:T(8,128)(2,1)S(1)} all-gather(bf16[4,160,128]{2,1,0:T(8,128)(2,1)S(1)} %copy.56), channel_id=1, replica_groups=mesh['y'=4,'z'=8,'xl'=2,'core'=2,'doc'=2] {'xl','core'}, dimensions={0}, use_global_device_ids=true | all-gather | bytes 819200 | tf_op jit(solution)/shard_map/all_gather | solution.py:301
  165.1 1.7 copy-done.1
  166.8 2.8 %cross_attention.1 = bf16[128,1024]{1,0:T(8,128)(2,1)} custom-call(bf16[16,160,128]{2,1,0:T(8,128)(2,1)S(1)} %all_gather.15.window_ref, bf16[1280,1024]{1,0:T(8,128)(2,1)S(1)} %copy-done, bf16[1280,1024]{1,0:T(8,128)(2,1)S(1)} %copy-done.1, bf16[128,1024]{1,0:T(8,128)(2,1)S(1)} %copy-done.3, f32[1,1024]{1,0:T(1,128)S(1)} %bitcast.71, s32[128,1]{1,0:T(8,128)S(1)} %copy.57.slot_ref), custom_call_target="tpu_custom_call" | custom-call | flops 1500000000 | bytes 3000000 | tf_op jit(solution)/shard_map/cross_attention/pallas_call | solution.py:308
  (95 shorter events, 11.1 us)
Async XLA Ops:
  10.3 12.9 %copy-start.11 = (bf16[1,257,1280]{2,1,0:T(8,128)(2,1)S(1)}, bf16[1,257,1280]{2,1,0:T(8,128)(2,1)}, u32[]{:S(2)}) copy-start(bf16[1,257,1280]{2,1,0:T(8,128)(2,1)} %param.17) | copy-start | bytes 1973764
  11.5 12.2 %copy-start.15 = (f32[1280]{0:T(1024)S(1)}, f32[1280]{0:T(1024)}, u32[]{:S(2)}) copy-start(f32[1280]{0:T(1024)} %param.19) | copy-start | bytes 15364
  11.5 13.3 %copy-start.12 = (bf16[128,1024]{1,0:T(8,128)(2,1)S(1)}, bf16[128,1024]{1,0:T(8,128)(2,1)}, u32[]{:S(2)}) copy-start(bf16[128,1024]{1,0:T(8,128)(2,1)} %param.28) | copy-start | bytes 786436
  11.5 36.8 %all-to-all-start = ((bf16[32,40,384]{2,1,0:T(8,128)(2,1)}), bf16[32,40,384]{2,1,0:T(8,128)(2,1)S(1)}, u32[]{:S(2)}, u32[]{:S(2)}) async-start(bf16[32,40,384]{2,1,0:T(8,128)(2,1)} %pack_weights.1), calls=%async_computation | async-start | bytes 1966080 | tf_op jit(solution)/shard_map/all_to_all | solution.py:233
  23.1 1.7 copy-start.13
  23.1 33.3 %all-gather.4.cloned.1.call-start = ((), (), s32[]{:S(2)}) async-start(), calls=%async_computation.5 | async-start | bytes 1740800 | tf_op jit(solution)/shard_map/all_gather | solution.py:240
  23.7 1.3 copy-start.14
  25.1 31.3 %copy-start.10 = (bf16[64,1280]{1,0:T(8,128)(2,1)S(1)}, bf16[64,1280]{1,0:T(8,128)(2,1)}, u32[]{:S(2)}) copy-start(bf16[64,1280]{1,0:T(8,128)(2,1)} %param.18) | copy-start | bytes 491524
  48.2 29.0 %copy-start.17 = (f32[1280]{0:T(1024)S(1)}, f32[1280]{0:T(1024)}, u32[]{:S(2)}) copy-start(f32[1280]{0:T(1024)} %param.20) | copy-start | bytes 15364
  48.2 27.9 %all-to-all-start.3 = ((bf16[32,96,128]{2,1,0:T(8,128)(2,1)}), bf16[32,96,128]{2,1,0:T(8,128)(2,1)S(1)}, u32[]{:S(2)}, u32[]{:S(2)}) async-start(bf16[32,96,128]{2,1,0:T(8,128)(2,1)} %pad_maximum_fusion), calls=%async_computation.3 | async-start | bytes 1572864 | tf_op jit(solution)/shard_map/all_to_all | solution.py:248
  55.7 87.9 %all-gather.6.cloned.1.call-start = ((), (), s32[]{:S(2)}) async-start(), calls=%async_computation.6 | async-start | bytes 2621440 | tf_op jit(solution)/shard_map/all_gather | solution.py:250
  56.4 24.7 %copy-start.2 = (bf16[544,1280]{1,0:T(8,128)(2,1)S(1)}, bf16[544,1280]{1,0:T(8,128)(2,1)}, u32[]{:S(2)}) copy-start(bf16[544,1280]{1,0:T(8,128)(2,1)} %all-gather.4.cloned.1.call-done.own_ref) | copy-start | bytes 4177924
  56.4 24.7 %collective-permute-start = (bf16[544,1280]{1,0:T(8,128)(2,1)}, bf16[544,1280]{1,0:T(8,128)(2,1)}, u32[]{:S(2)}, u32[]{:S(2)}) collective-permute-start(bf16[544,1280]{1,0:T(8,128)(2,1)} %all-gather.4.cloned.1.call-done.own_ref), channel_id=1, source_target_pairs={{0,2},{2,0},{1,3},{3,1},{4,6},{6,4},{5,7},{7,5},{8,10},{10,8},{9,1... | collective-permute-start | bytes 4177928 | tf_op jit(solution)/shard_map/ppermute | solution.py:241
  77.6 14.2 %collective-permute-start.4 = (bf16[1280,96]{1,0:T(8,128)(2,1)S(1)}, bf16[1280,96]{1,0:T(8,128)(2,1)S(1)}, u32[]{:S(2)}, u32[]{:S(2)}) collective-permute-start(bf16[1280,96]{1,0:T(8,128)(2,1)S(1)} %slice.9.refs_4_), channel_id=1, source_target_pairs={{0,64},{64,128},{128,192},{192,0},{1,65},{65,129},{129,193},{193,1... | collective-permute-start | bytes 737288 | tf_op jit(solution)/shard_map/ppermute | solution.py:266
  80.1 11.9 %collective-permute-start.5 = (bf16[1280,96]{1,0:T(8,128)(2,1)S(1)}, bf16[1280,96]{1,0:T(8,128)(2,1)S(1)}, u32[]{:S(2)}, u32[]{:S(2)}) collective-permute-start(bf16[1280,96]{1,0:T(8,128)(2,1)S(1)} %slice.9.refs_4_), channel_id=1, source_target_pairs={{0,128},{64,192},{128,0},{192,64},{1,129},{65,193},{129,1},{193,65... | collective-permute-start | bytes 737288 | tf_op jit(solution)/shard_map/ppermute | solution.py:266
  80.2 18.7 %collective-permute-start.6 = (bf16[1280,96]{1,0:T(8,128)(2,1)S(1)}, bf16[1280,96]{1,0:T(8,128)(2,1)}, u32[]{:S(2)}, u32[]{:S(2)}) collective-permute-start(bf16[1280,96]{1,0:T(8,128)(2,1)S(1)} %slice.9.refs_4_), channel_id=1, source_target_pairs={{0,192},{64,0},{128,64},{192,128},{1,193},{65,1},{129,65},{193,129... | collective-permute-start | bytes 737288 | tf_op jit(solution)/shard_map/ppermute | solution.py:266
  81.1 10.7 %copy-start.18 = (s32[32]{0:T(128)S(1)}, s32[32]{0:T(128)}, u32[]{:S(2)}) copy-start(s32[32]{0:T(128)} %param.33) | copy-start | bytes 388
  85.8 24.9 %copy-start.16 = (f32[1280]{0:T(1024)S(1)}, f32[1280]{0:T(1024)}, u32[]{:S(2)}) copy-start(f32[1280]{0:T(1024)} %param.21) | copy-start | bytes 15364
  85.9 13.0 %collective-permute-start.1 = (bf16[64,96]{1,0:T(8,128)(2,1)S(1)}, bf16[64,96]{1,0:T(8,128)(2,1)S(1)}, u32[]{:S(2)}, u32[]{:S(2)}) collective-permute-start(bf16[64,96]{1,0:T(8,128)(2,1)S(1)} %get-tuple-element.19), channel_id=1, source_target_pairs={{0,64},{64,128},{128,192},{192,0},{1,65},{65,129},{129,193},{193,1... | collective-permute-start | bytes 36872 | tf_op jit(solution)/shard_map/ppermute | solution.py:265
  88.4 13.5 %collective-permute-start.2 = (bf16[64,96]{1,0:T(8,128)(2,1)S(1)}, bf16[64,96]{1,0:T(8,128)(2,1)S(1)}, u32[]{:S(2)}, u32[]{:S(2)}) collective-permute-start(bf16[64,96]{1,0:T(8,128)(2,1)S(1)} %get-tuple-element.18), channel_id=1, source_target_pairs={{0,128},{64,192},{128,0},{192,64},{1,129},{65,193},{129,1},{193,65... | collective-permute-start | bytes 36872 | tf_op jit(solution)/shard_map/ppermute | solution.py:265
  91.8 10.0 %collective-permute-start.3 = (bf16[64,96]{1,0:T(8,128)(2,1)S(1)}, bf16[64,96]{1,0:T(8,128)(2,1)S(1)}, u32[]{:S(2)}, u32[]{:S(2)}) collective-permute-start(bf16[64,96]{1,0:T(8,128)(2,1)S(1)} %get-tuple-element.17), channel_id=1, source_target_pairs={{0,192},{64,0},{128,64},{192,128},{1,193},{65,1},{129,65},{193,129... | collective-permute-start | bytes 36872 | tf_op jit(solution)/shard_map/ppermute | solution.py:265
  103.4 2.0 %collective-permute-start.7 = (f32[16,1280]{1,0:T(8,128)S(1)}, f32[16,1280]{1,0:T(8,128)S(1)}, u32[]{:S(2)}, u32[]{:S(2)}) collective-permute-start(f32[16,1280]{1,0:T(8,128)S(1)} %get-tuple-element.14), channel_id=1, source_target_pairs={{0,2},{2,0},{4,6},{6,4},{1,3},{3,1},{5,7},{7,5},{8,10},{10,8},{12,... | collective-permute-start | bytes 245768 | tf_op jit(solution)/shard_map/ppermute | solution.py:280
  103.5 5.3 %collective-permute-start.8 = (f32[16,1280]{1,0:T(8,128)S(1)}, f32[16,1280]{1,0:T(8,128)S(1)}, u32[]{:S(2)}, u32[]{:S(2)}) collective-permute-start(f32[16,1280]{1,0:T(8,128)S(1)} %get-tuple-element.16), channel_id=1, source_target_pairs={{0,4},{2,6},{4,0},{6,2},{1,5},{3,7},{5,1},{7,3},{8,12},{10,14},{12... | collective-permute-start | bytes 245768 | tf_op jit(solution)/shard_map/ppermute | solution.py:280
  104.1 5.6 %collective-permute-start.9 = (f32[16,1280]{1,0:T(8,128)S(1)}, f32[16,1280]{1,0:T(8,128)S(1)}, u32[]{:S(2)}, u32[]{:S(2)}) collective-permute-start(f32[16,1280]{1,0:T(8,128)S(1)} %get-tuple-element.15), channel_id=1, source_target_pairs={{0,6},{2,4},{4,2},{6,0},{1,7},{3,5},{5,3},{7,1},{8,14},{10,12},{12... | collective-permute-start | bytes 245768 | tf_op jit(solution)/shard_map/ppermute | solution.py:280
  111.6 16.3 %all-to-all-start.1 = ((bf16[32,5,128]{2,1,0:T(8,128)(2,1)}), bf16[32,5,128]{2,1,0:T(8,128)(2,1)S(1)}, u32[]{:S(2)}, u32[]{:S(2)}) async-start(bf16[32,5,128]{2,1,0:T(8,128)(2,1)} %reshape.159), calls=%async_computation.1 | async-start | bytes 131072 | tf_op jit(solution)/shard_map/all_to_all | solution.py:294
  128.9 14.7 %all-to-all-start.2 = ((bf16[32,20,128]{2,1,0:T(8,128)(2,1)}), bf16[32,20,128]{2,1,0:T(8,128)(2,1)S(1)}, u32[]{:S(2)}, u32[]{:S(2)}) async-start(bf16[32,20,128]{2,1,0:T(8,128)(2,1)} %copy.53), calls=%async_computation.2 | async-start | bytes 393216 | tf_op jit(solution)/shard_map/all_to_all | solution.py:297
  143.6 1.6 copy-start.8
  145.2 19.9 %copy-start = (bf16[1280,1024]{1,0:T(8,128)(2,1)S(1)}, bf16[1280,1024]{1,0:T(8,128)(2,1)}, u32[]{:S(2)}) copy-start(bf16[1280,1024]{1,0:T(8,128)(2,1)} %key_ref.3) | copy-start | bytes 7864324
  151.0 14.1 %copy-start.3 = (bf16[128,1024]{1,0:T(8,128)(2,1)S(1)}, bf16[128,1024]{1,0:T(8,128)(2,1)}, u32[]{:S(2)}) copy-start(bf16[128,1024]{1,0:T(8,128)(2,1)} %query_ref.3) | copy-start | bytes 786436
  151.0 14.1 %copy-start.7 = (f32[1024]{0:T(1024)S(1)}, f32[1024]{0:T(1024)}, u32[]{:S(2)}) copy-start(f32[1024]{0:T(1024)} %param.32) | copy-start | bytes 12292
  151.0 18.6 %all-to-all-start.4 = ((bf16[32,32,128]{2,1,0:T(8,128)(2,1)}), bf16[32,32,128]{2,1,0:T(8,128)(2,1)S(1)}, u32[]{:S(2)}, u32[]{:S(2)}) async-start(bf16[32,32,128]{2,1,0:T(8,128)(2,1)} %self_attention.1), calls=%async_computation.4 | async-start | bytes 524288 | tf_op jit(solution)/shard_map/all_to_all | solution.py:324
  165.1 1.7 copy-start.1
  (4 other events, 3.4 us)
Sparse Core Ops, SparseCore 0:
  25.8 30.5 all-gather.3
  77.4 34.1 all-gather.5

commit v3 on v2

--- a/solution.py
+++ b/solution.py
@@ -48,17 +48,25 @@
     )
 
 
-def pack_kernel(query_ref, key_ref, value_ref, out_ref, packed_ref):
+def pack_kernel(query_ref, key_ref, value_ref, out_ref, pair_key_ref, pair_value_ref, packed_ref):
     heads = query_ref.shape[1] // RHD
     copies = packed_ref.shape[0] // heads
+    piece = pair_key_ref.shape[0] // heads
     out_columns = out_ref[...].T
     for head in range(heads):
         span = slice(head * RHD, (head + 1) * RHD)
         row = jnp.concatenate(
             [query_ref[:, span], key_ref[:, span], value_ref[:, span], out_columns[:, span]], 1
-        )
+        ).astype(jnp.float32)
+        row = jnp.concatenate([row[:, lane : lane + 128] for lane in range(0, 4 * RHD, 128)], 0)
+        row = row.astype(jnp.bfloat16)
+        here = slice(head * piece, (head + 1) * piece)
         for copy in range(copies):
-            packed_ref[head * copies + copy] = row
+            target = head * copies + copy
+            lanes = slice(copy * HD, (copy + 1) * HD)
+            packed_ref[target, 0:piece] = pair_key_ref[here, lanes]
+            packed_ref[target, piece : 2 * piece] = pair_value_ref[here, lanes]
+            packed_ref[target, 2 * piece :] = row
 
 
 def heads_kernel(core_ref, own_ref, other_ref, latent_ref, weight_ref, out_ref):
@@ -66,7 +74,12 @@
     images, latent_rows, _ = out_ref.shape
     half = own_ref.shape[0] // images
     overlap = 2 * half - 257
-    weight = weight_ref[...]
+    packed = weight_ref[:, 64:, :].astype(jnp.float32)
+    blocks, depth = packed.shape[0], packed.shape[1] // 3
+    weight = jnp.concatenate(
+        [packed[:, lane * depth : (lane + 1) * depth].reshape(blocks * depth, 128) for lane in range(3)],
+        1,
+    ).astype(jnp.bfloat16)
 
     def project(rows):
         return jnp.dot(rows, weight, preferred_element_type=jnp.float32).astype(jnp.bfloat16)
@@ -97,7 +110,8 @@
             context = context + jnp.dot(
                 weights.astype(jnp.bfloat16), values, preferred_element_type=jnp.float32
             )
-        out_ref[image] = (context / total).astype(jnp.bfloat16)
+        context = jnp.concatenate([jnp.zeros((latent_rows, 128 - RHD), jnp.float32), context / total], 1)
+        out_ref[image] = context.astype(jnp.bfloat16)
 
 
 def project_kernel(*refs):
@@ -222,42 +236,36 @@
     latent_rows, full_width = latents.shape
     bf16, f32 = jnp.bfloat16, jnp.float32
 
-    depth, columns = rs_query.shape
-    weights = call(
-        pack_kernel,
-        jax.ShapeDtypeStruct((blocks, depth, 4 * RHD), bf16),
-        [VMEM] * 4,
-        "pack_weights",
-        1000000,
-    )(rs_query, rs_key, rs_value, rs_out)
-    weights = lax.all_to_all(weights, BLK, 0, 0, tiled=True)
-    weights = weights.reshape(blocks * depth, 4 * RHD)
-
     patches = features.shape[1]
     half = -(-patches // 16) * 8
     own_rows = lax.dynamic_slice_in_dim(features[0], own_core * (patches - half), half, 0)
     own_rows = layer_norm(own_rows, context_gain).astype(bf16)
+    own_rows, rs_query = lax.optimization_barrier((own_rows, rs_query))
     own_rows = lax.all_gather(own_rows, "y", axis=0, tiled=True)
     other_rows = lax.ppermute(own_rows, "core", [(0, 1), (1, 0)])
     latent_norm = layer_norm(latents, latent_gain).astype(bf16)
 
-    packed = jnp.concatenate(
-        [by_head(part, y_size, z_size) for part in (text_query, text_key, text_value)], 1
-    )
-    packed, weights = lax.optimization_barrier((packed, weights))
+    depth = rs_query.shape[0]
+    weight_rows = depth * 4 * RHD // 128
+    packed = call(
+        pack_kernel,
+        jax.ShapeDtypeStruct((blocks, 2 * piece + weight_rows, 128), bf16),
+        [VMEM] * 6,
+        "pack_targets",
+        1000000,
+    )(rs_query, rs_key, rs_value, rs_out, text_key, text_value)
     packed = lax.all_to_all(packed, BLK, 0, 0, tiled=True)
-    head_query = packed[:, 0:piece]
-    pairs = lax.all_gather(packed[:, piece:], "y", axis=0, tiled=False)
+    out_weight = packed[:, 2 * piece + weight_rows - depth :].reshape(blocks * depth, 128)
+    pairs = packed[:, 0 : 2 * piece]
 
     contexts = call(
         heads_kernel,
-        jax.ShapeDtypeStruct((y_size, latent_rows, RHD), bf16),
+        jax.ShapeDtypeStruct((y_size, latent_rows, 128), bf16),
         [SMEM] + [VMEM] * 4,
         "resampler_heads",
         1000000000,
-    )(own_core[None], own_rows, other_rows, latent_norm, weights)
-
-    out_weight = weights[:, 3 * RHD :]
+    )(own_core[None], own_rows, other_rows, latent_norm, packed)
+
     context_parts, weight_parts = [], []
     for step in range(y_size):
         part = lax.dynamic_index_in_dim(contexts, (own_y + step) % y_size, 0, keepdims=False)
@@ -272,6 +280,9 @@
         70000000,
     )(*context_parts, *weight_parts)
 
+    pairs, partial_out = lax.optimization_barrier((pairs, partial_out))
+    pairs = lax.all_gather(pairs, "y", axis=0, tiled=False)
+
     quarter = latent_rows // heads_of
     summed = lax.dynamic_slice_in_dim(partial_out, own_img * quarter, quarter, 0)
     for step in range(1, heads_of):
@@ -291,11 +302,17 @@
     tiles = full_width // 128
     chunk = quarter * tiles // blocks
     spread = jnp.transpose(resampled.reshape(quarter, tiles, 128), (1, 0, 2))
-    spread = lax.all_to_all(spread.reshape(blocks, chunk, 128), BLK, 0, 0, tiled=True)
+    spread = spread.reshape(blocks, chunk, 128)
+    head_query = by_head(text_query, y_size, z_size)
+    padding = jnp.zeros((blocks, -chunk % 8, 128), bf16)
+    spread = jnp.concatenate([head_query, spread, padding], 1)
+    spread = lax.all_to_all(spread, BLK, 0, 0, tiled=True)
+    head_query, spread = spread[:, 0:piece], spread[:, piece : piece + chunk]
     chosen = jnp.einsum("dsi,icl->dscl", choice, spread, preferred_element_type=f32)
     chosen = chosen.astype(bf16).reshape(blocks, slots * chunk, 128)
+    chosen, head_query = lax.optimization_barrier((chosen, head_query))
     chosen = lax.all_to_all(chosen, BLK, 0, 0, tiled=True)
-    chosen, pairs = lax.optimization_barrier((chosen, pairs))
+    arrived = chosen
     chosen = jnp.transpose(chosen.reshape(blocks, slots, chunk, 128), (1, 0, 2, 3))
     chosen = chosen.reshape(slots, blocks * chunk, 128)
     window = lax.all_gather(chosen, IMG, axis=0, tiled=True)
@@ -321,6 +338,7 @@
         1200000000,
         scratch=[pltpu.VMEM((y_size, 128, blocks * piece), f32)],
     )(own_y[None], head_query, pairs)
+    self_rows, arrived = lax.optimization_barrier((self_rows, arrived))
     self_rows = lax.all_to_all(self_rows, BLK, 0, 0, tiled=True)
     self_out = jnp.transpose(self_rows.reshape(y_size, z_size, piece, HD), (0, 2, 1, 3))
     return (cross_out, self_out.reshape(tokens, -1))

time: 181 us -> 158 us (0.87)
  waiting for transfers between devices: 73 us -> 56.7 us
  local copies, waits for them, and re-layouts: 11.6 us -> 6.57 us
  starting transfers between devices: 49.2 us -> 45.1 us
  other arithmetic: 5.8 us -> 8.96 us
    all_gather x1, waiting for transfers between devices: 0.68 us -> 25.1 us  [shards(): own_rows = lax.all_gather(own_rows, 'y', axis=0, tiled=True)]
    all_to_all x2 -> x1, waiting for transfers between devices: 30.4 us -> 11.9 us  [shards(): spread = lax.all_to_all(spread, BLK, 0, 0, tiled=True)]
    all_to_all x2 -> x1, starting transfers between devices: 19.7 us -> 8.4 us  [shards(): spread = lax.all_to_all(spread, BLK, 0, 0, tiled=True)]
    all_to_all x1, waiting for transfers between devices: 19.4 us -> 9.7 us  [shards(): packed = lax.all_to_all(packed, BLK, 0, 0, tiled=True)]
    ppermute x3, waiting for transfers between devices: 8.19 us -> 2.58 us  [shards(): lax.ppermute(out_weight, 'y', turn)]
    all_to_all x1, waiting for transfers between devices: 7.21 us -> 1.64 us  [shards(): chosen = lax.all_to_all(chosen, BLK, 0, 0, tiled=True)]
    all_to_all x1, starting transfers between devices: 7.43 us -> 11.6 us  [shards(): packed = lax.all_to_all(packed, BLK, 0, 0, tiled=True)]
    unnamed x43 -> x37, local copies, waits for them, and re-layouts: 7.54 us -> 4.3 us
  transfers between devices with their start and end apart: 17 -> 16, of which waited for: 10 -> 9; matrix products, arithmetic and copies ran while one was open for 6% -> 5% of each run, Pallas kernels for 5% -> 9%
where the time goes in v3:
time: 158 us; the launch traced here: 156 us
  waiting for transfers between devices  56.7 us (36%)
  starting transfers between devices  45.1 us (29%)
  Pallas kernels  16.5 us (10%)
  between operations  14.5 us (9%)
  other arithmetic  8.96 us (6%)
  blocking collectives  7 us (4%)
  local copies, waits for them, and re-layouts  6.57 us (4%)
    all_gather x1, waiting for transfers between devices, shards(): own_rows = lax.all_gather(own_rows, 'y', axis=0, tiled=True)  25.1 us
    all_to_all x1, waiting for transfers between devices, shards(): spread = lax.all_to_all(spread, BLK, 0, 0, tiled=True)  11.9 us
    all_to_all x1, starting transfers between devices, shards(): packed = lax.all_to_all(packed, BLK, 0, 0, tiled=True)  11.6 us
    all_to_all x1, waiting for transfers between devices, shards(): packed = lax.all_to_all(packed, BLK, 0, 0, tiled=True)  9.7 us
    all_to_all x1, starting transfers between devices, shards(): spread = lax.all_to_all(spread, BLK, 0, 0, tiled=True)  8.4 us
    all_to_all x1, starting transfers between devices, shards(): self_rows = lax.all_to_all(self_rows, BLK, 0, 0, tiled=True)  8.28 us
    all_gather x1, blocking collectives, shards(): window = lax.all_gather(chosen, IMG, axis=0, tiled=True)  7 us
    all_to_all x1, starting transfers between devices, shards(): chosen = lax.all_to_all(chosen, BLK, 0, 0, tiled=True)  6.58 us
  transfers between devices with their start and end apart: 16, of which 9 were waited for; matrix products, arithmetic and copies ran while one was open for 5% of the time, Pallas kernels for 9%

profile of v3, /device:TPU:26, one launch (start us, length us, event | category | flops | bytes accessed | tf_op | source)
XLA Modules:
  0.0 155.6 jit_solution(5233528195266446178)
XLA Ops:
  7.3 1.2 convert_reduce_fusion
  8.5 1.2 fusion.3
  9.8 2.0 %fusion.5 = bf16[136,1280]{1,0:T(8,128)(2,1)} fusion(f32[1280]{0:T(1024)} %param.19, f32[136]{0:T(256)S(1)} %add_rsqrt_fusion, f32[136]{0:T(256)S(1)} %broadcast_multiply_fusion, bf16[1,257,1280]{2,1,0:T(8,128)(2,1)} %param.17, s32[]{:T(128)S(6)} %select_n.63), kind=kLoop, calls=%fused_computation.8 | loop fusion | flops 870400 | bytes 702532 | tf_op jit(solution)/shard_map/convert_element_type | solution.py:242
  12.0 1.4 pack_targets.1
  13.4 11.6 %all-to-all-start = ((bf16[32,184,128]{2,1,0:T(8,128)(2,1)}), bf16[32,184,128]{2,1,0:T(8,128)(2,1)S(1)}, u32[]{:S(2)}, u32[]{:S(2)}) async-start(bf16[32,184,128]{2,1,0:T(8,128)(2,1)} %pack_targets.1), calls=%async_computation | async-start | bytes 3014656 | tf_op jit(solution)/shard_map/all_to_all | solution.py:257
  25.1 25.1 %all-gather.4.cloned.1.call-done.own_ref = bf16[544,1280]{1,0:T(8,128)(2,1)} async-done(((bf16[136,1280]{1,0:T(8,128)(2,1)}), bf16[544,1280]{1,0:T(8,128)(2,1)}) %all-gather.4.cloned.1.call-update) | async-done | bytes 1392656 | tf_op jit(solution)/shard_map/all_gather | solution.py:244
  51.1 9.7 %all-to-all-done.weight_ref = bf16[32,184,128]{2,1,0:T(8,128)(2,1)S(1)} async-done(((bf16[32,184,128]{2,1,0:T(8,128)(2,1)}), bf16[32,184,128]{2,1,0:T(8,128)(2,1)S(1)}, u32[]{:S(2)}, u32[]{:S(2)}) %all-to-all-start) | async-done | bytes 1507360 | tf_op jit(solution)/shard_map/all_to_all | solution.py:257
  60.9 2.5 %collective-permute-start.4 = (bf16[1280,128]{1,0:T(8,128)(2,1)S(1)}, bf16[1280,128]{1,0:T(8,128)(2,1)}, u32[]{:S(2)}, u32[]{:S(2)}) collective-permute-start(bf16[1280,128]{1,0:T(8,128)(2,1)S(1)} %bitcast.57), channel_id=1, source_target_pairs={{0,64},{64,128},{128,192},{192,0},{1,65},{65,129},{129,193},{193,1... | collective-permute-start | bytes 983048 | tf_op jit(solution)/shard_map/ppermute | solution.py:274
  64.3 0.8 fusion.10.latent_ref
  65.2 4.8 %resampler_heads.1 = bf16[4,64,128]{2,1,0:T(8,128)(2,1)S(1)} custom-call(s32[1]{0:T(128)} %bitcast.5.core_ref, bf16[544,1280]{1,0:T(8,128)(2,1)S(1)} %copy-done.2, bf16[544,1280]{1,0:T(8,128)(2,1)} %collective-permute-done.other_ref, bf16[64,1280]{1,0:T(8,128)(2,1)S(1)} %fusion.10.latent_ref, bf16[32,184,128]{2,1,0:T(8,128)(2,1)S(1)} %all-to-all-done.weight_ref), custom_call_target="tpu_custom_call" | custom-call | flops 1000000000 | bytes 3000000 | tf_op jit(solution)/shard_map/resampler_heads/pallas_call | solution.py:261
  70.1 2.7 %collective-permute-start.1 = (bf16[64,128]{1,0:T(8,128)(2,1)S(1)}, bf16[64,128]{1,0:T(8,128)(2,1)S(1)}, u32[]{:S(2)}, u32[]{:S(2)}) collective-permute-start(bf16[64,128]{1,0:T(8,128)(2,1)S(1)} %get-tuple-element.25), channel_id=1, source_target_pairs={{0,64},{64,128},{128,192},{192,0},{1,65},{65,129},{129,193},{193,1... | collective-permute-start | bytes 49160 | tf_op jit(solution)/shard_map/ppermute | solution.py:273
  72.7 2.0 %collective-permute-start.2 = (bf16[64,128]{1,0:T(8,128)(2,1)S(1)}, bf16[64,128]{1,0:T(8,128)(2,1)S(1)}, u32[]{:S(2)}, u32[]{:S(2)}) collective-permute-start(bf16[64,128]{1,0:T(8,128)(2,1)S(1)} %get-tuple-element.24), channel_id=1, source_target_pairs={{0,128},{64,192},{128,0},{192,64},{1,129},{65,193},{129,1},{193,65... | collective-permute-start | bytes 49160 | tf_op jit(solution)/shard_map/ppermute | solution.py:273
  74.7 0.9 slice.16
  75.6 2.6 %collective-permute-done.6.refs_7_ = bf16[1280,128]{1,0:T(8,128)(2,1)} collective-permute-done((bf16[1280,128]{1,0:T(8,128)(2,1)S(1)}, bf16[1280,128]{1,0:T(8,128)(2,1)}, u32[]{:S(2)}, u32[]{:S(2)}) %collective-permute-start.6) | collective-permute-done | bytes 327712 | tf_op jit(solution)/shard_map/ppermute | solution.py:274
  78.6 1.6 %collective-permute-done.3.refs_3_ = bf16[64,128]{1,0:T(8,128)(2,1)S(1)} collective-permute-done((bf16[64,128]{1,0:T(8,128)(2,1)S(1)}, bf16[64,128]{1,0:T(8,128)(2,1)S(1)}, u32[]{:S(2)}, u32[]{:S(2)}) %collective-permute-start.3) | collective-permute-done | bytes 16416 | tf_op jit(solution)/shard_map/ppermute | solution.py:273
  80.2 1.7 %project_out.1 = f32[64,1280]{1,0:T(8,128)S(1)} custom-call(bf16[64,128]{1,0:T(8,128)(2,1)S(1)} %get-tuple-element.26.refs_0_, bf16[64,128]{1,0:T(8,128)(2,1)S(1)} %collective-permute-done.1.refs_1_, bf16[64,128]{1,0:T(8,128)(2,1)S(1)} %collective-permute-done.2.refs_2_, bf16[64,128]{1,0:T(8,128)(2,1)S(1)} %collective-permute-done.3.refs_3_, ...), custom_call_target="tpu_custom_call" | custom-call | flops 70000000 | bytes 3000000 | tf_op jit(solution)/shard_map/project_out/pallas_call | solution.py:275
  83.0 1.2 collective-permute-start.9
  84.8 2.9 %collective-permute-done.8 = f32[16,1280]{1,0:T(8,128)S(1)} collective-permute-done((f32[16,1280]{1,0:T(8,128)S(1)}, f32[16,1280]{1,0:T(8,128)S(1)}, u32[]{:S(2)}, u32[]{:S(2)}) %collective-permute-start.8) | collective-permute-done | bytes 81952 | tf_op jit(solution)/shard_map/ppermute | solution.py:291
  87.7 0.8 collective-permute-done.9
  89.0 0.9 maximum_maximum_fusion
  89.9 8.4 %all-to-all-start.1 = ((bf16[32,40,128]{2,1,0:T(8,128)(2,1)}), bf16[32,40,128]{2,1,0:T(8,128)(2,1)S(1)}, u32[]{:S(2)}, u32[]{:S(2)}) async-start(bf16[32,40,128]{2,1,0:T(8,128)(2,1)} %maximum_maximum_fusion), calls=%async_computation.1 | async-start | bytes 655360 | tf_op jit(solution)/shard_map/all_to_all | solution.py:309
  98.5 11.9 %all-to-all-done.1 = bf16[32,40,128]{2,1,0:T(8,128)(2,1)S(1)} async-done(((bf16[32,40,128]{2,1,0:T(8,128)(2,1)}), bf16[32,40,128]{2,1,0:T(8,128)(2,1)S(1)}, u32[]{:S(2)}, u32[]{:S(2)}) %all-to-all-start.1) | async-done | bytes 327712 | tf_op jit(solution)/shard_map/all_to_all | solution.py:309
  110.8 0.7 copy.47
  111.5 6.6 %all-to-all-start.2 = ((bf16[32,20,128]{2,1,0:T(8,128)(2,1)}), bf16[32,20,128]{2,1,0:T(8,128)(2,1)S(1)}, u32[]{:S(2)}, u32[]{:S(2)}) async-start(bf16[32,20,128]{2,1,0:T(8,128)(2,1)} %copy.47), calls=%async_computation.2 | async-start | bytes 393216 | tf_op jit(solution)/shard_map/all_to_all | solution.py:314
  118.2 1.6 %copy-done.10 = bf16[128,64,128]{2,1,0:T(8,128)(2,1)S(1)} copy-done((bf16[128,64,128]{2,1,0:T(8,128)(2,1)S(1)}, bf16[128,64,128]{2,1,0:T(8,128)(2,1)}, u32[]{:S(2)}) %copy-start.10) | copy-done | bytes 2097176
  119.8 5.8 %self_attention.1 = bf16[32,32,128]{2,1,0:T(8,128)(2,1)} custom-call(s32[1]{0:T(128)} %bitcast.19.own_ref, bf16[32,32,128]{2,1,0:T(8,128)(2,1)S(1)} %slice.19.q_ref, bf16[4,32,64,128]{3,2,1,0:T(8,128)(2,1)S(1)} %bitcast.62), custom_call_target="tpu_custom_call" | custom-call | flops 1200000000 | bytes 3000000 | tf_op jit(solution)/shard_map/self_attention/pallas_call | solution.py:333
  125.6 1.6 %all-to-all-done.2 = bf16[32,20,128]{2,1,0:T(8,128)(2,1)S(1)} async-done(((bf16[32,20,128]{2,1,0:T(8,128)(2,1)}), bf16[32,20,128]{2,1,0:T(8,128)(2,1)S(1)}, u32[]{:S(2)}, u32[]{:S(2)}) %all-to-all-start.2) | async-done | bytes 163872 | tf_op jit(solution)/shard_map/all_to_all | solution.py:314
  127.3 8.3 %all-to-all-start.3 = ((bf16[32,32,128]{2,1,0:T(8,128)(2,1)}), bf16[32,32,128]{2,1,0:T(8,128)(2,1)S(1)}, u32[]{:S(2)}, u32[]{:S(2)}) async-start(bf16[32,32,128]{2,1,0:T(8,128)(2,1)} %self_attention.1), calls=%async_computation.3 | async-start | bytes 524288 | tf_op jit(solution)/shard_map/all_to_all | solution.py:342
  136.4 7.0 %all_gather.13.window_ref = bf16[16,160,128]{2,1,0:T(8,128)(2,1)S(1)} all-gather(bf16[4,160,128]{2,1,0:T(8,128)(2,1)S(1)} %copy.50), channel_id=1, replica_groups=mesh['y'=4,'z'=8,'xl'=2,'core'=2,'doc'=2] {'xl','core'}, dimensions={0}, use_global_device_ids=true | all-gather | bytes 819200 | tf_op jit(solution)/shard_map/all_gather | solution.py:318
  143.4 1.7 %copy-done.1 = bf16[1280,1024]{1,0:T(8,128)(2,1)S(1)} copy-done((bf16[1280,1024]{1,0:T(8,128)(2,1)S(1)}, bf16[1280,1024]{1,0:T(8,128)(2,1)}, u32[]{:S(2)}) %copy-start.1) | copy-done | bytes 2621464
  145.1 2.8 %cross_attention.1 = bf16[128,1024]{1,0:T(8,128)(2,1)} custom-call(bf16[16,160,128]{2,1,0:T(8,128)(2,1)S(1)} %all_gather.13.window_ref, bf16[1280,1024]{1,0:T(8,128)(2,1)S(1)} %copy-done, bf16[1280,1024]{1,0:T(8,128)(2,1)S(1)} %copy-done.1, bf16[128,1024]{1,0:T(8,128)(2,1)S(1)} %copy-done.5, f32[1,1024]{1,0:T(1,128)S(1)} %bitcast.61, s32[128,1]{1,0:T(8,128)S(1)} %copy.51.slot_ref), custom_call_target="tpu_custom_call" | custom-call | flops 1500000000 | bytes 3000000 | tf_op jit(solution)/shard_map/cross_attention/pallas_call | solution.py:325
  148.0 0.8 copy.61
  (88 shorter events, 6.1 us)
Async XLA Ops:
  7.2 4.8 %copy-start.6 = (bf16[40,384]{1,0:T(8,128)(2,1)S(1)}, bf16[40,384]{1,0:T(8,128)(2,1)}, u32[]{:S(2)}) copy-start(bf16[40,384]{1,0:T(8,128)(2,1)} %query_ref.1) | copy-start | bytes 92164
  7.2 4.6 %copy-start.13 = (bf16[384,40]{0,1:T(8,128)(2,1)S(1)}, bf16[384,40]{0,1:T(8,128)(2,1)}, u32[]{:S(2)}) copy-start(bf16[384,40]{0,1:T(8,128)(2,1)} %param.25) | copy-start | bytes 92164
  7.2 4.8 %copy-start.7 = (bf16[40,384]{1,0:T(8,128)(2,1)S(1)}, bf16[40,384]{1,0:T(8,128)(2,1)}, u32[]{:S(2)}) copy-start(bf16[40,384]{1,0:T(8,128)(2,1)} %key_ref.2) | copy-start | bytes 92164
  7.2 4.8 %copy-start.8 = (bf16[40,384]{1,0:T(8,128)(2,1)S(1)}, bf16[40,384]{1,0:T(8,128)(2,1)}, u32[]{:S(2)}) copy-start(bf16[40,384]{1,0:T(8,128)(2,1)} %value_ref.2) | copy-start | bytes 92164
  7.2 4.8 %copy-start.3 = (bf16[128,1024]{1,0:T(8,128)(2,1)S(1)}, bf16[128,1024]{1,0:T(8,128)(2,1)}, u32[]{:S(2)}) copy-start(bf16[128,1024]{1,0:T(8,128)(2,1)} %pair_key_ref.1) | copy-start | bytes 786436
  7.2 4.8 %copy-start.4 = (bf16[128,1024]{1,0:T(8,128)(2,1)S(1)}, bf16[128,1024]{1,0:T(8,128)(2,1)}, u32[]{:S(2)}) copy-start(bf16[128,1024]{1,0:T(8,128)(2,1)} %pair_value_ref.1) | copy-start | bytes 786436
  7.2 43.0 %all-gather.4.cloned.1.call-start = ((), (), s32[]{:S(2)}) async-start(), calls=%async_computation.4 | async-start | bytes 1740800 | tf_op jit(solution)/shard_map/all_gather | solution.py:244
  13.4 36.9 %copy-start.11 = (bf16[64,1280]{1,0:T(8,128)(2,1)S(1)}, bf16[64,1280]{1,0:T(8,128)(2,1)}, u32[]{:S(2)}) copy-start(bf16[64,1280]{1,0:T(8,128)(2,1)} %param.18) | copy-start | bytes 491524
  13.4 47.5 %all-to-all-start = ((bf16[32,184,128]{2,1,0:T(8,128)(2,1)}), bf16[32,184,128]{2,1,0:T(8,128)(2,1)S(1)}, u32[]{:S(2)}, u32[]{:S(2)}) async-start(bf16[32,184,128]{2,1,0:T(8,128)(2,1)} %pack_targets.1), calls=%async_computation | async-start | bytes 3014656 | tf_op jit(solution)/shard_map/all_to_all | solution.py:257
  25.0 93.2 %all-gather.6.cloned.1.call-start = ((), (), s32[]{:S(2)}) async-start(), calls=%async_computation.5 | async-start | bytes 2621440 | tf_op jit(solution)/shard_map/all_gather | solution.py:284
  50.2 15.0 %copy-start.2 = (bf16[544,1280]{1,0:T(8,128)(2,1)S(1)}, bf16[544,1280]{1,0:T(8,128)(2,1)}, u32[]{:S(2)}) copy-start(bf16[544,1280]{1,0:T(8,128)(2,1)} %all-gather.4.cloned.1.call-done.own_ref) | copy-start | bytes 4177924
  50.2 15.0 %collective-permute-start = (bf16[544,1280]{1,0:T(8,128)(2,1)}, bf16[544,1280]{1,0:T(8,128)(2,1)}, u32[]{:S(2)}, u32[]{:S(2)}) collective-permute-start(bf16[544,1280]{1,0:T(8,128)(2,1)} %all-gather.4.cloned.1.call-done.own_ref), channel_id=1, source_target_pairs={{0,2},{2,0},{1,3},{3,1},{4,6},{6,4},{5,7},{7,5},{8,10},{10,8},{9,1... | collective-permute-start | bytes 4177928 | tf_op jit(solution)/shard_map/ppermute | solution.py:245
  60.9 13.9 %collective-permute-start.4 = (bf16[1280,128]{1,0:T(8,128)(2,1)S(1)}, bf16[1280,128]{1,0:T(8,128)(2,1)}, u32[]{:S(2)}, u32[]{:S(2)}) collective-permute-start(bf16[1280,128]{1,0:T(8,128)(2,1)S(1)} %bitcast.57), channel_id=1, source_target_pairs={{0,64},{64,128},{128,192},{192,0},{1,65},{65,129},{129,193},{193,1... | collective-permute-start | bytes 983048 | tf_op jit(solution)/shard_map/ppermute | solution.py:274
  63.4 12.3 %collective-permute-start.5 = (bf16[1280,128]{1,0:T(8,128)(2,1)S(1)}, bf16[1280,128]{1,0:T(8,128)(2,1)}, u32[]{:S(2)}, u32[]{:S(2)}) collective-permute-start(bf16[1280,128]{1,0:T(8,128)(2,1)S(1)} %bitcast.58), channel_id=1, source_target_pairs={{0,128},{64,192},{128,0},{192,64},{1,129},{65,193},{129,1},{193,65... | collective-permute-start | bytes 983048 | tf_op jit(solution)/shard_map/ppermute | solution.py:274
  63.7 14.5 %collective-permute-start.6 = (bf16[1280,128]{1,0:T(8,128)(2,1)S(1)}, bf16[1280,128]{1,0:T(8,128)(2,1)}, u32[]{:S(2)}, u32[]{:S(2)}) collective-permute-start(bf16[1280,128]{1,0:T(8,128)(2,1)S(1)} %bitcast.59), channel_id=1, source_target_pairs={{0,192},{64,0},{128,64},{192,128},{1,193},{65,1},{129,65},{193,129... | collective-permute-start | bytes 983048 | tf_op jit(solution)/shard_map/ppermute | solution.py:274
  70.1 8.1 %collective-permute-start.1 = (bf16[64,128]{1,0:T(8,128)(2,1)S(1)}, bf16[64,128]{1,0:T(8,128)(2,1)S(1)}, u32[]{:S(2)}, u32[]{:S(2)}) collective-permute-start(bf16[64,128]{1,0:T(8,128)(2,1)S(1)} %get-tuple-element.25), channel_id=1, source_target_pairs={{0,64},{64,128},{128,192},{192,0},{1,65},{65,129},{129,193},{193,1... | collective-permute-start | bytes 49160 | tf_op jit(solution)/shard_map/ppermute | solution.py:273
  72.7 5.9 %collective-permute-start.2 = (bf16[64,128]{1,0:T(8,128)(2,1)S(1)}, bf16[64,128]{1,0:T(8,128)(2,1)S(1)}, u32[]{:S(2)}, u32[]{:S(2)}) collective-permute-start(bf16[64,128]{1,0:T(8,128)(2,1)S(1)} %get-tuple-element.24), channel_id=1, source_target_pairs={{0,128},{64,192},{128,0},{192,64},{1,129},{65,193},{129,1},{193,65... | collective-permute-start | bytes 49160 | tf_op jit(solution)/shard_map/ppermute | solution.py:273
  74.7 7.3 %copy-start.12 = (bf16[128,1024]{1,0:T(8,128)(2,1)S(1)}, bf16[128,1024]{1,0:T(8,128)(2,1)}, u32[]{:S(2)}) copy-start(bf16[128,1024]{1,0:T(8,128)(2,1)} %param.28) | copy-start | bytes 786436
  74.7 5.5 %collective-permute-start.3 = (bf16[64,128]{1,0:T(8,128)(2,1)S(1)}, bf16[64,128]{1,0:T(8,128)(2,1)S(1)}, u32[]{:S(2)}, u32[]{:S(2)}) collective-permute-start(bf16[64,128]{1,0:T(8,128)(2,1)S(1)} %get-tuple-element.23), channel_id=1, source_target_pairs={{0,192},{64,0},{128,64},{192,128},{1,193},{65,1},{129,65},{193,129... | collective-permute-start | bytes 49160 | tf_op jit(solution)/shard_map/ppermute | solution.py:273
  80.2 4.0 %copy-start.16 = (s32[32]{0:T(128)S(1)}, s32[32]{0:T(128)}, u32[]{:S(2)}) copy-start(s32[32]{0:T(128)} %param.33) | copy-start | bytes 388
  81.9 6.9 %copy-start.14 = (f32[1280]{0:T(1024)S(1)}, f32[1280]{0:T(1024)}, u32[]{:S(2)}) copy-start(f32[1280]{0:T(1024)} %param.21) | copy-start | bytes 15364
  82.2 2.6 %collective-permute-start.7 = (f32[16,1280]{1,0:T(8,128)S(1)}, f32[16,1280]{1,0:T(8,128)S(1)}, u32[]{:S(2)}, u32[]{:S(2)}) collective-permute-start(f32[16,1280]{1,0:T(8,128)S(1)} %get-tuple-element.20), channel_id=1, source_target_pairs={{0,2},{2,0},{4,6},{6,4},{1,3},{3,1},{5,7},{7,5},{8,10},{10,8},{12,... | collective-permute-start | bytes 245768 | tf_op jit(solution)/shard_map/ppermute | solution.py:291
  82.3 5.3 %collective-permute-start.8 = (f32[16,1280]{1,0:T(8,128)S(1)}, f32[16,1280]{1,0:T(8,128)S(1)}, u32[]{:S(2)}, u32[]{:S(2)}) collective-permute-start(f32[16,1280]{1,0:T(8,128)S(1)} %get-tuple-element.22), channel_id=1, source_target_pairs={{0,4},{2,6},{4,0},{6,2},{1,5},{3,7},{5,1},{7,3},{8,12},{10,14},{12... | collective-permute-start | bytes 245768 | tf_op jit(solution)/shard_map/ppermute | solution.py:291
  83.0 5.5 %collective-permute-start.9 = (f32[16,1280]{1,0:T(8,128)S(1)}, f32[16,1280]{1,0:T(8,128)S(1)}, u32[]{:S(2)}, u32[]{:S(2)}) collective-permute-start(f32[16,1280]{1,0:T(8,128)S(1)} %get-tuple-element.21), channel_id=1, source_target_pairs={{0,6},{2,4},{4,2},{6,0},{1,7},{3,5},{5,3},{7,1},{8,14},{10,12},{12... | collective-permute-start | bytes 245768 | tf_op jit(solution)/shard_map/ppermute | solution.py:291
  89.9 20.6 %all-to-all-start.1 = ((bf16[32,40,128]{2,1,0:T(8,128)(2,1)}), bf16[32,40,128]{2,1,0:T(8,128)(2,1)S(1)}, u32[]{:S(2)}, u32[]{:S(2)}) async-start(bf16[32,40,128]{2,1,0:T(8,128)(2,1)} %maximum_maximum_fusion), calls=%async_computation.1 | async-start | bytes 655360 | tf_op jit(solution)/shard_map/all_to_all | solution.py:309
  111.5 15.8 %all-to-all-start.2 = ((bf16[32,20,128]{2,1,0:T(8,128)(2,1)}), bf16[32,20,128]{2,1,0:T(8,128)(2,1)S(1)}, u32[]{:S(2)}, u32[]{:S(2)}) async-start(bf16[32,20,128]{2,1,0:T(8,128)(2,1)} %copy.47), calls=%async_computation.2 | async-start | bytes 393216 | tf_op jit(solution)/shard_map/all_to_all | solution.py:314
  118.2 1.6 %copy-start.10 = (bf16[128,64,128]{2,1,0:T(8,128)(2,1)S(1)}, bf16[128,64,128]{2,1,0:T(8,128)(2,1)}, u32[]{:S(2)}) copy-start(bf16[128,64,128]{2,1,0:T(8,128)(2,1)} %all-gather.6.cloned.1.call-done) | copy-start | bytes 6291460
  119.8 23.6 %copy-start = (bf16[1280,1024]{1,0:T(8,128)(2,1)S(1)}, bf16[1280,1024]{1,0:T(8,128)(2,1)}, u32[]{:S(2)}) copy-start(bf16[1280,1024]{1,0:T(8,128)(2,1)} %key_ref.3) | copy-start | bytes 7864324
  125.6 17.8 %copy-start.5 = (bf16[128,1024]{1,0:T(8,128)(2,1)S(1)}, bf16[128,1024]{1,0:T(8,128)(2,1)}, u32[]{:S(2)}) copy-start(bf16[128,1024]{1,0:T(8,128)(2,1)} %query_ref.2) | copy-start | bytes 786436
  125.6 17.8 %copy-start.9 = (f32[1024]{0:T(1024)S(1)}, f32[1024]{0:T(1024)}, u32[]{:S(2)}) copy-start(f32[1024]{0:T(1024)} %param.32) | copy-start | bytes 12292
  127.3 20.7 %all-to-all-start.3 = ((bf16[32,32,128]{2,1,0:T(8,128)(2,1)}), bf16[32,32,128]{2,1,0:T(8,128)(2,1)S(1)}, u32[]{:S(2)}, u32[]{:S(2)}) async-start(bf16[32,32,128]{2,1,0:T(8,128)(2,1)} %self_attention.1), calls=%async_computation.3 | async-start | bytes 524288 | tf_op jit(solution)/shard_map/all_to_all | solution.py:342
  143.4 1.7 %copy-start.1 = (bf16[1280,1024]{1,0:T(8,128)(2,1)S(1)}, bf16[1280,1024]{1,0:T(8,128)(2,1)}, u32[]{:S(2)}) copy-start(bf16[1280,1024]{1,0:T(8,128)(2,1)} %value_ref.3) | copy-start | bytes 7864324
  (1 other events, 0.7 us)
Sparse Core Ops, SparseCore 0:
  11.9 38.2 all-gather.3
  82.1 34.5 all-gather.5

commit v4 on v3

--- a/solution.py
+++ b/solution.py
@@ -48,24 +48,42 @@
     )
 
 
-def pack_kernel(query_ref, key_ref, value_ref, out_ref, pair_key_ref, pair_value_ref, packed_ref):
-    heads = query_ref.shape[1] // RHD
-    copies = packed_ref.shape[0] // heads
-    piece = pair_key_ref.shape[0] // heads
-    out_columns = out_ref[...].T
+def prelude_kernel(core_ref, context_gain, latent_gain, *refs):
+    count = 8
+    sources, (own_ref, latent_ref, packed_ref) = refs[:count], refs[count : count + 3]
+    held, done = refs[count + 3 : 2 * count + 3], refs[2 * count + 3]
+    copies = [
+        pltpu.make_async_copy(source, target, done.at[place])
+        for place, (source, target) in enumerate(zip(sources, held))
+    ]
+    for copy in copies:
+        copy.start()
+    features, latents, query, key, value, out, text_key, text_value = held
+    for copy in copies[:2]:
+        copy.wait()
+    half, patches = own_ref.shape[0], features.shape[0]
+    rows = features[...].astype(jnp.float32)
+    rows = jnp.where(core_ref[0] == 0, rows[:half], rows[patches - half :])
+    own_ref[...] = layer_norm(rows, context_gain[...].reshape(1, -1)).astype(jnp.bfloat16)
+    latent_ref[...] = layer_norm(latents[...], latent_gain[...].reshape(1, -1)).astype(jnp.bfloat16)
+    for copy in copies[2:]:
+        copy.wait()
+    heads = query.shape[1] // RHD
+    images = packed_ref.shape[0] // heads
+    piece = text_key.shape[0] // heads
     for head in range(heads):
         span = slice(head * RHD, (head + 1) * RHD)
         row = jnp.concatenate(
-            [query_ref[:, span], key_ref[:, span], value_ref[:, span], out_columns[:, span]], 1
+            [query[:, span], key[:, span], value[:, span], out[:, span]], 1
         ).astype(jnp.float32)
         row = jnp.concatenate([row[:, lane : lane + 128] for lane in range(0, 4 * RHD, 128)], 0)
         row = row.astype(jnp.bfloat16)
         here = slice(head * piece, (head + 1) * piece)
-        for copy in range(copies):
-            target = head * copies + copy
-            lanes = slice(copy * HD, (copy + 1) * HD)
-            packed_ref[target, 0:piece] = pair_key_ref[here, lanes]
-            packed_ref[target, piece : 2 * piece] = pair_value_ref[here, lanes]
+        for image in range(images):
+            target = head * images + image
+            lanes = slice(image * HD, (image + 1) * HD)
+            packed_ref[target, 0:piece] = text_key[here, lanes]
+            packed_ref[target, piece : 2 * piece] = text_value[here, lanes]
             packed_ref[target, 2 * piece :] = row
 
 
@@ -238,22 +256,34 @@
 
     patches = features.shape[1]
     half = -(-patches // 16) * 8
-    own_rows = lax.dynamic_slice_in_dim(features[0], own_core * (patches - half), half, 0)
-    own_rows = layer_norm(own_rows, context_gain).astype(bf16)
-    own_rows, rs_query = lax.optimization_barrier((own_rows, rs_query))
+    depth = rs_query.shape[0]
+    weight_rows = depth * 4 * RHD // 128
+    operands = (
+        features[0],
+        latents,
+        rs_query,
+        rs_key,
+        rs_value,
+        jnp.transpose(rs_out),
+        text_key,
+        text_value,
+    )
+    own_rows, latent_norm, packed = call(
+        prelude_kernel,
+        (
+            jax.ShapeDtypeStruct((half, full_width), bf16),
+            jax.ShapeDtypeStruct(latents.shape, bf16),
+            jax.ShapeDtypeStruct((blocks, 2 * piece + weight_rows, 128), bf16),
+        ),
+        [SMEM, VMEM, VMEM] + [pl.BlockSpec(memory_space=pl.ANY)] * len(operands),
+        "norm_and_pack",
+        1000000,
+        limit=60,
+        scratch=[pltpu.VMEM(part.shape, part.dtype) for part in operands]
+        + [pltpu.SemaphoreType.DMA((len(operands),))],
+    )(own_core[None], context_gain, latent_gain, *operands)
     own_rows = lax.all_gather(own_rows, "y", axis=0, tiled=True)
     other_rows = lax.ppermute(own_rows, "core", [(0, 1), (1, 0)])
-    latent_norm = layer_norm(latents, latent_gain).astype(bf16)
-
-    depth = rs_query.shape[0]
-    weight_rows = depth * 4 * RHD // 128
-    packed = call(
-        pack_kernel,
-        jax.ShapeDtypeStruct((blocks, 2 * piece + weight_rows, 128), bf16),
-        [VMEM] * 6,
-        "pack_targets",
-        1000000,
-    )(rs_query, rs_key, rs_value, rs_out, text_key, text_value)
     packed = lax.all_to_all(packed, BLK, 0, 0, tiled=True)
     out_weight = packed[:, 2 * piece + weight_rows - depth :].reshape(blocks * depth, 128)
     pairs = packed[:, 0 : 2 * piece]

time: 158 us -> 157 us (level)
  other arithmetic: 8.96 us -> 3.55 us
  local copies, waits for them, and re-layouts: 6.57 us -> 8.65 us
    convert_element_type x2 -> x0, other arithmetic: 2.84 us -> none  [the longest x1 2.02 us: shards(): own_rows = layer_norm(own_rows, context_gain).astype(bf16)]
    pallas_call x1, Pallas kernels: 1.36 us -> 3.71 us  [shards(): call(prelude_kernel, (jax.ShapeDtypeStruct((half, full_width), bf16), jax...]
    unnamed x37 -> x22, local copies, waits for them, and re-layouts: 4.3 us -> 6.4 us
    all_gather x1, waiting for transfers between devices: 25.1 us -> 26.9 us  [shards(): own_rows = lax.all_gather(own_rows, 'y', axis=0, tiled=True)]
  transfers between devices with their start and end apart: 16 -> 16, of which waited for: 9 -> 9; matrix products, arithmetic and copies ran while one was open for 5% -> 4% of each run, Pallas kernels for 9% -> 8%
where the time goes in v4:
time: 157 us; the launch traced here: 154 us
  waiting for transfers between devices  57.5 us (37%)
  starting transfers between devices  45 us (29%)
  Pallas kernels  17.4 us (11%)
  between operations  14.3 us (9%)
  local copies, waits for them, and re-layouts  8.65 us (6%)
  blocking collectives  6.96 us (4%)
  other arithmetic  3.55 us (2%)
    all_gather x1, waiting for transfers between devices, shards(): own_rows = lax.all_gather(own_rows, 'y', axis=0, tiled=True)  26.9 us
    all_to_all x1, waiting for transfers between devices, shards(): spread = lax.all_to_all(spread, BLK, 0, 0, tiled=True)  11.9 us
    all_to_all x1, starting transfers between devices, shards(): packed = lax.all_to_all(packed, BLK, 0, 0, tiled=True)  11.5 us
    all_to_all x1, waiting for transfers between devices, shards(): packed = lax.all_to_all(packed, BLK, 0, 0, tiled=True)  8.83 us
    all_to_all x1, starting transfers between devices, shards(): spread = lax.all_to_all(spread, BLK, 0, 0, tiled=True)  8.4 us
    all_to_all x1, starting transfers between devices, shards(): self_rows = lax.all_to_all(self_rows, BLK, 0, 0, tiled=True)  8.27 us
    all_gather x1, blocking collectives, shards(): window = lax.all_gather(chosen, IMG, axis=0, tiled=True)  6.96 us
    all_to_all x1, starting transfers between devices, shards(): chosen = lax.all_to_all(chosen, BLK, 0, 0, tiled=True)  6.58 us
  transfers between devices with their start and end apart: 16, of which 9 were waited for; matrix products, arithmetic and copies ran while one was open for 4% of the time, Pallas kernels for 8%

profile of v4, /device:TPU:26, one launch (start us, length us, event | category | flops | bytes accessed | tf_op | source)
XLA Modules:
  0.0 153.6 jit_solution(3694634378102756060)
XLA Ops:
  7.2 3.7 %norm_and_pack.1 = (bf16[136,1280]{1,0:T(8,128)(2,1)}, bf16[64,1280]{1,0:T(8,128)(2,1)}, bf16[32,184,128]{2,1,0:T(8,128)(2,1)}) custom-call(s32[1]{0:T(128)} %bitcast.4.core_ref, f32[1280]{0:T(1024)} %context_gain.1, f32[1280]{0:T(1024)} %latent_gain.1, bf16[257,1280]{1,0:T(8,128)(2,1)} %bitcast.55, bf16[64,1280]{1,0:T(8,128)(2,1)} %refs_1_.1, ...), custom_call_target="tpu_custom_call" | custom-call | flops 1000000 | bytes 3000000 | tf_op jit(solution)/shard_map/norm_and_pack/pallas_call | solution.py:271
  11.0 11.5 %all-to-all-start = ((bf16[32,184,128]{2,1,0:T(8,128)(2,1)}), bf16[32,184,128]{2,1,0:T(8,128)(2,1)S(1)}, u32[]{:S(2)}, u32[]{:S(2)}) async-start(bf16[32,184,128]{2,1,0:T(8,128)(2,1)} %get-tuple-element.10), calls=%async_computation | async-start | bytes 3014656 | tf_op jit(solution)/shard_map/all_to_all | solution.py:287
  22.5 26.9 %all-gather.4.cloned.1.call-done.own_ref = bf16[544,1280]{1,0:T(8,128)(2,1)} async-done(((bf16[136,1280]{1,0:T(8,128)(2,1)}), bf16[544,1280]{1,0:T(8,128)(2,1)}) %all-gather.4.cloned.1.call-update) | async-done | bytes 1392656 | tf_op jit(solution)/shard_map/all_gather | solution.py:285
  49.5 8.8 %all-to-all-done.weight_ref = bf16[32,184,128]{2,1,0:T(8,128)(2,1)S(1)} async-done(((bf16[32,184,128]{2,1,0:T(8,128)(2,1)}), bf16[32,184,128]{2,1,0:T(8,128)(2,1)S(1)}, u32[]{:S(2)}, u32[]{:S(2)}) %all-to-all-start) | async-done | bytes 1507360 | tf_op jit(solution)/shard_map/all_to_all | solution.py:287
  58.3 2.5 %collective-permute-start.4 = (bf16[1280,128]{1,0:T(8,128)(2,1)S(1)}, bf16[1280,128]{1,0:T(8,128)(2,1)S(1)}, u32[]{:S(2)}, u32[]{:S(2)}) collective-permute-start(bf16[1280,128]{1,0:T(8,128)(2,1)S(1)} %bitcast.45), channel_id=1, source_target_pairs={{0,64},{64,128},{128,192},{192,0},{1,65},{65,129},{129,193},{193,1... | collective-permute-start | bytes 983048 | tf_op jit(solution)/shard_map/ppermute | solution.py:304
  61.1 0.7 collective-permute-start.6
  61.8 1.3 copy-done.2
  63.1 0.9 copy-done.4
  64.1 3.5 %resampler_heads.1 = bf16[4,64,128]{2,1,0:T(8,128)(2,1)S(1)} custom-call(s32[1]{0:T(128)} %bitcast.4.core_ref, bf16[544,1280]{1,0:T(8,128)(2,1)S(1)} %copy-done.2, bf16[544,1280]{1,0:T(8,128)(2,1)S(1)} %collective-permute-done.other_ref, bf16[64,1280]{1,0:T(8,128)(2,1)S(1)} %copy-done.4, bf16[32,184,128]{2,1,0:T(8,128)(2,1)S(1)} %all-to-all-done.weight_ref), custom_call_target="tpu_custom_call" | custom-call | flops 1000000000 | bytes 3000000 | tf_op jit(solution)/shard_map/resampler_heads/pallas_call | solution.py:291
  67.5 2.7 %collective-permute-start.1 = (bf16[64,128]{1,0:T(8,128)(2,1)S(1)}, bf16[64,128]{1,0:T(8,128)(2,1)S(1)}, u32[]{:S(2)}, u32[]{:S(2)}) collective-permute-start(bf16[64,128]{1,0:T(8,128)(2,1)S(1)} %get-tuple-element.27), channel_id=1, source_target_pairs={{0,64},{64,128},{128,192},{192,0},{1,65},{65,129},{129,193},{193,1... | collective-permute-start | bytes 49160 | tf_op jit(solution)/shard_map/ppermute | solution.py:303
  70.2 2.0 %collective-permute-start.2 = (bf16[64,128]{1,0:T(8,128)(2,1)S(1)}, bf16[64,128]{1,0:T(8,128)(2,1)S(1)}, u32[]{:S(2)}, u32[]{:S(2)}) collective-permute-start(bf16[64,128]{1,0:T(8,128)(2,1)S(1)} %get-tuple-element.26), channel_id=1, source_target_pairs={{0,128},{64,192},{128,0},{192,64},{1,129},{65,193},{129,1},{193,65... | collective-permute-start | bytes 49160 | tf_op jit(solution)/shard_map/ppermute | solution.py:303
  72.2 0.9 slice.16
  73.1 2.6 %collective-permute-done.6.refs_7_ = bf16[1280,128]{1,0:T(8,128)(2,1)} collective-permute-done((bf16[1280,128]{1,0:T(8,128)(2,1)S(1)}, bf16[1280,128]{1,0:T(8,128)(2,1)}, u32[]{:S(2)}, u32[]{:S(2)}) %collective-permute-start.6) | collective-permute-done | bytes 327712 | tf_op jit(solution)/shard_map/ppermute | solution.py:304
  76.1 1.5 collective-permute-done.3.refs_3_
  77.6 1.6 %project_out.1 = f32[64,1280]{1,0:T(8,128)S(1)} custom-call(bf16[64,128]{1,0:T(8,128)(2,1)S(1)} %get-tuple-element.28.refs_0_, bf16[64,128]{1,0:T(8,128)(2,1)S(1)} %collective-permute-done.1.refs_1_, bf16[64,128]{1,0:T(8,128)(2,1)S(1)} %collective-permute-done.2.refs_2_, bf16[64,128]{1,0:T(8,128)(2,1)S(1)} %collective-permute-done.3.refs_3_, ...), custom_call_target="tpu_custom_call" | custom-call | flops 70000000 | bytes 3000000 | tf_op jit(solution)/shard_map/project_out/pallas_call | solution.py:305
  80.2 1.2 collective-permute-start.9
  82.1 2.8 %collective-permute-done.8 = f32[16,1280]{1,0:T(8,128)S(1)} collective-permute-done((f32[16,1280]{1,0:T(8,128)S(1)}, f32[16,1280]{1,0:T(8,128)S(1)}, u32[]{:S(2)}, u32[]{:S(2)}) %collective-permute-start.8) | collective-permute-done | bytes 81952 | tf_op jit(solution)/shard_map/ppermute | solution.py:321
  85.0 0.8 collective-permute-done.9
  85.8 0.9 fusion.8
  87.1 0.9 maximum_maximum_fusion
  88.0 8.4 %all-to-all-start.1 = ((bf16[32,40,128]{2,1,0:T(8,128)(2,1)}), bf16[32,40,128]{2,1,0:T(8,128)(2,1)S(1)}, u32[]{:S(2)}, u32[]{:S(2)}) async-start(bf16[32,40,128]{2,1,0:T(8,128)(2,1)} %maximum_maximum_fusion), calls=%async_computation.1 | async-start | bytes 655360 | tf_op jit(solution)/shard_map/all_to_all | solution.py:339
  96.6 11.9 %all-to-all-done.1 = bf16[32,40,128]{2,1,0:T(8,128)(2,1)S(1)} async-done(((bf16[32,40,128]{2,1,0:T(8,128)(2,1)}), bf16[32,40,128]{2,1,0:T(8,128)(2,1)S(1)}, u32[]{:S(2)}, u32[]{:S(2)}) %all-to-all-start.1) | async-done | bytes 327712 | tf_op jit(solution)/shard_map/all_to_all | solution.py:339
  108.8 0.7 copy.43
  109.5 6.6 %all-to-all-start.2 = ((bf16[32,20,128]{2,1,0:T(8,128)(2,1)}), bf16[32,20,128]{2,1,0:T(8,128)(2,1)S(1)}, u32[]{:S(2)}, u32[]{:S(2)}) async-start(bf16[32,20,128]{2,1,0:T(8,128)(2,1)} %copy.43), calls=%async_computation.2 | async-start | bytes 393216 | tf_op jit(solution)/shard_map/all_to_all | solution.py:344
  116.3 1.6 %copy-done.6 = bf16[128,64,128]{2,1,0:T(8,128)(2,1)S(1)} copy-done((bf16[128,64,128]{2,1,0:T(8,128)(2,1)S(1)}, bf16[128,64,128]{2,1,0:T(8,128)(2,1)}, u32[]{:S(2)}) %copy-start.6) | copy-done | bytes 2097176
  117.8 5.8 %self_attention.1 = bf16[32,32,128]{2,1,0:T(8,128)(2,1)} custom-call(s32[1]{0:T(128)} %bitcast.20.own_ref, bf16[32,32,128]{2,1,0:T(8,128)(2,1)S(1)} %slice.19.q_ref, bf16[4,32,64,128]{3,2,1,0:T(8,128)(2,1)S(1)} %bitcast.50), custom_call_target="tpu_custom_call" | custom-call | flops 1200000000 | bytes 3000000 | tf_op jit(solution)/shard_map/self_attention/pallas_call | solution.py:363
  123.6 1.6 %all-to-all-done.2 = bf16[32,20,128]{2,1,0:T(8,128)(2,1)S(1)} async-done(((bf16[32,20,128]{2,1,0:T(8,128)(2,1)}), bf16[32,20,128]{2,1,0:T(8,128)(2,1)S(1)}, u32[]{:S(2)}, u32[]{:S(2)}) %all-to-all-start.2) | async-done | bytes 163872 | tf_op jit(solution)/shard_map/all_to_all | solution.py:344
  125.3 8.3 %all-to-all-start.3 = ((bf16[32,32,128]{2,1,0:T(8,128)(2,1)}), bf16[32,32,128]{2,1,0:T(8,128)(2,1)S(1)}, u32[]{:S(2)}, u32[]{:S(2)}) async-start(bf16[32,32,128]{2,1,0:T(8,128)(2,1)} %self_attention.1), calls=%async_computation.3 | async-start | bytes 524288 | tf_op jit(solution)/shard_map/all_to_all | solution.py:372
  134.4 7.0 %all_gather.13.window_ref = bf16[16,160,128]{2,1,0:T(8,128)(2,1)S(1)} all-gather(bf16[4,160,128]{2,1,0:T(8,128)(2,1)S(1)} %copy.46), channel_id=1, replica_groups=mesh['y'=4,'z'=8,'xl'=2,'core'=2,'doc'=2] {'xl','core'}, dimensions={0}, use_global_device_ids=true | all-gather | bytes 819200 | tf_op jit(solution)/shard_map/all_gather | solution.py:348
  141.4 1.7 %copy-done.1 = bf16[1280,1024]{1,0:T(8,128)(2,1)S(1)} copy-done((bf16[1280,1024]{1,0:T(8,128)(2,1)S(1)}, bf16[1280,1024]{1,0:T(8,128)(2,1)}, u32[]{:S(2)}) %copy-start.1) | copy-done | bytes 2621464
  143.1 2.8 %cross_attention.1 = bf16[128,1024]{1,0:T(8,128)(2,1)} custom-call(bf16[16,160,128]{2,1,0:T(8,128)(2,1)S(1)} %all_gather.13.window_ref, bf16[1280,1024]{1,0:T(8,128)(2,1)S(1)} %copy-done, bf16[1280,1024]{1,0:T(8,128)(2,1)S(1)} %copy-done.1, bf16[128,1024]{1,0:T(8,128)(2,1)S(1)} %copy-done.3, f32[1,1024]{1,0:T(1,128)S(1)} %bitcast.49, s32[128,1]{1,0:T(8,128)S(1)} %copy.47.slot_ref), custom_call_target="tpu_custom_call" | custom-call | flops 1500000000 | bytes 3000000 | tf_op jit(solution)/shard_map/cross_attention/pallas_call | solution.py:355
  146.0 0.8 copy.57
  (63 shorter events, 4.3 us)
Async XLA Ops:
  7.2 42.3 %all-gather.4.cloned.1.call-start = ((), (), s32[]{:S(2)}) async-start(), calls=%async_computation.4 | async-start | bytes 1740800 | tf_op jit(solution)/shard_map/all_gather | solution.py:285
  11.0 47.3 %all-to-all-start = ((bf16[32,184,128]{2,1,0:T(8,128)(2,1)}), bf16[32,184,128]{2,1,0:T(8,128)(2,1)S(1)}, u32[]{:S(2)}, u32[]{:S(2)}) async-start(bf16[32,184,128]{2,1,0:T(8,128)(2,1)} %get-tuple-element.10), calls=%async_computation | async-start | bytes 3014656 | tf_op jit(solution)/shard_map/all_to_all | solution.py:287
  22.5 93.7 %all-gather.6.cloned.1.call-start = ((), (), s32[]{:S(2)}) async-start(), calls=%async_computation.5 | async-start | bytes 2621440 | tf_op jit(solution)/shard_map/all_gather | solution.py:314
  49.4 12.4 %collective-permute-start = (bf16[544,1280]{1,0:T(8,128)(2,1)}, bf16[544,1280]{1,0:T(8,128)(2,1)S(1)}, u32[]{:S(2)}, u32[]{:S(2)}) collective-permute-start(bf16[544,1280]{1,0:T(8,128)(2,1)} %all-gather.4.cloned.1.call-done.own_ref), channel_id=1, source_target_pairs={{0,2},{2,0},{1,3},{3,1},{4,6},{6,4},{5,7},{7,5},{8,10},{10,8},{9,1... | collective-permute-start | bytes 4177928 | tf_op jit(solution)/shard_map/ppermute | solution.py:286
  58.3 13.9 %collective-permute-start.4 = (bf16[1280,128]{1,0:T(8,128)(2,1)S(1)}, bf16[1280,128]{1,0:T(8,128)(2,1)S(1)}, u32[]{:S(2)}, u32[]{:S(2)}) collective-permute-start(bf16[1280,128]{1,0:T(8,128)(2,1)S(1)} %bitcast.45), channel_id=1, source_target_pairs={{0,64},{64,128},{128,192},{192,0},{1,65},{65,129},{129,193},{193,1... | collective-permute-start | bytes 983048 | tf_op jit(solution)/shard_map/ppermute | solution.py:304
  60.8 12.3 %collective-permute-start.5 = (bf16[1280,128]{1,0:T(8,128)(2,1)S(1)}, bf16[1280,128]{1,0:T(8,128)(2,1)}, u32[]{:S(2)}, u32[]{:S(2)}) collective-permute-start(bf16[1280,128]{1,0:T(8,128)(2,1)S(1)} %bitcast.46), channel_id=1, source_target_pairs={{0,128},{64,192},{128,0},{192,64},{1,129},{65,193},{129,1},{193,65... | collective-permute-start | bytes 983048 | tf_op jit(solution)/shard_map/ppermute | solution.py:304
  61.1 14.5 %collective-permute-start.6 = (bf16[1280,128]{1,0:T(8,128)(2,1)S(1)}, bf16[1280,128]{1,0:T(8,128)(2,1)}, u32[]{:S(2)}, u32[]{:S(2)}) collective-permute-start(bf16[1280,128]{1,0:T(8,128)(2,1)S(1)} %bitcast.47), channel_id=1, source_target_pairs={{0,192},{64,0},{128,64},{192,128},{1,193},{65,1},{129,65},{193,129... | collective-permute-start | bytes 983048 | tf_op jit(solution)/shard_map/ppermute | solution.py:304
  61.8 1.3 copy-start.2
  63.1 0.9 copy-start.4
  67.5 8.1 %collective-permute-start.1 = (bf16[64,128]{1,0:T(8,128)(2,1)S(1)}, bf16[64,128]{1,0:T(8,128)(2,1)S(1)}, u32[]{:S(2)}, u32[]{:S(2)}) collective-permute-start(bf16[64,128]{1,0:T(8,128)(2,1)S(1)} %get-tuple-element.27), channel_id=1, source_target_pairs={{0,64},{64,128},{128,192},{192,0},{1,65},{65,129},{129,193},{193,1... | collective-permute-start | bytes 49160 | tf_op jit(solution)/shard_map/ppermute | solution.py:303
  70.2 5.9 %collective-permute-start.2 = (bf16[64,128]{1,0:T(8,128)(2,1)S(1)}, bf16[64,128]{1,0:T(8,128)(2,1)S(1)}, u32[]{:S(2)}, u32[]{:S(2)}) collective-permute-start(bf16[64,128]{1,0:T(8,128)(2,1)S(1)} %get-tuple-element.26), channel_id=1, source_target_pairs={{0,128},{64,192},{128,0},{192,64},{1,129},{65,193},{129,1},{193,65... | collective-permute-start | bytes 49160 | tf_op jit(solution)/shard_map/ppermute | solution.py:303
  72.2 7.1 %copy-start.7 = (bf16[128,1024]{1,0:T(8,128)(2,1)S(1)}, bf16[128,1024]{1,0:T(8,128)(2,1)}, u32[]{:S(2)}) copy-start(bf16[128,1024]{1,0:T(8,128)(2,1)} %param.28) | copy-start | bytes 786436
  72.2 5.3 %collective-permute-start.3 = (bf16[64,128]{1,0:T(8,128)(2,1)S(1)}, bf16[64,128]{1,0:T(8,128)(2,1)S(1)}, u32[]{:S(2)}, u32[]{:S(2)}) collective-permute-start(bf16[64,128]{1,0:T(8,128)(2,1)S(1)} %get-tuple-element.25), channel_id=1, source_target_pairs={{0,192},{64,0},{128,64},{192,128},{1,193},{65,1},{129,65},{193,129... | collective-permute-start | bytes 49160 | tf_op jit(solution)/shard_map/ppermute | solution.py:303
  77.6 3.9 %copy-start.9 = (s32[32]{0:T(128)S(1)}, s32[32]{0:T(128)}, u32[]{:S(2)}) copy-start(s32[32]{0:T(128)} %param.33) | copy-start | bytes 388
  79.2 7.7 %copy-start.8 = (f32[1280]{0:T(1024)S(1)}, f32[1280]{0:T(1024)}, u32[]{:S(2)}) copy-start(f32[1280]{0:T(1024)} %param.21) | copy-start | bytes 15364
  79.5 2.6 %collective-permute-start.7 = (f32[16,1280]{1,0:T(8,128)S(1)}, f32[16,1280]{1,0:T(8,128)S(1)}, u32[]{:S(2)}, u32[]{:S(2)}) collective-permute-start(f32[16,1280]{1,0:T(8,128)S(1)} %get-tuple-element.22), channel_id=1, source_target_pairs={{0,2},{2,0},{4,6},{6,4},{1,3},{3,1},{5,7},{7,5},{8,10},{10,8},{12,... | collective-permute-start | bytes 245768 | tf_op jit(solution)/shard_map/ppermute | solution.py:321
  79.6 5.3 %collective-permute-start.8 = (f32[16,1280]{1,0:T(8,128)S(1)}, f32[16,1280]{1,0:T(8,128)S(1)}, u32[]{:S(2)}, u32[]{:S(2)}) collective-permute-start(f32[16,1280]{1,0:T(8,128)S(1)} %get-tuple-element.24), channel_id=1, source_target_pairs={{0,4},{2,6},{4,0},{6,2},{1,5},{3,7},{5,1},{7,3},{8,12},{10,14},{12... | collective-permute-start | bytes 245768 | tf_op jit(solution)/shard_map/ppermute | solution.py:321
  80.2 5.5 %collective-permute-start.9 = (f32[16,1280]{1,0:T(8,128)S(1)}, f32[16,1280]{1,0:T(8,128)S(1)}, u32[]{:S(2)}, u32[]{:S(2)}) collective-permute-start(f32[16,1280]{1,0:T(8,128)S(1)} %get-tuple-element.23), channel_id=1, source_target_pairs={{0,6},{2,4},{4,2},{6,0},{1,7},{3,5},{5,3},{7,1},{8,14},{10,12},{12... | collective-permute-start | bytes 245768 | tf_op jit(solution)/shard_map/ppermute | solution.py:321
  88.0 20.6 %all-to-all-start.1 = ((bf16[32,40,128]{2,1,0:T(8,128)(2,1)}), bf16[32,40,128]{2,1,0:T(8,128)(2,1)S(1)}, u32[]{:S(2)}, u32[]{:S(2)}) async-start(bf16[32,40,128]{2,1,0:T(8,128)(2,1)} %maximum_maximum_fusion), calls=%async_computation.1 | async-start | bytes 655360 | tf_op jit(solution)/shard_map/all_to_all | solution.py:339
  109.5 15.8 %all-to-all-start.2 = ((bf16[32,20,128]{2,1,0:T(8,128)(2,1)}), bf16[32,20,128]{2,1,0:T(8,128)(2,1)S(1)}, u32[]{:S(2)}, u32[]{:S(2)}) async-start(bf16[32,20,128]{2,1,0:T(8,128)(2,1)} %copy.43), calls=%async_computation.2 | async-start | bytes 393216 | tf_op jit(solution)/shard_map/all_to_all | solution.py:344
  116.3 1.6 %copy-start.6 = (bf16[128,64,128]{2,1,0:T(8,128)(2,1)S(1)}, bf16[128,64,128]{2,1,0:T(8,128)(2,1)}, u32[]{:S(2)}) copy-start(bf16[128,64,128]{2,1,0:T(8,128)(2,1)} %all-gather.6.cloned.1.call-done) | copy-start | bytes 6291460
  117.8 23.5 %copy-start = (bf16[1280,1024]{1,0:T(8,128)(2,1)S(1)}, bf16[1280,1024]{1,0:T(8,128)(2,1)}, u32[]{:S(2)}) copy-start(bf16[1280,1024]{1,0:T(8,128)(2,1)} %key_ref.1) | copy-start | bytes 7864324
  123.6 17.7 %copy-start.3 = (bf16[128,1024]{1,0:T(8,128)(2,1)S(1)}, bf16[128,1024]{1,0:T(8,128)(2,1)}, u32[]{:S(2)}) copy-start(bf16[128,1024]{1,0:T(8,128)(2,1)} %query_ref.1) | copy-start | bytes 786436
  123.6 17.7 %copy-start.5 = (f32[1024]{0:T(1024)S(1)}, f32[1024]{0:T(1024)}, u32[]{:S(2)}) copy-start(f32[1024]{0:T(1024)} %param.32) | copy-start | bytes 12292
  125.3 20.6 %all-to-all-start.3 = ((bf16[32,32,128]{2,1,0:T(8,128)(2,1)}), bf16[32,32,128]{2,1,0:T(8,128)(2,1)S(1)}, u32[]{:S(2)}, u32[]{:S(2)}) async-start(bf16[32,32,128]{2,1,0:T(8,128)(2,1)} %self_attention.1), calls=%async_computation.3 | async-start | bytes 524288 | tf_op jit(solution)/shard_map/all_to_all | solution.py:372
  141.4 1.7 %copy-start.1 = (bf16[1280,1024]{1,0:T(8,128)(2,1)S(1)}, bf16[1280,1024]{1,0:T(8,128)(2,1)}, u32[]{:S(2)}) copy-start(bf16[1280,1024]{1,0:T(8,128)(2,1)} %value_ref.1) | copy-start | bytes 7864324
Sparse Core Ops, SparseCore 0:
  11.1 38.2 all-gather.3
  79.4 34.5 all-gather.5

commit v5 on v4

--- a/solution.py
+++ b/solution.py
@@ -76,7 +76,11 @@
         row = jnp.concatenate(
             [query[:, span], key[:, span], value[:, span], out[:, span]], 1
         ).astype(jnp.float32)
-        row = jnp.concatenate([row[:, lane : lane + 128] for lane in range(0, 4 * RHD, 128)], 0)
+        starts = [(up, 3 * RHD + lane) for up in range(0, 40, 8) for lane in (0, 32, 64)]
+        starts += [(up, 256) for up in range(0, 40, 8)]
+        blocks = [row[up : up + 8, lane : lane + 32] for up, lane in starts]
+        mixed = [jnp.concatenate(blocks[at : at + 4], 1) for at in range(0, 20, 4)]
+        row = jnp.concatenate([row[:, :128], row[:, 128:256], *mixed], 0)
         row = row.astype(jnp.bfloat16)
         here = slice(head * piece, (head + 1) * piece)
         for image in range(images):
@@ -94,9 +98,11 @@
     overlap = 2 * half - 257
     packed = weight_ref[:, 64:, :].astype(jnp.float32)
     blocks, depth = packed.shape[0], packed.shape[1] // 3
+    mixed = packed[:, 2 * depth :]
+    rest = [mixed[:, 24:32, 96:]] + [mixed[:, 32:, lane : lane + 32] for lane in (0, 32, 64, 96)]
+    parts = [packed[:, :depth], packed[:, depth : 2 * depth], jnp.concatenate(rest, 1)]
     weight = jnp.concatenate(
-        [packed[:, lane * depth : (lane + 1) * depth].reshape(blocks * depth, 128) for lane in range(3)],
-        1,
+        [part.reshape(blocks * depth, part.shape[2]) for part in parts], 1
     ).astype(jnp.bfloat16)
 
     def project(rows):
@@ -132,12 +138,28 @@
         out_ref[image] = context.astype(jnp.bfloat16)
 
 
+def unpack_kernel(*refs):
+    count = len(refs) // 2
+    for packed_ref, out_ref in zip(refs[:count], refs[count:]):
+        packed = packed_ref[...].astype(jnp.float32).reshape(32, 32, 128)
+        rows = []
+        for up in range(5):
+            places = [divmod(3 * up + lane, 4) for lane in range(3)]
+            rows.append(
+                jnp.concatenate(
+                    [packed[:, 8 * g : 8 * g + 8, 32 * at : 32 * at + 32] for g, at in places], 2
+                )
+            )
+        rows = jnp.concatenate(rows, 1).reshape(out_ref.shape)
+        out_ref[...] = rows.astype(jnp.bfloat16)
+
+
 def project_kernel(*refs):
     parts, partial_ref = refs[:-1], refs[-1]
     count = len(parts) // 2
     total = 0.0
     for context_ref, weight_ref in zip(parts[:count], parts[count:]):
-        total = total + dot_t(context_ref[...], weight_ref[...])
+        total = total + dot_t(context_ref[...][:, 128 - RHD :], weight_ref[...])
     partial_ref[...] = total
 
 
@@ -285,7 +307,8 @@
     own_rows = lax.all_gather(own_rows, "y", axis=0, tiled=True)
     other_rows = lax.ppermute(own_rows, "core", [(0, 1), (1, 0)])
     packed = lax.all_to_all(packed, BLK, 0, 0, tiled=True)
-    out_weight = packed[:, 2 * piece + weight_rows - depth :].reshape(blocks * depth, 128)
+    first = 2 * piece + weight_rows - depth
+    out_weight = packed[:, first : first + 32].reshape(blocks * 32, 128)
     pairs = packed[:, 0 : 2 * piece]
 
     contexts = call(
@@ -302,6 +325,13 @@
         turn = [(source, (source + step) % y_size) for source in range(y_size)]
         context_parts.append(lax.ppermute(part, "y", turn) if step else part)
         weight_parts.append(lax.ppermute(out_weight, "y", turn) if step else out_weight)
+    weight_parts = call(
+        unpack_kernel,
+        tuple(jax.ShapeDtypeStruct((full_width, RHD), bf16) for _ in range(y_size)),
+        [VMEM] * y_size,
+        "unpack_o",
+        1000000,
+    )(*weight_parts)
     partial_out = call(
         project_kernel,
         jax.ShapeDtypeStruct((latent_rows, full_width), f32),

time: 157 us -> 154 us (0.981)
  waiting for transfers between devices: 57.5 us -> 55.6 us
  starting transfers between devices: 45 us -> 43.3 us
    ppermute x3, waiting for transfers between devices: 2.59 us -> 0.01 us  [shards(): lax.ppermute(out_weight, 'y', turn)]
    all_to_all x1, starting transfers between devices: 8.4 us -> 6.81 us  [shards(): spread = lax.all_to_all(spread, BLK, 0, 0, tiled=True)]
  transfers between devices with their start and end apart: 16 -> 16, of which waited for: 9 -> 8; matrix products, arithmetic and copies ran while one was open for 4% -> 4% of each run, Pallas kernels for 8% -> 9%
where the time goes in v5:
time: 154 us; the launch traced here: 151 us
  waiting for transfers between devices  55.6 us (36%)
  starting transfers between devices  43.3 us (28%)
  Pallas kernels  17.9 us (12%)
  between operations  14.4 us (9%)
  local copies, waits for them, and re-layouts  8.63 us (6%)
  blocking collectives  7 us (5%)
  other arithmetic  3.69 us (2%)
    all_gather x1, waiting for transfers between devices, shards(): own_rows = lax.all_gather(own_rows, 'y', axis=0, tiled=True)  26.9 us
    all_to_all x1, waiting for transfers between devices, shards(): spread = lax.all_to_all(spread, BLK, 0, 0, tiled=True)  11.9 us
    all_to_all x1, starting transfers between devices, shards(): packed = lax.all_to_all(packed, BLK, 0, 0, tiled=True)  11.5 us
    all_to_all x1, waiting for transfers between devices, shards(): packed = lax.all_to_all(packed, BLK, 0, 0, tiled=True)  8.93 us
    all_to_all x1, starting transfers between devices, shards(): self_rows = lax.all_to_all(self_rows, BLK, 0, 0, tiled=True)  8.27 us
    all_gather x1, blocking collectives, shards(): window = lax.all_gather(chosen, IMG, axis=0, tiled=True)  7 us
    all_to_all x1, starting transfers between devices, shards(): spread = lax.all_to_all(spread, BLK, 0, 0, tiled=True)  6.81 us
    all_to_all x1, starting transfers between devices, shards(): chosen = lax.all_to_all(chosen, BLK, 0, 0, tiled=True)  6.58 us
  transfers between devices with their start and end apart: 16, of which 8 were waited for; matrix products, arithmetic and copies ran while one was open for 4% of the time, Pallas kernels for 9%

profile of v5, /device:TPU:26, one launch (start us, length us, event | category | flops | bytes accessed | tf_op | source)
XLA Modules:
  0.0 150.7 jit_solution(1708917766124930423)
XLA Ops:
  7.2 3.7 %norm_and_pack.1 = (bf16[136,1280]{1,0:T(8,128)(2,1)}, bf16[64,1280]{1,0:T(8,128)(2,1)}, bf16[32,184,128]{2,1,0:T(8,128)(2,1)}) custom-call(s32[1]{0:T(128)} %bitcast.4.core_ref, f32[1280]{0:T(1024)} %context_gain.1, f32[1280]{0:T(1024)} %latent_gain.1, bf16[257,1280]{1,0:T(8,128)(2,1)} %bitcast.55, bf16[64,1280]{1,0:T(8,128)(2,1)} %refs_1_.1, ...), custom_call_target="tpu_custom_call" | custom-call | flops 1000000 | bytes 3000000 | tf_op jit(solution)/shard_map/norm_and_pack/pallas_call | solution.py:293
  11.0 11.5 %all-to-all-start = ((bf16[32,184,128]{2,1,0:T(8,128)(2,1)}), bf16[32,184,128]{2,1,0:T(8,128)(2,1)S(1)}, u32[]{:S(2)}, u32[]{:S(2)}) async-start(bf16[32,184,128]{2,1,0:T(8,128)(2,1)} %get-tuple-element.14), calls=%async_computation | async-start | bytes 3014656 | tf_op jit(solution)/shard_map/all_to_all | solution.py:309
  22.6 26.9 %all-gather.4.cloned.1.call-done.own_ref = bf16[544,1280]{1,0:T(8,128)(2,1)} async-done(((bf16[136,1280]{1,0:T(8,128)(2,1)}), bf16[544,1280]{1,0:T(8,128)(2,1)}) %all-gather.4.cloned.1.call-update) | async-done | bytes 1392656 | tf_op jit(solution)/shard_map/all_gather | solution.py:307
  49.5 8.9 %all-to-all-done.weight_ref = bf16[32,184,128]{2,1,0:T(8,128)(2,1)S(1)} async-done(((bf16[32,184,128]{2,1,0:T(8,128)(2,1)}), bf16[32,184,128]{2,1,0:T(8,128)(2,1)S(1)}, u32[]{:S(2)}, u32[]{:S(2)}) %all-to-all-start) | async-done | bytes 1507360 | tf_op jit(solution)/shard_map/all_to_all | solution.py:309
  58.5 2.4 %collective-permute-start.4 = (bf16[1024,128]{1,0:T(8,128)(2,1)S(1)}, bf16[1024,128]{1,0:T(8,128)(2,1)S(1)}, u32[]{:S(2)}, u32[]{:S(2)}) collective-permute-start(bf16[1024,128]{1,0:T(8,128)(2,1)S(1)} %bitcast.45), channel_id=1, source_target_pairs={{0,64},{64,128},{128,192},{192,0},{1,65},{65,129},{129,193},{193,1... | collective-permute-start | bytes 786440 | tf_op jit(solution)/shard_map/ppermute | solution.py:327
  61.8 1.3 copy-done.2
  63.2 0.9 copy-done.4
  64.1 3.5 %resampler_heads.1 = bf16[4,64,128]{2,1,0:T(8,128)(2,1)S(1)} custom-call(s32[1]{0:T(128)} %bitcast.4.core_ref, bf16[544,1280]{1,0:T(8,128)(2,1)S(1)} %copy-done.2, bf16[544,1280]{1,0:T(8,128)(2,1)S(1)} %collective-permute-done.other_ref, bf16[64,1280]{1,0:T(8,128)(2,1)S(1)} %copy-done.4, bf16[32,184,128]{2,1,0:T(8,128)(2,1)S(1)} %all-to-all-done.weight_ref), custom_call_target="tpu_custom_call" | custom-call | flops 1000000000 | bytes 3000000 | tf_op jit(solution)/shard_map/resampler_heads/pallas_call | solution.py:314
  67.6 2.7 %collective-permute-start.1 = (bf16[64,128]{1,0:T(8,128)(2,1)S(1)}, bf16[64,128]{1,0:T(8,128)(2,1)S(1)}, u32[]{:S(2)}, u32[]{:S(2)}) collective-permute-start(bf16[64,128]{1,0:T(8,128)(2,1)S(1)} %get-tuple-element.35), channel_id=1, source_target_pairs={{0,64},{64,128},{128,192},{192,0},{1,65},{65,129},{129,193},{193,1... | collective-permute-start | bytes 49160 | tf_op jit(solution)/shard_map/ppermute | solution.py:326
  70.2 2.0 %collective-permute-start.2 = (bf16[64,128]{1,0:T(8,128)(2,1)S(1)}, bf16[64,128]{1,0:T(8,128)(2,1)S(1)}, u32[]{:S(2)}, u32[]{:S(2)}) collective-permute-start(bf16[64,128]{1,0:T(8,128)(2,1)S(1)} %get-tuple-element.34), channel_id=1, source_target_pairs={{0,128},{64,192},{128,0},{192,64},{1,129},{65,193},{129,1},{193,65... | collective-permute-start | bytes 49160 | tf_op jit(solution)/shard_map/ppermute | solution.py:326
  72.3 0.9 slice.16
  73.1 1.5 unpack_o.1
  74.7 0.8 collective-permute-done.2.refs_2_
  75.5 1.7 %collective-permute-done.3.refs_3_ = bf16[64,128]{1,0:T(8,128)(2,1)S(1)} collective-permute-done((bf16[64,128]{1,0:T(8,128)(2,1)S(1)}, bf16[64,128]{1,0:T(8,128)(2,1)S(1)}, u32[]{:S(2)}, u32[]{:S(2)}) %collective-permute-start.3) | collective-permute-done | bytes 16416 | tf_op jit(solution)/shard_map/ppermute | solution.py:326
  78.8 1.2 collective-permute-start.9
  80.1 0.7 fusion.7
  80.8 2.8 %collective-permute-done.8 = f32[16,1280]{1,0:T(8,128)S(1)} collective-permute-done((f32[16,1280]{1,0:T(8,128)S(1)}, f32[16,1280]{1,0:T(8,128)S(1)}, u32[]{:S(2)}, u32[]{:S(2)}) %collective-permute-start.8) | collective-permute-done | bytes 81952 | tf_op jit(solution)/shard_map/ppermute | solution.py:351
  83.6 0.8 collective-permute-done.9
  84.4 0.9 fusion.8
  85.7 0.9 maximum_maximum_fusion
  86.5 6.8 %all-to-all-start.1 = ((bf16[32,40,128]{2,1,0:T(8,128)(2,1)}), bf16[32,40,128]{2,1,0:T(8,128)(2,1)S(1)}, u32[]{:S(2)}, u32[]{:S(2)}) async-start(bf16[32,40,128]{2,1,0:T(8,128)(2,1)} %maximum_maximum_fusion), calls=%async_computation.1 | async-start | bytes 655360 | tf_op jit(solution)/shard_map/all_to_all | solution.py:369
  93.6 11.9 %all-to-all-done.1 = bf16[32,40,128]{2,1,0:T(8,128)(2,1)S(1)} async-done(((bf16[32,40,128]{2,1,0:T(8,128)(2,1)}), bf16[32,40,128]{2,1,0:T(8,128)(2,1)S(1)}, u32[]{:S(2)}, u32[]{:S(2)}) %all-to-all-start.1) | async-done | bytes 327712 | tf_op jit(solution)/shard_map/all_to_all | solution.py:369
  105.8 0.7 copy.43
  106.5 6.6 %all-to-all-start.2 = ((bf16[32,20,128]{2,1,0:T(8,128)(2,1)}), bf16[32,20,128]{2,1,0:T(8,128)(2,1)S(1)}, u32[]{:S(2)}, u32[]{:S(2)}) async-start(bf16[32,20,128]{2,1,0:T(8,128)(2,1)} %copy.43), calls=%async_computation.2 | async-start | bytes 393216 | tf_op jit(solution)/shard_map/all_to_all | solution.py:374
  113.3 1.6 %copy-done.6 = bf16[128,64,128]{2,1,0:T(8,128)(2,1)S(1)} copy-done((bf16[128,64,128]{2,1,0:T(8,128)(2,1)S(1)}, bf16[128,64,128]{2,1,0:T(8,128)(2,1)}, u32[]{:S(2)}) %copy-start.6) | copy-done | bytes 2097176
  114.8 5.8 %self_attention.1 = bf16[32,32,128]{2,1,0:T(8,128)(2,1)} custom-call(s32[1]{0:T(128)} %bitcast.20.own_ref, bf16[32,32,128]{2,1,0:T(8,128)(2,1)S(1)} %slice.19.q_ref, bf16[4,32,64,128]{3,2,1,0:T(8,128)(2,1)S(1)} %bitcast.50), custom_call_target="tpu_custom_call" | custom-call | flops 1200000000 | bytes 3000000 | tf_op jit(solution)/shard_map/self_attention/pallas_call | solution.py:393
  120.6 1.6 %all-to-all-done.2 = bf16[32,20,128]{2,1,0:T(8,128)(2,1)S(1)} async-done(((bf16[32,20,128]{2,1,0:T(8,128)(2,1)}), bf16[32,20,128]{2,1,0:T(8,128)(2,1)S(1)}, u32[]{:S(2)}, u32[]{:S(2)}) %all-to-all-start.2) | async-done | bytes 163872 | tf_op jit(solution)/shard_map/all_to_all | solution.py:374
  122.3 8.3 %all-to-all-start.3 = ((bf16[32,32,128]{2,1,0:T(8,128)(2,1)}), bf16[32,32,128]{2,1,0:T(8,128)(2,1)S(1)}, u32[]{:S(2)}, u32[]{:S(2)}) async-start(bf16[32,32,128]{2,1,0:T(8,128)(2,1)} %self_attention.1), calls=%async_computation.3 | async-start | bytes 524288 | tf_op jit(solution)/shard_map/all_to_all | solution.py:402
  131.5 7.0 %all_gather.13.window_ref = bf16[16,160,128]{2,1,0:T(8,128)(2,1)S(1)} all-gather(bf16[4,160,128]{2,1,0:T(8,128)(2,1)S(1)} %copy.46), channel_id=1, replica_groups=mesh['y'=4,'z'=8,'xl'=2,'core'=2,'doc'=2] {'xl','core'}, dimensions={0}, use_global_device_ids=true | all-gather | bytes 819200 | tf_op jit(solution)/shard_map/all_gather | solution.py:378
  138.5 1.7 %copy-done.1 = bf16[1280,1024]{1,0:T(8,128)(2,1)S(1)} copy-done((bf16[1280,1024]{1,0:T(8,128)(2,1)S(1)}, bf16[1280,1024]{1,0:T(8,128)(2,1)}, u32[]{:S(2)}) %copy-start.1) | copy-done | bytes 2621464
  140.2 2.8 %cross_attention.1 = bf16[128,1024]{1,0:T(8,128)(2,1)} custom-call(bf16[16,160,128]{2,1,0:T(8,128)(2,1)S(1)} %all_gather.13.window_ref, bf16[1280,1024]{1,0:T(8,128)(2,1)S(1)} %copy-done, bf16[1280,1024]{1,0:T(8,128)(2,1)S(1)} %copy-done.1, bf16[128,1024]{1,0:T(8,128)(2,1)S(1)} %copy-done.3, f32[1,1024]{1,0:T(1,128)S(1)} %bitcast.49, s32[128,1]{1,0:T(8,128)S(1)} %copy.47.slot_ref), custom_call_target="tpu_custom_call" | custom-call | flops 1500000000 | bytes 3000000 | tf_op jit(solution)/shard_map/cross_attention/pallas_call | solution.py:385
  143.1 0.8 copy.57
  (64 shorter events, 4.6 us)
Async XLA Ops:
  7.2 42.3 %all-gather.4.cloned.1.call-start = ((), (), s32[]{:S(2)}) async-start(), calls=%async_computation.4 | async-start | bytes 1740800 | tf_op jit(solution)/shard_map/all_gather | solution.py:307
  11.0 47.4 %all-to-all-start = ((bf16[32,184,128]{2,1,0:T(8,128)(2,1)}), bf16[32,184,128]{2,1,0:T(8,128)(2,1)S(1)}, u32[]{:S(2)}, u32[]{:S(2)}) async-start(bf16[32,184,128]{2,1,0:T(8,128)(2,1)} %get-tuple-element.14), calls=%async_computation | async-start | bytes 3014656 | tf_op jit(solution)/shard_map/all_to_all | solution.py:309
  22.5 90.7 %all-gather.6.cloned.1.call-start = ((), (), s32[]{:S(2)}) async-start(), calls=%async_computation.5 | async-start | bytes 2621440 | tf_op jit(solution)/shard_map/all_gather | solution.py:344
  49.5 12.4 %collective-permute-start = (bf16[544,1280]{1,0:T(8,128)(2,1)}, bf16[544,1280]{1,0:T(8,128)(2,1)S(1)}, u32[]{:S(2)}, u32[]{:S(2)}) collective-permute-start(bf16[544,1280]{1,0:T(8,128)(2,1)} %all-gather.4.cloned.1.call-done.own_ref), channel_id=1, source_target_pairs={{0,2},{2,0},{1,3},{3,1},{4,6},{6,4},{5,7},{7,5},{8,10},{10,8},{9,1... | collective-permute-start | bytes 4177928 | tf_op jit(solution)/shard_map/ppermute | solution.py:308
  58.5 13.8 %collective-permute-start.4 = (bf16[1024,128]{1,0:T(8,128)(2,1)S(1)}, bf16[1024,128]{1,0:T(8,128)(2,1)S(1)}, u32[]{:S(2)}, u32[]{:S(2)}) collective-permute-start(bf16[1024,128]{1,0:T(8,128)(2,1)S(1)} %bitcast.45), channel_id=1, source_target_pairs={{0,64},{64,128},{128,192},{192,0},{1,65},{65,129},{129,193},{193,1... | collective-permute-start | bytes 786440 | tf_op jit(solution)/shard_map/ppermute | solution.py:327
  60.9 12.3 %collective-permute-start.5 = (bf16[1024,128]{1,0:T(8,128)(2,1)S(1)}, bf16[1024,128]{1,0:T(8,128)(2,1)}, u32[]{:S(2)}, u32[]{:S(2)}) collective-permute-start(bf16[1024,128]{1,0:T(8,128)(2,1)S(1)} %bitcast.46), channel_id=1, source_target_pairs={{0,128},{64,192},{128,0},{192,64},{1,129},{65,193},{129,1},{193,65... | collective-permute-start | bytes 786440 | tf_op jit(solution)/shard_map/ppermute | solution.py:327
  61.2 12.0 %collective-permute-start.6 = (bf16[1024,128]{1,0:T(8,128)(2,1)S(1)}, bf16[1024,128]{1,0:T(8,128)(2,1)}, u32[]{:S(2)}, u32[]{:S(2)}) collective-permute-start(bf16[1024,128]{1,0:T(8,128)(2,1)S(1)} %bitcast.47), channel_id=1, source_target_pairs={{0,192},{64,0},{128,64},{192,128},{1,193},{65,1},{129,65},{193,129... | collective-permute-start | bytes 786440 | tf_op jit(solution)/shard_map/ppermute | solution.py:327
  61.8 1.3 copy-start.2
  63.2 0.9 copy-start.4
  67.6 7.1 %collective-permute-start.1 = (bf16[64,128]{1,0:T(8,128)(2,1)S(1)}, bf16[64,128]{1,0:T(8,128)(2,1)S(1)}, u32[]{:S(2)}, u32[]{:S(2)}) collective-permute-start(bf16[64,128]{1,0:T(8,128)(2,1)S(1)} %get-tuple-element.35), channel_id=1, source_target_pairs={{0,64},{64,128},{128,192},{192,0},{1,65},{65,129},{129,193},{193,1... | collective-permute-start | bytes 49160 | tf_op jit(solution)/shard_map/ppermute | solution.py:326
  70.2 5.2 %collective-permute-start.2 = (bf16[64,128]{1,0:T(8,128)(2,1)S(1)}, bf16[64,128]{1,0:T(8,128)(2,1)S(1)}, u32[]{:S(2)}, u32[]{:S(2)}) collective-permute-start(bf16[64,128]{1,0:T(8,128)(2,1)S(1)} %get-tuple-element.34), channel_id=1, source_target_pairs={{0,128},{64,192},{128,0},{192,64},{1,129},{65,193},{129,1},{193,65... | collective-permute-start | bytes 49160 | tf_op jit(solution)/shard_map/ppermute | solution.py:326
  72.3 5.0 %collective-permute-start.3 = (bf16[64,128]{1,0:T(8,128)(2,1)S(1)}, bf16[64,128]{1,0:T(8,128)(2,1)S(1)}, u32[]{:S(2)}, u32[]{:S(2)}) collective-permute-start(bf16[64,128]{1,0:T(8,128)(2,1)S(1)} %get-tuple-element.33), channel_id=1, source_target_pairs={{0,192},{64,0},{128,64},{192,128},{1,193},{65,1},{129,65},{193,129... | collective-permute-start | bytes 49160 | tf_op jit(solution)/shard_map/ppermute | solution.py:326
  73.1 4.8 %copy-start.7 = (bf16[128,1024]{1,0:T(8,128)(2,1)S(1)}, bf16[128,1024]{1,0:T(8,128)(2,1)}, u32[]{:S(2)}) copy-start(bf16[128,1024]{1,0:T(8,128)(2,1)} %param.28) | copy-start | bytes 786436
  77.2 2.9 %copy-start.9 = (s32[32]{0:T(128)S(1)}, s32[32]{0:T(128)}, u32[]{:S(2)}) copy-start(s32[32]{0:T(128)} %param.33) | copy-start | bytes 388
  77.8 7.7 %copy-start.8 = (f32[1280]{0:T(1024)S(1)}, f32[1280]{0:T(1024)}, u32[]{:S(2)}) copy-start(f32[1280]{0:T(1024)} %param.21) | copy-start | bytes 15364
  78.1 2.7 %collective-permute-start.7 = (f32[16,1280]{1,0:T(8,128)S(1)}, f32[16,1280]{1,0:T(8,128)S(1)}, u32[]{:S(2)}, u32[]{:S(2)}) collective-permute-start(f32[16,1280]{1,0:T(8,128)S(1)} %get-tuple-element.30), channel_id=1, source_target_pairs={{0,2},{2,0},{4,6},{6,4},{1,3},{3,1},{5,7},{7,5},{8,10},{10,8},{12,... | collective-permute-start | bytes 245768 | tf_op jit(solution)/shard_map/ppermute | solution.py:351
  78.2 5.3 %collective-permute-start.8 = (f32[16,1280]{1,0:T(8,128)S(1)}, f32[16,1280]{1,0:T(8,128)S(1)}, u32[]{:S(2)}, u32[]{:S(2)}) collective-permute-start(f32[16,1280]{1,0:T(8,128)S(1)} %get-tuple-element.32), channel_id=1, source_target_pairs={{0,4},{2,6},{4,0},{6,2},{1,5},{3,7},{5,1},{7,3},{8,12},{10,14},{12... | collective-permute-start | bytes 245768 | tf_op jit(solution)/shard_map/ppermute | solution.py:351
  78.8 5.5 %collective-permute-start.9 = (f32[16,1280]{1,0:T(8,128)S(1)}, f32[16,1280]{1,0:T(8,128)S(1)}, u32[]{:S(2)}, u32[]{:S(2)}) collective-permute-start(f32[16,1280]{1,0:T(8,128)S(1)} %get-tuple-element.31), channel_id=1, source_target_pairs={{0,6},{2,4},{4,2},{6,0},{1,7},{3,5},{5,3},{7,1},{8,14},{10,12},{12... | collective-permute-start | bytes 245768 | tf_op jit(solution)/shard_map/ppermute | solution.py:351
  86.5 19.0 %all-to-all-start.1 = ((bf16[32,40,128]{2,1,0:T(8,128)(2,1)}), bf16[32,40,128]{2,1,0:T(8,128)(2,1)S(1)}, u32[]{:S(2)}, u32[]{:S(2)}) async-start(bf16[32,40,128]{2,1,0:T(8,128)(2,1)} %maximum_maximum_fusion), calls=%async_computation.1 | async-start | bytes 655360 | tf_op jit(solution)/shard_map/all_to_all | solution.py:369
  106.5 15.7 %all-to-all-start.2 = ((bf16[32,20,128]{2,1,0:T(8,128)(2,1)}), bf16[32,20,128]{2,1,0:T(8,128)(2,1)S(1)}, u32[]{:S(2)}, u32[]{:S(2)}) async-start(bf16[32,20,128]{2,1,0:T(8,128)(2,1)} %copy.43), calls=%async_computation.2 | async-start | bytes 393216 | tf_op jit(solution)/shard_map/all_to_all | solution.py:374
  113.2 1.6 %copy-start.6 = (bf16[128,64,128]{2,1,0:T(8,128)(2,1)S(1)}, bf16[128,64,128]{2,1,0:T(8,128)(2,1)}, u32[]{:S(2)}) copy-start(bf16[128,64,128]{2,1,0:T(8,128)(2,1)} %all-gather.6.cloned.1.call-done) | copy-start | bytes 6291460
  114.8 23.6 %copy-start = (bf16[1280,1024]{1,0:T(8,128)(2,1)S(1)}, bf16[1280,1024]{1,0:T(8,128)(2,1)}, u32[]{:S(2)}) copy-start(bf16[1280,1024]{1,0:T(8,128)(2,1)} %key_ref.1) | copy-start | bytes 7864324
  120.6 17.8 %copy-start.3 = (bf16[128,1024]{1,0:T(8,128)(2,1)S(1)}, bf16[128,1024]{1,0:T(8,128)(2,1)}, u32[]{:S(2)}) copy-start(bf16[128,1024]{1,0:T(8,128)(2,1)} %query_ref.1) | copy-start | bytes 786436
  120.6 17.8 %copy-start.5 = (f32[1024]{0:T(1024)S(1)}, f32[1024]{0:T(1024)}, u32[]{:S(2)}) copy-start(f32[1024]{0:T(1024)} %param.32) | copy-start | bytes 12292
  122.3 20.7 %all-to-all-start.3 = ((bf16[32,32,128]{2,1,0:T(8,128)(2,1)}), bf16[32,32,128]{2,1,0:T(8,128)(2,1)S(1)}, u32[]{:S(2)}, u32[]{:S(2)}) async-start(bf16[32,32,128]{2,1,0:T(8,128)(2,1)} %self_attention.1), calls=%async_computation.3 | async-start | bytes 524288 | tf_op jit(solution)/shard_map/all_to_all | solution.py:402
  138.5 1.7 %copy-start.1 = (bf16[1280,1024]{1,0:T(8,128)(2,1)S(1)}, bf16[1280,1024]{1,0:T(8,128)(2,1)}, u32[]{:S(2)}) copy-start(bf16[1280,1024]{1,0:T(8,128)(2,1)} %value_ref.1) | copy-start | bytes 7864324
Sparse Core Ops, SparseCore 0:
  11.1 38.2 all-gather.3
  78.0 32.9 all-gather.5
